TPU v7x, 256 devices: a whole 4x4x8 slice. The times are simulated.
256 devices in a mesh: req: 32 (over x, z), tp: 8 (over y, core).
Axes of the slice: x: 4, y: 4, z: 8, core: 2. Of those that a mesh axis runs over, the one named last changes fastest.
Arguments:
- queries: bfloat16 [4, 1024, 8192], P(None, 'req', 'tp'), may hold values from -8 to 8
- new_kv: bfloat16 [4, 1024, 2, 1024], P(None, 'req', None, 'tp'), may hold values from -8 to 8
- prefill_page_pool: bfloat16 [8192, 2, 16, 1024], P('req', None, None, 'tp'), may hold values from -6 to 6
- page_table: int32 [1024, 8], P('req'), may hold values from 0 to 255, as said below
- prompt_len: int32 [1024], P('req'), may hold values from 1 to 128
- dest_device: int32 [1024], P('req'), may hold values from 0 to 31, as said below
- ssm_state: float32 [1024, 16, 16384], P('req', None, 'tp'), may hold values from -4 to 4
- conv_state: bfloat16 [1024, 3, 16384], P('req', None, 'tp'), may hold values from -6 to 6
- mamba_x: bfloat16 [4, 1024, 16384], P(None, 'req', 'tp'), may hold values from -6 to 6
- mamba_z: bfloat16 [4, 1024, 16384], P(None, 'req', 'tp'), may hold values from -6 to 6
- conv_weight: float32 [4, 16384], P(None, 'tp'), may hold values from -3 to 3
- conv_bias: float32 [16384], P('tp'), may hold values from -0.5 to 0.5
- x_proj: bfloat16 [16384, 544], P('tp'), may hold values from -0.046875 to 0.046875
- dt_gain: float32 [512], replicated, may hold values from 0.25 to 1.75
- dt_proj: bfloat16 [512, 16384], P(None, 'tp'), may hold values from -0.25 to 0.25
- dt_bias: float32 [16384], P('tp'), may hold values from -3 to 0
- a_log: float32 [16, 16384], P(None, 'tp'), may hold values from -1 to 2.8
- skip_d: float32 [16384], P('tp'), may hold values from 0.5 to 1.5
Outputs:
- attn_out: bfloat16 [4, 1024, 8192], P(None, 'req', 'tp')
- mamba_out: bfloat16 [4, 1024, 16384], P(None, 'req', 'tp')
Inputs may be any that keep to these rules, and one draw needn't show every extreme that they name: `dest_device`: each prefill device hands exactly 1 of its requests to every decode device. `page_table`: the entries of one prefill device's rows are distinct pages of its own pool; only the first ceil(prompt_len / 16) of a row hold the request's tokens.
All inputs are finite; a program needn't handle non-finite values.
Results may differ from a plain program's by a relative error of at most 0.01.
Values may be sent and summed in bfloat16 or wider, within the bound.
No kernel may reach another device: no remote copies, remote signals or barrier semaphores. Data moves between devices by JAX's collectives and lax.ppermute only.
A program may use at most 128 MiB of HBM per device.

v0:
```python
import math

import jax
import jax.numpy as jnp
from jax import lax
from jax.sharding import PartitionSpec as P

HEAD_SIZE = 128


EPSILON = 1e-06
HIGHEST = lax.Precision.HIGHEST


def cached_part(grouped, cache_keys, cache_values, key_valid, score_scale):
    scores = (
        jnp.einsum("trkgd,rskd->trkgs", grouped, cache_keys, preferred_element_type=jnp.float32)
        * score_scale
    )
    scores = jnp.where(key_valid[None, :, None, None, :], scores, -jnp.inf)
    row_max = jnp.max(scores, axis=4)
    weights = jnp.exp(scores - row_max[..., None])
    row_total = jnp.sum(weights, axis=4)
    weighted = jnp.einsum(
        "trkgs,rskd->trkgd", weights, cache_values.astype(jnp.float32), precision=HIGHEST
    )
    return (weighted, row_max, row_total)


def recent_part(grouped, fresh_kv, score_scale):
    step_count = grouped.shape[0]
    scores = (
        jnp.einsum(
            "trkgd,urkd->trkgu", grouped, fresh_kv[:, :, 0], preferred_element_type=jnp.float32
        )
        * score_scale
    )
    causal = jnp.arange(step_count)[None, :] <= jnp.arange(step_count)[:, None]
    scores = jnp.where(causal[:, None, None, None, :], scores, -jnp.inf)
    row_max = jnp.max(scores, axis=4)
    weights = jnp.exp(scores - row_max[..., None])
    row_total = jnp.sum(weights, axis=4)
    weighted = jnp.einsum(
        "trkgu,urkd->trkgd", weights, fresh_kv[:, :, 1].astype(jnp.float32), precision=HIGHEST
    )
    return (weighted, row_max, row_total)


def mamba_steps(
    start_state,
    conv_rows,
    mamba_x,
    mamba_z,
    conv_weight,
    conv_bias,
    x_proj,
    dt_gain,
    dt_proj,
    dt_bias,
    a_log,
    skip_d,
):
    step_count = mamba_x.shape[0]
    tap_count = conv_weight.shape[0]
    rank_width = dt_proj.shape[0]
    state_size = a_log.shape[0]
    window = jnp.concatenate(
        [jnp.transpose(conv_rows, (1, 0, 2)), mamba_x.astype(jnp.float32)], axis=0
    )
    convolved = conv_bias + sum(
        (conv_weight[offset] * window[offset : offset + step_count] for offset in range(tap_count))
    )
    conv_out = jax.nn.silu(convolved).astype(jnp.bfloat16)
    inputs = conv_out.astype(jnp.float32)
    gate_values = jax.nn.silu(mamba_z.astype(jnp.float32))
    decay_log = -jnp.exp(a_log)
    hidden_state = start_state
    outputs = []
    for moment in range(step_count):
        current = lax.psum(
            jnp.dot(conv_out[moment], x_proj, preferred_element_type=jnp.float32), "tp"
        )
        dt_low = current[:, :rank_width]
        b_coef = current[:, rank_width : rank_width + state_size]
        c_coef = current[:, rank_width + state_size :]
        normed = (
            dt_low
            * lax.rsqrt(jnp.mean(dt_low * dt_low, axis=-1, keepdims=True) + EPSILON)
            * dt_gain
        ).astype(jnp.bfloat16)
        step_rate = jax.nn.softplus(
            jnp.dot(normed, dt_proj, preferred_element_type=jnp.float32) + dt_bias
        )
        hidden_state = (
            jnp.exp(step_rate[:, None, :] * decay_log[None]) * hidden_state
            + (step_rate * inputs[moment])[:, None, :] * b_coef[:, :, None]
        )
        reading = jnp.sum(c_coef[:, :, None] * hidden_state, axis=1) + skip_d * inputs[moment]
        outputs.append(reading * gate_values[moment])
    return jnp.stack(outputs).astype(jnp.bfloat16)


def per_device(
    queries,
    new_kv,
    prefill_page_pool,
    page_table,
    prompt_len,
    dest_device,
    ssm_state,
    conv_state,
    mamba_x,
    mamba_z,
    conv_weight,
    conv_bias,
    x_proj,
    dt_gain,
    dt_proj,
    dt_bias,
    a_log,
    skip_d,
):
    local_reqs = dest_device.shape[0]
    step_count = queries.shape[0]
    kv_heads = prefill_page_pool.shape[3] // HEAD_SIZE
    q_heads = queries.shape[2] // HEAD_SIZE
    group_width = q_heads // kv_heads
    cache_len = page_table.shape[1] * prefill_page_pool.shape[2]
    score_scale = 1.0 / math.sqrt(HEAD_SIZE)
    send_order = jnp.argsort(dest_device * local_reqs + jnp.arange(local_reqs, dtype=jnp.int32))
    grouped = queries.reshape(step_count, local_reqs, kv_heads, group_width, HEAD_SIZE)
    fresh_kv = new_kv.reshape(step_count, local_reqs, 2, kv_heads, HEAD_SIZE)
    picked = prefill_page_pool[page_table[send_order]]
    key_valid = jnp.arange(cache_len)[None, :] < prompt_len[send_order][:, None]
    arrived, arrived_mask = (
        lax.all_to_all(picked, "req", split_axis=0, concat_axis=0, tiled=True),
        lax.all_to_all(
            key_valid.astype(jnp.bfloat16), "req", split_axis=0, concat_axis=0, tiled=True
        ),
    )
    cache_keys = arrived[:, :, 0].reshape(local_reqs, cache_len, kv_heads, HEAD_SIZE)
    cache_values = arrived[:, :, 1].reshape(local_reqs, cache_len, kv_heads, HEAD_SIZE)
    weighted, row_max, row_total = cached_part(
        grouped, cache_keys, cache_values, arrived_mask > 0, score_scale
    )
    recent_weighted, recent_max, recent_total = recent_part(grouped, fresh_kv, score_scale)
    joint_max = jnp.maximum(row_max, recent_max)
    old_weight = jnp.exp(row_max - joint_max)
    new_weight = jnp.exp(recent_max - joint_max)
    combined = weighted * old_weight[..., None] + recent_weighted * new_weight[..., None]
    combined = combined / (row_total * old_weight + recent_total * new_weight)[..., None]
    attn_out = combined.reshape(step_count, local_reqs, q_heads * HEAD_SIZE).astype(jnp.bfloat16)
    moved_ssm, moved_conv = (
        lax.all_to_all(ssm_state[send_order], "req", split_axis=0, concat_axis=0, tiled=True),
        lax.all_to_all(
            conv_state[send_order].astype(jnp.float32),
            "req",
            split_axis=0,
            concat_axis=0,
            tiled=True,
        ),
    )
    mamba_out = mamba_steps(
        moved_ssm,
        moved_conv,
        mamba_x,
        mamba_z,
        conv_weight,
        conv_bias,
        x_proj,
        dt_gain,
        dt_proj,
        dt_bias,
        a_log,
        skip_d,
    )
    return (attn_out, mamba_out)


def solution(mesh):
    return jax.shard_map(
        per_device,
        mesh=mesh,
        in_specs=(
            P(None, "req", "tp"),
            P(None, "req", None, "tp"),
            P("req", None, None, "tp"),
            P("req", None),
            P("req"),
            P("req"),
            P("req", None, "tp"),
            P("req", None, "tp"),
            P(None, "req", "tp"),
            P(None, "req", "tp"),
            P(None, "tp"),
            P("tp"),
            P("tp", None),
            P(),
            P(None, "tp"),
            P("tp"),
            P(None, "tp"),
            P("tp"),
        ),
        out_specs=(P(None, "req", "tp"), P(None, "req", "tp")),
        check_vma=False,
    )
```

profile of v0, /device:TPU:32, one launch (start us, length us, event | category | flops | bytes accessed | tf_op | source)
XLA Modules:
  0.0 250.2 jit_solution(851375050842177981)
XLA Ops:
  8.0 1.6 sort.17
  11.7 11.2 %all-to-all-start.1 = ((bf16[32,1,128]{2,1,0:T(2,128)(2,1)}), bf16[32,1,128]{2,1,0:T(2,128)(2,1)S(1)}, u32[]{:S(2)}, u32[]{:S(2)}) async-start(bf16[32,1,128]{2,1,0:T(2,128)(2,1)} %compare_convert_fusion), calls=%async_computation.1 | async-start | bytes 32768 | tf_op jit(solution)/shard_map/all_to_all | solution.py:137
  22.9 2.7 %gather_fusion.3 = bf16[32,3,2048]{2,0,1:T(8,128)(2,1)S(1)} fusion(bf16[32,3,2048]{2,0,1:T(8,128)(2,1)} %param.25, s32[1024]{0:T(1024)S(1)} %pad_clamp_fusion.1), kind=kCustom, calls=%fused_computation.3 | custom fusion | bytes 786560 | tf_op jit(solution)/shard_map/gather | solution.py:156
  26.9 4.5 %all-to-all-done.1 = bf16[32,1,128]{2,1,0:T(2,128)(2,1)S(1)} async-done(((bf16[32,1,128]{2,1,0:T(2,128)(2,1)}), bf16[32,1,128]{2,1,0:T(2,128)(2,1)S(1)}, u32[]{:S(2)}, u32[]{:S(2)}) %all-to-all-start.1) | async-done | bytes 8224 | tf_op jit(solution)/shard_map/all_to_all | solution.py:137
  32.0 5.3 %all-to-all-start.2 = ((f32[32,3,2048]{2,1,0:T(4,128)}), f32[32,3,2048]{2,1,0:T(4,128)S(1)}, u32[]{:S(2)}, u32[]{:S(2)}) async-start(f32[32,3,2048]{2,1,0:T(4,128)} %copy.45), calls=%async_computation.2 | async-start | bytes 2097152 | tf_op jit(solution)/shard_map/all_to_all | solution.py:155
  38.1 3.8 %gather_fusion.1 = bf16[256,2,16,128]{3,2,1,0:T(8,128)(2,1)} fusion(bf16[256,2,16,128]{3,2,1,0:T(8,128)(2,1)} %param.20, s32[1024]{0:T(1024)S(1)} %pad_clamp_fusion), kind=kCustom, calls=%fused_computation.1 | custom fusion | bytes 4195328 | tf_op jit(solution)/shard_map/gather | solution.py:133
  41.8 3.4 %copy.40 = bf16[32,8,2,16,128]{4,3,1,2,0:T(8,128)(2,1)} copy(bf16[32,8,2,16,128]{4,3,2,1,0:T(8,128)(2,1)} %bitcast.156) | data formatting | bytes 4194304 | tf_op jit(solution)/shard_map/gather | solution.py:133
  45.3 20.0 %all-to-all-done.2 = f32[32,3,2048]{2,1,0:T(4,128)S(1)} async-done(((f32[32,3,2048]{2,1,0:T(4,128)}), f32[32,3,2048]{2,1,0:T(4,128)S(1)}, u32[]{:S(2)}, u32[]{:S(2)}) %all-to-all-start.2) | async-done | bytes 786464 | tf_op jit(solution)/shard_map/all_to_all | solution.py:155
  65.3 5.2 %all-to-all-start = ((bf16[32,8,2,16,128]{4,3,1,2,0:T(8,128)(2,1)}), bf16[32,8,2,16,128]{4,3,1,2,0:T(8,128)(2,1)}, u32[]{:S(2)}, u32[]{:S(2)}) async-start(bf16[32,8,2,16,128]{4,3,1,2,0:T(8,128)(2,1)} %copy.40), calls=%async_computation | async-start | bytes 4194304 | tf_op jit(solution)/shard_map/all_to_all | solution.py:136
  70.5 5.0 %gather_fusion.4 = f32[32,16,2048]{2,1,0:T(8,128)} fusion(f32[32,16,2048]{2,1,0:T(8,128)} %param.24, s32[1024]{0:T(1024)S(1)} %pad_clamp_fusion.1), kind=kCustom, calls=%fused_computation.4 | custom fusion | bytes 8388736 | tf_op jit(solution)/shard_map/gather | solution.py:154
  75.5 44.5 %all-to-all-done = bf16[32,8,2,16,128]{4,3,1,2,0:T(8,128)(2,1)} async-done(((bf16[32,8,2,16,128]{4,3,1,2,0:T(8,128)(2,1)}), bf16[32,8,2,16,128]{4,3,1,2,0:T(8,128)(2,1)}, u32[]{:S(2)}, u32[]{:S(2)}) %all-to-all-start) | async-done | bytes 2097184 | tf_op jit(solution)/shard_map/all_to_all | solution.py:136
  120.0 6.3 %all-to-all-start.3 = ((f32[32,16,2048]{2,1,0:T(8,128)}), f32[32,16,2048]{2,1,0:T(8,128)}, u32[]{:S(2)}, u32[]{:S(2)}) async-start(f32[32,16,2048]{2,1,0:T(8,128)} %gather_fusion.4), calls=%async_computation.3 | async-start | bytes 8388608 | tf_op jit(solution)/shard_map/all_to_all | solution.py:154
  131.9 1.6 exponential_negate_fusion
  133.5 2.3 convert_multiply_fusion
  142.5 68.6 %all-reduce.3.cloned.1.call-done = (f32[32,544]{1,0:T(8,128)}, f32[32,544]{1,0:T(8,128)}, f32[32,544]{1,0:T(8,128)}, f32[32,544]{1,0:T(8,128)}) async-done(((f32[32,544]{1,0:T(8,128)}, f32[32,544]{1,0:T(8,128)}, f32[32,544]{1,0:T(8,128)}, f32[32,544]{1,0:T(8,128)}), (f32[32,544]{1,0:T(8,128)}, f32[32,544]{1,0:T(8,128)}, f32[32,544]{1,0:T(8,128)}, f32[32,544]{1,0:T(8,128)})) %all-reduce.3.cloned.1.call-update) | async-done | bytes 278544 | tf_op jit(solution)/shard_map/psum | solution.py:80
  213.3 1.5 fusion.52
  216.3 2.2 compare_select_fusion.3
  218.5 2.2 compare_select_fusion.2
  222.0 1.7 bitcast_multiply_fusion
  223.7 2.0 fusion.51
  227.6 1.8 fusion.5
  229.4 1.7 convert_element_type.48
  231.1 1.7 copy.47
  232.8 9.3 %multiply_reduce_fusion.1 = (f32[32,2048]{1,0:T(8,128)S(1)}, f32[32,2048]{1,0:T(8,128)S(1)}, f32[32,2048]{1,0:T(8,128)S(1)}, f32[32,2048]{1,0:T(8,128)S(1)}) fusion(f32[32,16]{1,0:T(8,128)} %get-tuple-element.58, f32[32,2048]{1,0:T(8,128)} %get-tuple-element.32, f32[32,2048]{1,0:T(8,128)} %copy-done.4, f32[32,16]{1,0:T(8,128)} %get-tuple-element.59, ...), kind=kLoop, calls=%fused_computation.6 | loop fusion | flops 24903680 | bytes 7487488 | tf_op jit(solution)/shard_map/reduce_sum | solution.py:98
  (93 shorter events, 25.6 us)
Async XLA Ops:
  7.2 129.6 %copy-start = (bf16[2048,544]{0,1:T(8,128)(2,1)S(1)}, bf16[2048,544]{0,1:T(8,128)(2,1)}, u32[]{:S(2)}) copy-start(bf16[2048,544]{0,1:T(8,128)(2,1)} %param.30) | copy-start | bytes 6684676
  11.0 26.3 %copy-start.24 = (s32[32,8]{0,1:T(8,128)S(1)}, s32[32,8]{0,1:T(8,128)}, u32[]{:S(2)}) copy-start(s32[32,8]{0,1:T(8,128)} %param.21) | copy-start | bytes 3076
  11.7 19.7 %all-to-all-start.1 = ((bf16[32,1,128]{2,1,0:T(2,128)(2,1)}), bf16[32,1,128]{2,1,0:T(2,128)(2,1)S(1)}, u32[]{:S(2)}, u32[]{:S(2)}) async-start(bf16[32,1,128]{2,1,0:T(2,128)(2,1)} %compare_convert_fusion), calls=%async_computation.1 | async-start | bytes 32768 | tf_op jit(solution)/shard_map/all_to_all | solution.py:137
  32.0 33.3 %all-to-all-start.2 = ((f32[32,3,2048]{2,1,0:T(4,128)}), f32[32,3,2048]{2,1,0:T(4,128)S(1)}, u32[]{:S(2)}, u32[]{:S(2)}) async-start(f32[32,3,2048]{2,1,0:T(4,128)} %copy.45), calls=%async_computation.2 | async-start | bytes 2097152 | tf_op jit(solution)/shard_map/all_to_all | solution.py:155
  65.3 54.7 %all-to-all-start = ((bf16[32,8,2,16,128]{4,3,1,2,0:T(8,128)(2,1)}), bf16[32,8,2,16,128]{4,3,1,2,0:T(8,128)(2,1)}, u32[]{:S(2)}, u32[]{:S(2)}) async-start(bf16[32,8,2,16,128]{4,3,1,2,0:T(8,128)(2,1)} %copy.40), calls=%async_computation | async-start | bytes 4194304 | tf_op jit(solution)/shard_map/all_to_all | solution.py:136
  75.5 52.2 %copy-start.11 = (bf16[4,32,1024]{2,1,0:T(8,128)(2,1)S(1)}, bf16[4,32,1024]{2,1,0:T(8,128)(2,1)}, u32[]{:S(2)}) copy-start(bf16[4,32,1024]{2,1,0:T(8,128)(2,1)} %param.18) | copy-start | bytes 786436
  120.0 112.9 %all-to-all-start.3 = ((f32[32,16,2048]{2,1,0:T(8,128)}), f32[32,16,2048]{2,1,0:T(8,128)}, u32[]{:S(2)}, u32[]{:S(2)}) async-start(f32[32,16,2048]{2,1,0:T(8,128)} %gather_fusion.4), calls=%async_computation.3 | async-start | bytes 8388608 | tf_op jit(solution)/shard_map/all_to_all | solution.py:154
  126.3 9.9 %copy-start.22 = (f32[2048]{0:T(1024)S(1)}, f32[2048]{0:T(1024)}, u32[]{:S(2)}) copy-start(f32[2048]{0:T(1024)} %param.29) | copy-start | bytes 24580
  126.3 84.8 %all-reduce.3.cloned.1.call-start = ((), (), s32[]{:S(2)}) async-start(), calls=%async_computation.4 | async-start | bytes 655360 | tf_op jit(solution)/shard_map/psum | solution.py:80
  127.8 5.7 %copy-start.5 = (bf16[16,8,8,128]{3,2,1,0:T(8,128)(2,1)}, bf16[16,8,8,128]{3,2,1,0:T(8,128)(2,1)S(1)}, u32[]{:S(2)}) copy-start(bf16[16,8,8,128]{3,2,1,0:T(8,128)(2,1)S(1)} %copy.52) | copy-start | bytes 786436
  128.7 4.7 %copy-start.18 = (bf16[4,32,2,128]{3,0,1,2:T(4,128)(2,1)}, bf16[4,32,2,128]{3,0,1,2:T(4,128)(2,1)S(1)}, u32[]{:S(2)}) copy-start(bf16[4,32,2,128]{3,0,1,2:T(4,128)(2,1)S(1)} %copy.65) | copy-start | bytes 196612
  130.0 3.4 %copy-start.9 = (f32[4,32,1,8,4]{3,4,0,1,2:T(4,128)}, f32[4,32,1,8,4]{3,4,0,1,2:T(4,128)S(1)}, u32[]{:S(2)}) copy-start(f32[4,32,1,8,4]{3,4,0,1,2:T(4,128)S(1)} %get-tuple-element.48) | copy-start | bytes 49156
  130.1 3.4 %copy-start.12 = (f32[4,32,8]{2,0,1:T(4,128)}, f32[4,32,8]{2,0,1:T(4,128)S(1)}, u32[]{:S(2)}) copy-start(f32[4,32,8]{2,0,1:T(4,128)S(1)} %get-tuple-element.47) | copy-start | bytes 12292
  138.1 4.3 %copy-start.17 = (bf16[32,1,128]{2,1,0:T(2,128)(2,1)S(1)}, bf16[32,1,128]{2,1,0:T(2,128)(2,1)}, u32[]{:S(2)}) copy-start(bf16[32,1,128]{2,1,0:T(2,128)(2,1)} %copy-done.16) | copy-start | bytes 24580
  138.2 78.1 %copy-start.15 = (f32[2048]{0:T(1024)S(1)}, f32[2048]{0:T(1024)}, u32[]{:S(2)}) copy-start(f32[2048]{0:T(1024)} %param.33) | copy-start | bytes 24580
  138.2 78.1 %copy-start.20 = (f32[512]{0:T(512)S(1)}, f32[512]{0:T(512)}, u32[]{:S(2)}) copy-start(f32[512]{0:T(512)} %param.31) | copy-start | bytes 6148
  211.1 9.6 %copy-start.1 = (bf16[512,2048]{1,0:T(8,128)(2,1)S(1)}, bf16[512,2048]{1,0:T(8,128)(2,1)}, u32[]{:S(2)}) copy-start(bf16[512,2048]{1,0:T(8,128)(2,1)} %param.32) | copy-start | bytes 6291460
  211.1 9.6 %copy-start.8 = (f32[32,544]{1,0:T(8,128)S(1)}, f32[32,544]{1,0:T(8,128)}, u32[]{:S(2)}) copy-start(f32[32,544]{1,0:T(8,128)} %get-tuple-element.16) | copy-start | bytes 208900
  211.1 10.9 %copy-start.7 = (f32[32,544]{1,0:T(8,128)S(1)}, f32[32,544]{1,0:T(8,128)}, u32[]{:S(2)}) copy-start(f32[32,544]{1,0:T(8,128)} %get-tuple-element.19) | copy-start | bytes 208900
  222.0 3.7 %copy-start.6 = (bf16[16,8,8,128]{3,2,1,0:T(8,128)(2,1)S(1)}, bf16[16,8,8,128]{3,2,1,0:T(8,128)(2,1)}, u32[]{:S(2)}) copy-start(bf16[16,8,8,128]{3,2,1,0:T(8,128)(2,1)} %copy-done.5) | copy-start | bytes 786436
  223.7 3.3 %copy-start.19 = (bf16[4,32,2,128]{3,0,1,2:T(4,128)(2,1)S(1)}, bf16[4,32,2,128]{3,0,1,2:T(4,128)(2,1)}, u32[]{:S(2)}) copy-start(bf16[4,32,2,128]{3,0,1,2:T(4,128)(2,1)} %copy-done.18) | copy-start | bytes 196612
  226.9 5.9 %copy-start.21 = (f32[32,16]{1,0:T(8,128)S(1)}, f32[32,16]{1,0:T(8,128)}, u32[]{:S(2)}) copy-start(f32[32,16]{1,0:T(8,128)} %get-tuple-element.35) | copy-start | bytes 6148
  232.8 9.4 %copy-start.2 = (f32[4,32,2048]{2,1,0:T(8,128)S(1)}, f32[4,32,2048]{2,1,0:T(8,128)}, u32[]{:S(2)}) copy-start(f32[4,32,2048]{2,1,0:T(8,128)} %convert_multiply_fusion) | copy-start | bytes 3145732
  232.8 9.4 %copy-start.23 = (f32[2048]{0:T(1024)S(1)}, f32[2048]{0:T(1024)}, u32[]{:S(2)}) copy-start(f32[2048]{0:T(1024)} %param.35) | copy-start | bytes 24580
  (6 other events, 11.7 us)
Sparse Core Ops, SparseCore 0:
  142.5 68.4 all-reduce.2
where the time goes:
time: 252 us; the launch traced here: 250 us
  waiting for transfers between devices  138 us (55%)
  local copies, waits for them, and re-layouts  30.5 us (12%)
  starting transfers between devices  28.3 us (11%)
  other arithmetic  22.6 us (9%)
  matrix products  16.8 us (7%)
  between operations  14.4 us (6%)
    psum x1, waiting for transfers between devices, mamba_steps(): lax.psum(jnp.dot(conv_out[moment], x_proj, preferred_element_type=jnp.flo...  68.6 us
    all_to_all x1, waiting for transfers between devices, per_device(): lax.all_to_all(picked, 'req', split_axis=0, concat_axis=0, tiled=True)  44.5 us
    all_to_all x1, waiting for transfers between devices, per_device(): lax.all_to_all(conv_state[send_order].astype(jnp.float32), 'req', split_a...  20 us
    all_to_all x1, starting transfers between devices, per_device(): lax.all_to_all(key_valid.astype(jnp.bfloat16), 'req', split_axis=0, conca...  11.2 us
    reduce_sum x1, other arithmetic, mamba_steps(): jnp.sum(c_coef[:, :, None] * hidden_state, axis=1) + skip_d * inputs[moment]  9.34 us
    gather x3, local copies, waits for them, and re-layouts, per_device(): picked = prefill_page_pool[page_table[send_order]]  7.78 us
    dot_general x4, matrix products, mamba_steps(): jnp.dot(normed, dt_proj, preferred_element_type=jnp.float32) + dt_bias  6.65 us
    all_to_all x1, starting transfers between devices, per_device(): lax.all_to_all(ssm_state[send_order], 'req', split_axis=0, concat_axis=0,...  6.34 us
  transfers between devices with their start and end apart: 5, of which 4 were waited for; matrix products, arithmetic and copies ran while one was open for 21% of the time, Pallas kernels for 0%

commit v1 on v0

v1 whole, which is shorter than its diff:
```python
import math

import jax
import jax.numpy as jnp
from jax import lax
from jax.sharding import PartitionSpec as P

HEAD_SIZE = 128
EPSILON = 1e-06


def tp_total(partial, dt_gain, rank_width):
    half = partial.shape[0] // 2
    core = lax.axis_index("tp") % 2
    low, high = partial[:half], partial[half:]
    mine = jnp.where(core == 0, low, high)
    other = jnp.where(core == 0, high, low)
    swap = [(j, j ^ 1) for j in range(8)]
    chip_sum = mine + lax.ppermute(other, "tp", swap)
    small = chip_sum.astype(jnp.bfloat16)
    total = chip_sum
    for hop in (2, 6, 4):
        got = lax.ppermute(small, "tp", [(j, (j + hop) % 8) for j in range(8)])
        total = total + got.astype(jnp.float32)
    dt_low = total[:, :rank_width]
    normed = (
        dt_low
        * lax.rsqrt(jnp.mean(dt_low * dt_low, axis=-1, keepdims=True) + EPSILON)
        * dt_gain
    ).astype(jnp.bfloat16)
    coef = total[:, rank_width:]
    coef_high = coef.astype(jnp.bfloat16)
    coef_low = (coef - coef_high.astype(jnp.float32)).astype(jnp.bfloat16)
    packed = jnp.concatenate([normed, coef_high, coef_low], axis=1)
    theirs = lax.ppermute(packed, "tp", swap)
    first = jnp.where(core == 0, packed, theirs)
    second = jnp.where(core == 0, theirs, packed)
    both = jnp.concatenate([first, second], axis=0)
    width = coef.shape[1]
    coef = both[:, rank_width : rank_width + width].astype(jnp.float32) + both[
        :, rank_width + width :
    ].astype(jnp.float32)
    return both[:, :rank_width], coef


def per_device(
    queries,
    new_kv,
    prefill_page_pool,
    page_table,
    prompt_len,
    dest_device,
    ssm_state,
    conv_state,
    mamba_x,
    mamba_z,
    conv_weight,
    conv_bias,
    x_proj,
    dt_gain,
    dt_proj,
    dt_bias,
    a_log,
    skip_d,
):
    steps, reqs, channels = mamba_x.shape
    rank_width = dt_proj.shape[0]
    state_size = a_log.shape[0]
    heads = queries.shape[2] // HEAD_SIZE
    cache_len = page_table.shape[1] * prefill_page_pool.shape[2]
    scale = 1.0 / math.sqrt(HEAD_SIZE)
    slots = jnp.arange(reqs, dtype=jnp.int32)
    order = jnp.sum(
        jnp.where(dest_device[None, :] == slots[:, None], slots[None, :], 0), axis=1
    )
    outgoing = jnp.concatenate(
        [
            jnp.transpose(mamba_x, (1, 0, 2)),
            jnp.transpose(queries, (1, 0, 2)),
            jnp.transpose(new_kv.reshape(steps, reqs, 2 * HEAD_SIZE), (1, 0, 2)),
        ],
        axis=2,
    )
    arrived = lax.all_to_all(outgoing, "req", split_axis=0, concat_axis=0, tiled=True)
    x_rows = arrived[:, :, :channels].astype(jnp.float32)
    query = arrived[:, :, channels : channels + heads * HEAD_SIZE].reshape(
        reqs, steps, heads, HEAD_SIZE
    )
    fresh = arrived[:, :, channels + heads * HEAD_SIZE :].reshape(reqs, steps, 2, HEAD_SIZE)

    window = jnp.concatenate([conv_state[order].astype(jnp.float32), x_rows], axis=1)
    convolved = conv_bias + sum(
        conv_weight[tap] * window[:, tap : tap + steps] for tap in range(conv_weight.shape[0])
    )
    conv_out = jax.nn.silu(convolved).astype(jnp.bfloat16)
    partial = jnp.dot(
        conv_out.reshape(reqs * steps, channels), x_proj, preferred_element_type=jnp.float32
    )
    normed, coef = tp_total(partial, dt_gain, rank_width)

    picked = prefill_page_pool[page_table[order]]
    keys = picked[:, :, 0].reshape(reqs, cache_len, HEAD_SIZE)
    values = picked[:, :, 1].reshape(reqs, cache_len, HEAD_SIZE)
    valid = jnp.arange(cache_len)[None, :] < prompt_len[order][:, None]
    flat_query = query.reshape(reqs, steps * heads, HEAD_SIZE)
    old = jnp.einsum("rqd,rsd->rqs", flat_query, keys, preferred_element_type=jnp.float32) * scale
    old = jnp.where(valid[:, None, :], old, -jnp.inf)
    new = (
        jnp.einsum("rqd,rud->rqu", flat_query, fresh[:, :, 0], preferred_element_type=jnp.float32)
        * scale
    )
    causal = jnp.arange(steps)[None, :] <= (jnp.arange(steps * heads) // heads)[:, None]
    new = jnp.where(causal[None], new, -jnp.inf)
    top = jnp.maximum(jnp.max(old, axis=2), jnp.max(new, axis=2))[..., None]
    old = jnp.exp(old - top)
    new = jnp.exp(new - top)
    total = jnp.sum(old, axis=2) + jnp.sum(new, axis=2)
    weighted = jnp.einsum(
        "rqs,rsd->rqd", old.astype(jnp.bfloat16), values, preferred_element_type=jnp.float32
    ) + jnp.einsum(
        "rqu,rud->rqd",
        new.astype(jnp.bfloat16),
        fresh[:, :, 1],
        preferred_element_type=jnp.float32,
    )
    attended = (weighted / total[..., None]).astype(jnp.bfloat16)
    attended = attended.reshape(reqs, steps, heads * HEAD_SIZE)

    rate = jax.nn.softplus(
        jnp.dot(normed, dt_proj, preferred_element_type=jnp.float32) + dt_bias
    ).reshape(reqs, steps, channels)
    coef = coef.reshape(reqs, steps, 2 * state_size)
    decay = -jnp.exp(a_log)
    inputs = conv_out.astype(jnp.float32)
    hidden = ssm_state[order]
    readings = []
    for step in range(steps):
        hidden = (
            jnp.exp(rate[:, step, None, :] * decay[None]) * hidden
            + (rate[:, step] * inputs[:, step])[:, None, :] * coef[:, step, :state_size, None]
        )
        readings.append(
            jnp.sum(coef[:, step, state_size:, None] * hidden, axis=1) + skip_d * inputs[:, step]
        )
    reading = jnp.stack(readings, axis=1).astype(jnp.bfloat16)

    returning = jnp.concatenate([reading, attended], axis=2)
    back = lax.all_to_all(returning, "req", split_axis=0, concat_axis=0, tiled=True)
    back = jnp.transpose(back, (1, 0, 2))
    gate = jax.nn.silu(mamba_z.astype(jnp.float32))
    mamba_out = (back[:, :, :channels].astype(jnp.float32) * gate).astype(jnp.bfloat16)
    return back[:, :, channels:], mamba_out


def solution(mesh):
    return jax.shard_map(
        per_device,
        mesh=mesh,
        in_specs=(
            P(None, "req", "tp"),
            P(None, "req", None, "tp"),
            P("req", None, None, "tp"),
            P("req", None),
            P("req"),
            P("req"),
            P("req", None, "tp"),
            P("req", None, "tp"),
            P(None, "req", "tp"),
            P(None, "req", "tp"),
            P(None, "tp"),
            P("tp"),
            P("tp", None),
            P(),
            P(None, "tp"),
            P("tp"),
            P(None, "tp"),
            P("tp"),
        ),
        out_specs=(P(None, "req", "tp"), P(None, "req", "tp")),
        check_vma=False,
    )
```

time: 252 us -> 127 us (0.50)
  waiting for transfers between devices: 138 us -> 10.6 us
  blocking collectives: 0 us -> 28.3 us
  between operations: 14.4 us -> 1.18 us
  starting transfers between devices: 28.3 us -> 16.9 us
  matrix products: 16.8 us -> 8.76 us
  local copies, waits for them, and re-layouts: 30.5 us -> 34.6 us
  other arithmetic: 22.6 us -> 26.3 us
    psum x1 -> x0, waiting for transfers between devices: 68.6 us -> none  [mamba_steps(): lax.psum(jnp.dot(conv_out[moment], x_proj, preferred_element_type=jnp.flo...]
    all_to_all x4 -> x1, waiting for transfers between devices: 69 us -> 4.97 us  [per_device(): lax.all_to_all(outgoing, 'req', split_axis=0, concat_axis=0, tiled=True)]
    all_to_all x0 -> x1, blocking collectives: none -> 28.3 us  [per_device(): lax.all_to_all(returning, 'req', split_axis=0, concat_axis=0, tiled=True)]
    all_to_all x4 -> x1, starting transfers between devices: 28 us -> 11.2 us  [per_device(): lax.all_to_all(outgoing, 'req', split_axis=0, concat_axis=0, tiled=True)]
    dot_general x12 -> x6, matrix products: 16.8 us -> 8.76 us  [the longest x1 3.56 us: per_device(): jnp.dot(normed, dt_proj, preferred_element_type=jnp.float32) + dt_bias]
    reshape x0 -> x6, local copies, waits for them, and re-layouts: none -> 7.33 us  [the longest x1 2.53 us: per_device(): rate = jax.nn.softplus(jnp.dot(normed, dt_proj, preferred_element_type=jn...]
    ppermute x0 -> x5, starting transfers between devices: none -> 5.67 us  [the longest x3 5.3 us: tp_total(): got = lax.ppermute(small, 'tp', [(j, (j + hop) % 8) for j in range(8)])]
    ppermute x0 -> x5, waiting for transfers between devices: none -> 5.66 us  [the longest x3 5.65 us: tp_total(): got = lax.ppermute(small, 'tp', [(j, (j + hop) % 8) for j in range(8)])]
  transfers between devices with their start and end apart: 5 -> 6, of which waited for: 4 -> 4; matrix products, arithmetic and copies ran while one was open for 21% -> 20% of each run, Pallas kernels for 0% -> 0%
where the time goes in v1:
time: 127 us
  local copies, waits for them, and re-layouts  34.6 us (27%)
  blocking collectives  28.3 us (22%)
  other arithmetic  26.3 us (21%)
  starting transfers between devices  16.9 us (13%)
  waiting for transfers between devices  10.6 us (8%)
  matrix products  8.76 us (7%)
    all_to_all x1, blocking collectives, per_device(): lax.all_to_all(returning, 'req', split_axis=0, concat_axis=0, tiled=True)  28.3 us
    all_to_all x1, starting transfers between devices, per_device(): lax.all_to_all(outgoing, 'req', split_axis=0, concat_axis=0, tiled=True)  11.2 us
    reduce_sum x1, other arithmetic, per_device(): jnp.sum(coef[:, step, state_size:, None] * hidden, axis=1)  7.66 us
    unnamed x59, local copies, waits for them, and re-layouts  6.08 us
    ppermute x3, waiting for transfers between devices, tp_total(): got = lax.ppermute(small, 'tp', [(j, (j + hop) % 8) for j in range(8)])  5.65 us
    ppermute x3, starting transfers between devices, tp_total(): got = lax.ppermute(small, 'tp', [(j, (j + hop) % 8) for j in range(8)])  5.3 us
    all_to_all x1, waiting for transfers between devices, per_device(): lax.all_to_all(outgoing, 'req', split_axis=0, concat_axis=0, tiled=True)  4.97 us
    gather x1, local copies, waits for them, and re-layouts, per_device(): hidden = ssm_state[order]  4.95 us
  transfers between devices with their start and end apart: 6, of which 4 were waited for; matrix products, arithmetic and copies ran while one was open for 20% of the time, Pallas kernels for 0%

profile of v1, /device:TPU:32, one launch (start us, length us, event | category | flops | bytes accessed | tf_op | source)
XLA Modules:
  0.0 126.7 jit_solution(6855866730080726794)
XLA Ops:
  2.9 1.5 %copy.168 = bf16[4,32,2048]{2,0,1:T(4,128)(2,1)S(1)} copy(bf16[4,32,2048]{2,1,0:T(8,128)(2,1)} %param.26) | data formatting | bytes 1048576 | tf_op args[8]
  4.4 1.3 %pad_maximum_fusion.1 = bf16[32,4,3328]{2,1,0:T(4,128)(2,1)} fusion(bf16[32,4,256]{2,1,0:T(4,128)(2,1)S(1)} %bitcast.77, bf16[32,4,1024]{2,1,0:T(4,128)(2,1)S(1)} %bitcast.74, bf16[32,4,2048]{2,1,0:T(4,128)(2,1)S(1)} %bitcast.73), kind=kLoop, calls=%fused_computation.43 | loop fusion | flops 2555904 | bytes 1703936 | tf_op jit(solution)/shard_map/concatenate | solution.py:76
  5.7 11.2 %all-to-all-start = ((bf16[32,4,3328]{2,1,0:T(4,128)(2,1)}), bf16[32,4,3328]{2,1,0:T(4,128)(2,1)}, u32[]{:S(2)}, u32[]{:S(2)}) async-start(bf16[32,4,3328]{2,1,0:T(4,128)(2,1)} %pad_maximum_fusion.1), calls=%async_computation | async-start | bytes 1703936 | tf_op jit(solution)/shard_map/all_to_all | solution.py:84
  18.6 1.7 %gather_fusion = bf16[32,3,2048]{2,0,1:T(8,128)(2,1)S(1)} fusion(bf16[32,3,2048]{2,0,1:T(8,128)(2,1)S(1)} %copy-done.2, s32[1024]{0:T(1024)S(1)} %pad_clamp_fusion.1), kind=kCustom, calls=%fused_computation | custom fusion | bytes 786560 | tf_op jit(solution)/shard_map/gather | solution.py:91
  20.3 1.4 %copy.99 = f32[32,3,2048]{2,1,0:T(4,128)} copy(bf16[32,3,2048]{2,0,1:T(8,128)(2,1)S(1)} %gather_fusion) | data formatting | bytes 1179648 | tf_op jit(solution)/shard_map/convert_element_type | solution.py:91
  21.7 5.0 %gather_fusion.1 = f32[32,16,2048]{2,1,0:T(8,128)} fusion(f32[32,16,2048]{2,1,0:T(8,128)} %param.24, s32[1024]{0:T(1024)S(1)} %pad_clamp_fusion.1), kind=kCustom, calls=%fused_computation.1 | custom fusion | bytes 8388736 | tf_op jit(solution)/shard_map/gather | solution.py:135
  26.7 3.8 %gather_fusion.4 = bf16[256,2,16,128]{3,2,1,0:T(8,128)(2,1)} fusion(bf16[256,2,16,128]{3,2,1,0:T(8,128)(2,1)} %param.20, s32[1024]{0:T(1024)S(1)} %pad_clamp_fusion), kind=kCustom, calls=%fused_computation.4 | custom fusion | bytes 4195328 | tf_op jit(solution)/shard_map/gather | solution.py:101
  31.7 3.6 %fusion.33 = (bf16[32,8,1,16,128]{4,3,2,1,0:T(8,128)(2,1)}, bf16[32,8,1,16,128]{4,3,2,1,0:T(8,128)(2,1)}) fusion(bf16[32,8,2,16,128]{4,3,2,1,0:T(8,128)(2,1)} %bitcast.69), kind=kLoop, calls=%fused_computation.107 | loop fusion | bytes 4194304 | tf_op jit(solution)/shard_map/slice | solution.py:103
  36.5 5.0 %all-to-all-done = bf16[32,4,3328]{2,1,0:T(4,128)(2,1)} async-done(((bf16[32,4,3328]{2,1,0:T(4,128)(2,1)}), bf16[32,4,3328]{2,1,0:T(4,128)(2,1)}, u32[]{:S(2)}, u32[]{:S(2)}) %all-to-all-start) | async-done | bytes 852000 | tf_op jit(solution)/shard_map/all_to_all | solution.py:84
  45.5 4.4 %fusion.30 = (f32[32,4,2048]{2,1,0:T(4,128)S(1)}, bf16[32,4,2048]{2,1,0:T(4,128)(2,1)}) fusion(f32[32,4,2048]{2,1,0:T(4,128)S(1)} %slice_convert_fusion, f32[2048]{0:T(1024)} %bitcast.80, f32[32,3,2048]{2,1,0:T(4,128)} %copy.99, f32[2048]{0:T(1024)} %bitcast.81, f32[2048]{0:T(1024)S(1)} %bitcast.79, f32[2048]{0:T(1024)S(1)} %bitcast.78, f32[2048]{0:T(1024)} %param.29), kind=kLoop, calls=%fused_computation.105 | loop fusion | flops 4456448 | bytes 3448832 | tf_op jit(solution)/shard_map/convert_element_type | solution.py:134
  49.9 2.0 %reshape.155 = bf16[128,2048]{1,0:T(8,128)(2,1)} reshape(bf16[32,4,2048]{2,1,0:T(4,128)(2,1)} %get-tuple-element.11) | data formatting | bytes 1048576 | tf_op jit(solution)/shard_map/reshape | solution.py:97
  51.9 1.9 %fusion.39 = f32[128,544]{0,1:T(8,128)S(1)} fusion(bf16[128,2048]{1,0:T(8,128)(2,1)} %reshape.155, bf16[2048,544]{0,1:T(8,128)(2,1)S(1)} %copy-done), kind=kOutput, calls=%fused_computation.113 | convolution fusion | flops 285212672 | bytes 3031040 | tf_op jit(solution)/shard_map/dot_general | solution.py:96
  56.8 3.3 %collective-permute-start.3 = (bf16[64,544]{0,1:T(8,128)(2,1)S(1)}, bf16[64,544]{0,1:T(8,128)(2,1)S(1)}, u32[]{:S(2)}, u32[]{:S(2)}) collective-permute-start(bf16[64,544]{0,1:T(8,128)(2,1)S(1)} %get-tuple-element.14), channel_id=1, source_target_pairs={{0,4},{1,5},{2,6},{3,7},{4,0},{5,1},{6,2},{7,3},{8,12},{9,13},{10,... | collective-permute-start | bytes 208904 | tf_op jit(solution)/shard_map/ppermute | solution.py:23
  62.2 2.7 %collective-permute-done.3 = bf16[64,544]{0,1:T(8,128)(2,1)S(1)} collective-permute-done((bf16[64,544]{0,1:T(8,128)(2,1)S(1)}, bf16[64,544]{0,1:T(8,128)(2,1)S(1)}, u32[]{:S(2)}, u32[]{:S(2)}) %collective-permute-start.3) | collective-permute-done | bytes 69664 | tf_op jit(solution)/shard_map/ppermute | solution.py:23
  64.9 2.9 %collective-permute-done.2 = bf16[64,544]{0,1:T(8,128)(2,1)S(1)} collective-permute-done((bf16[64,544]{0,1:T(8,128)(2,1)S(1)}, bf16[64,544]{0,1:T(8,128)(2,1)S(1)}, u32[]{:S(2)}, u32[]{:S(2)}) %collective-permute-start.2) | collective-permute-done | bytes 69664 | tf_op jit(solution)/shard_map/ppermute | solution.py:23
  68.6 1.2 fusion.2
  69.8 1.7 %reshape.159 = bf16[32,4,1024]{2,1,0:T(4,128)(2,1)} reshape(bf16[32,32,128]{2,1,0:T(8,128)(2,1)} %fusion.2) | data formatting | bytes 524288 | tf_op jit(solution)/shard_map/reshape | solution.py:127
  74.1 3.6 %compare_select_fusion = f32[128,2048]{1,0:T(8,128)} fusion(bf16[512,2048]{1,0:T(8,128)(2,1)} %param.32, f32[2048]{0:T(1024)} %param.33, bf16[64,576]{0,1:T(8,128)(2,1)} %copy-done.7, bf16[64,576]{0,1:T(8,128)(2,1)S(1)} %get-tuple-element.30), kind=kOutput, calls=%fused_computation.12 | convolution fusion | flops 270532608 | bytes 3301376 | tf_op jit(solution)/shard_map/dot_general | solution.py:130
  77.7 2.5 %reshape.157 = f32[32,4,2048]{2,1,0:T(4,128)} reshape(f32[128,2048]{1,0:T(8,128)} %compare_select_fusion) | data formatting | bytes 2097152 | tf_op jit(solution)/shard_map/reshape | solution.py:131
  80.3 4.3 %slice_multiply_fusion = (f32[32,1,2048]{2,1,0:T(1,128)S(1)}, f32[32,1,2048]{2,1,0:T(1,128)S(1)}, f32[32,1,2048]{2,1,0:T(1,128)S(1)}, f32[32,1,2048]{2,1,0:T(1,1...) fusion(f32[32,4,2048]{2,1,0:T(4,128)S(1)} %get-tuple-element.10, ...), kind=kLoop, calls=%fused_computation.72 | loop fusion | flops 262144 | bytes 4194304 | tf_op jit(solution)/shard_map/mul | solution.py:140
  85.4 7.7 %multiply_reduce_fusion.1 = (f32[32,2048]{1,0:T(8,128)S(1)}, f32[32,2048]{1,0:T(8,128)S(1)}, f32[32,2048]{1,0:T(8,128)S(1)}, f32[32,2048]{1,0:T(8,128)S(1)}) fusion(f32[32,16]{1,0:T(8,128)S(1)} %bitcast.85, f32[32,2048]{1,0:T(8,128)S(1)} %get-tuple-element.52, f32[32,2048]{1,0:T(8,128)S(1)} %get-tuple-element.53, f32[32,16]{1,0:T(8,128)S(1)} %bitcast.86, ...), kind=kLoop, calls=%fused_computation.6 | loop fusion | flops 24903680 | bytes 7487488 | tf_op jit(solution)/shard_map/reduce_sum | solution.py:143
  93.0 1.3 %add_convert_fusion.3 = (bf16[32,1,2048]{2,1,0:T(2,128)(2,1)S(1)}, bf16[32,1,2048]{2,1,0:T(2,128)(2,1)S(1)}, bf16[32,1,2048]{2,1,0:T(2,128)(2,1)S(1)}, bf16[32,1,2048]{2,1,0:T(2,128)(2,1)S(1)}) fusion(f32[32,2048]{1,0:T(8,128)S(1)} %get-tuple-element.9, f32[32,4,2048]{2,1,0:T(4,128)S(1)} %get-tuple-element.10, f32[2048]{0:T(1024)S(1)} %copy-done.20, ...), kind=kLoop, calls=%fused_computation.65 | loop fusion | flops 786432 | bytes 2629632 | tf_op jit(solution)/shard_map/convert
  94.4 1.3 %pad_maximum_fusion.2 = bf16[32,4,3072]{2,1,0:T(4,128)(2,1)S(1)} fusion(bf16[32,4,1024]{2,1,0:T(4,128)(2,1)S(1)} %copy-done.6, bf16[32,1,2048]{2,1,0:T(2,128)(2,1)S(1)} %get-tuple-element.25, bf16[32,1,2048]{2,1,0:T(2,128)(2,1)S(1)} %get-tuple-element.24, bf16[32,1,2048]{2,1,0:T(2,128)(2,1)S(1)} %get-tuple-element.23, ...), kind=kLoop, calls=%fused_computation.44 | loop fusion | flops 3932160 | bytes 1572864 | tf_op jit(solution)/shard_map/concatenate | solution.py:147
  95.7 28.3 %all_to_all.10 = bf16[32,4,3072]{2,1,0:T(4,128)(2,1)S(1)} all-to-all(bf16[32,4,3072]{2,1,0:T(4,128)(2,1)S(1)} %pad_maximum_fusion.2), channel_id=1, replica_groups=mesh['req'=32,'tp'=8] {'req'}, dimensions={0} | all-to-all | bytes 1572864 | tf_op jit(solution)/shard_map/all_to_all | solution.py:148
  (107 shorter events, 22.1 us)
Async XLA Ops:
  0.6 51.2 %copy-start = (bf16[2048,544]{0,1:T(8,128)(2,1)S(1)}, bf16[2048,544]{0,1:T(8,128)(2,1)}, u32[]{:S(2)}) copy-start(bf16[2048,544]{0,1:T(8,128)(2,1)} %param.30) | copy-start | bytes 6684676
  0.6 16.3 %copy-start.23 = (s32[32]{0:T(128)S(1)}, s32[32]{0:T(128)}, u32[]{:S(2)}) copy-start(s32[32]{0:T(128)} %param.23) | copy-start | bytes 388
  0.7 16.5 %copy-start.21 = (s32[32,8]{0,1:T(8,128)S(1)}, s32[32,8]{0,1:T(8,128)}, u32[]{:S(2)}) copy-start(s32[32,8]{0,1:T(8,128)} %param.21) | copy-start | bytes 3076
  0.7 16.5 %copy-start.1 = (s32[32]{0:T(128)S(1)}, s32[32]{0:T(128)}, u32[]{:S(2)}) copy-start(s32[32]{0:T(128)} %param.22) | copy-start | bytes 388
  0.7 17.9 %copy-start.2 = (bf16[32,3,2048]{2,0,1:T(8,128)(2,1)S(1)}, bf16[32,3,2048]{2,0,1:T(8,128)(2,1)}, u32[]{:S(2)}) copy-start(bf16[32,3,2048]{2,0,1:T(8,128)(2,1)} %param.25) | copy-start | bytes 1179652
  5.7 35.8 %all-to-all-start = ((bf16[32,4,3328]{2,1,0:T(4,128)(2,1)}), bf16[32,4,3328]{2,1,0:T(4,128)(2,1)}, u32[]{:S(2)}, u32[]{:S(2)}) async-start(bf16[32,4,3328]{2,1,0:T(4,128)(2,1)} %pad_maximum_fusion.1), calls=%async_computation | async-start | bytes 1703936 | tf_op jit(solution)/shard_map/all_to_all | solution.py:84
  26.7 8.6 %copy-start.14 = (f32[4,2048]{1,0:T(4,128)S(1)}, f32[4,2048]{1,0:T(4,128)}, u32[]{:S(2)}) copy-start(f32[4,2048]{1,0:T(4,128)} %param.28) | copy-start | bytes 98308
  26.7 9.2 %copy-start.10 = (f32[16,2048]{1,0:T(8,128)S(1)}, f32[16,2048]{1,0:T(8,128)}, u32[]{:S(2)}) copy-start(f32[16,2048]{1,0:T(8,128)} %param.34) | copy-start | bytes 393220
  49.9 5.3 %copy-start.15 = (pred[32,128]{1,0:T(8,128)(4,1)S(1)}, pred[32,128]{1,0:T(8,128)(4,1)}, u32[]{:S(2)}) copy-start(pred[32,128]{1,0:T(8,128)(4,1)} %iota_compare_fusion) | copy-start | bytes 12292
  53.8 14.3 %copy-start.22 = (f32[512]{0:T(512)S(1)}, f32[512]{0:T(512)}, u32[]{:S(2)}) copy-start(f32[512]{0:T(512)} %param.31) | copy-start | bytes 6148
  53.8 14.8 %copy-start.5 = (bf16[32,8,1,16,128]{4,3,2,1,0:T(8,128)(2,1)S(1)}, bf16[32,8,1,16,128]{4,3,2,1,0:T(8,128)(2,1)}, u32[]{:S(2)}) copy-start(bf16[32,8,1,16,128]{4,3,2,1,0:T(8,128)(2,1)} %get-tuple-element.20) | copy-start | bytes 3145732
  53.9 2.7 %collective-permute-start = (f32[64,544]{0,1:T(8,128)S(1)}, f32[64,544]{0,1:T(8,128)S(1)}, u32[]{:S(2)}, u32[]{:S(2)}) collective-permute-start(f32[64,544]{0,1:T(8,128)S(1)} %slice_select_fusion), channel_id=1, source_target_pairs={{0,1},{1,0},{2,3},{3,2},{4,5},{5,4},{6,7},{7,6},{8,9},{9,8},{10,11... | collective-permute-start | bytes 417800 | tf_op jit(solution)/shard_map/ppermute | solution.py:19
  56.8 8.1 %collective-permute-start.3 = (bf16[64,544]{0,1:T(8,128)(2,1)S(1)}, bf16[64,544]{0,1:T(8,128)(2,1)S(1)}, u32[]{:S(2)}, u32[]{:S(2)}) collective-permute-start(bf16[64,544]{0,1:T(8,128)(2,1)S(1)} %get-tuple-element.14), channel_id=1, source_target_pairs={{0,4},{1,5},{2,6},{3,7},{4,0},{5,1},{6,2},{7,3},{8,12},{9,13},{10,... | collective-permute-start | bytes 208904 | tf_op jit(solution)/shard_map/ppermute | solution.py:23
  60.1 7.7 %collective-permute-start.2 = (bf16[64,544]{0,1:T(8,128)(2,1)S(1)}, bf16[64,544]{0,1:T(8,128)(2,1)S(1)}, u32[]{:S(2)}, u32[]{:S(2)}) collective-permute-start(bf16[64,544]{0,1:T(8,128)(2,1)S(1)} %get-tuple-element.14), channel_id=1, source_target_pairs={{0,6},{1,7},{2,0},{3,1},{4,2},{5,3},{6,4},{7,5},{8,14},{9,15},{10,... | collective-permute-start | bytes 208904 | tf_op jit(solution)/shard_map/ppermute | solution.py:23
  61.1 6.7 %collective-permute-start.1 = (bf16[64,544]{0,1:T(8,128)(2,1)S(1)}, bf16[64,544]{0,1:T(8,128)(2,1)S(1)}, u32[]{:S(2)}, u32[]{:S(2)}) collective-permute-start(bf16[64,544]{0,1:T(8,128)(2,1)S(1)} %get-tuple-element.14), channel_id=1, source_target_pairs={{0,2},{1,3},{2,4},{3,5},{4,6},{5,7},{6,0},{7,1},{8,10},{9,11},{10,... | collective-permute-start | bytes 208904 | tf_op jit(solution)/shard_map/ppermute | solution.py:23
  68.2 3.3 %collective-permute-start.4 = (bf16[64,576]{0,1:T(8,128)(2,1)S(1)}, bf16[64,576]{0,1:T(8,128)(2,1)}, u32[]{:S(2)}, u32[]{:S(2)}) collective-permute-start(bf16[64,576]{0,1:T(8,128)(2,1)S(1)} %pad_maximum_fusion.3), channel_id=1, source_target_pairs={{0,1},{1,0},{2,3},{3,2},{4,5},{5,4},{6,7},{7,6},{8,9},{9,8},{10,11... | collective-permute-start | bytes 221192 | tf_op jit(solution)/shard_map/ppermute | solution.py:35
  80.2 5.1 %copy-start.11 = (f32[16,2048]{1,0:T(8,128)S(1)}, f32[16,2048]{1,0:T(8,128)}, u32[]{:S(2)}) copy-start(f32[16,2048]{1,0:T(8,128)} %exponential_negate_fusion) | copy-start | bytes 393220
  80.2 5.1 %copy-start.16 = (f32[32,1,16]{2,1,0:T(1,128)S(1)}, f32[32,1,16]{2,1,0:T(1,128)}, u32[]{:S(2)}) copy-start(f32[32,1,16]{2,1,0:T(1,128)} %get-tuple-element.36) | copy-start | bytes 6148
  80.2 5.1 %copy-start.17 = (f32[32,1,16]{2,1,0:T(1,128)S(1)}, f32[32,1,16]{2,1,0:T(1,128)}, u32[]{:S(2)}) copy-start(f32[32,1,16]{2,1,0:T(1,128)} %get-tuple-element.37) | copy-start | bytes 6148
  80.2 5.1 %copy-start.18 = (f32[32,1,16]{2,1,0:T(1,128)S(1)}, f32[32,1,16]{2,1,0:T(1,128)}, u32[]{:S(2)}) copy-start(f32[32,1,16]{2,1,0:T(1,128)} %get-tuple-element.38) | copy-start | bytes 6148
  80.2 5.1 %copy-start.19 = (f32[32,1,16]{2,1,0:T(1,128)S(1)}, f32[32,1,16]{2,1,0:T(1,128)}, u32[]{:S(2)}) copy-start(f32[32,1,16]{2,1,0:T(1,128)} %get-tuple-element.39) | copy-start | bytes 6148
  85.3 7.8 %copy-start.20 = (f32[2048]{0:T(1024)S(1)}, f32[2048]{0:T(1024)}, u32[]{:S(2)}) copy-start(f32[2048]{0:T(1024)} %param.35) | copy-start | bytes 24580
  85.3 9.0 %copy-start.6 = (bf16[32,4,1024]{2,1,0:T(4,128)(2,1)S(1)}, bf16[32,4,1024]{2,1,0:T(4,128)(2,1)}, u32[]{:S(2)}) copy-start(bf16[32,4,1024]{2,1,0:T(4,128)(2,1)} %reshape.159) | copy-start | bytes 786436
  93.0 31.1 %copy-start.8 = (bf16[4,32,2048]{2,1,0:T(8,128)(2,1)S(1)}, bf16[4,32,2048]{2,1,0:T(8,128)(2,1)}, u32[]{:S(2)}) copy-start(bf16[4,32,2048]{2,1,0:T(8,128)(2,1)} %param.27) | copy-start | bytes 1572868
  (7 other events, 18.5 us)

commit v2 on v1

v2 whole, which is shorter than its diff:
```python
import math

import jax
import jax.numpy as jnp
from jax import lax
from jax.experimental import pallas as pl
from jax.experimental.pallas import tpu as pltpu
from jax.sharding import PartitionSpec as P

HEAD_SIZE = 128
EPSILON = 1e-06
REQS = 32
STEPS = 4
ROWS = 2 * STEPS
LANES = 128
HALF = 1024
QUARTER = 512
RANK = 512
STATE = 16
PAGES = 8
PAGE_TOKENS = 16
PROJ = RANK + 2 * STATE
SEND = HALF + QUARTER + HEAD_SIZE
BACK = HALF + QUARTER
F32 = jnp.float32
BF16 = jnp.bfloat16


def vmem():
    return pl.BlockSpec(memory_space=pltpu.VMEM)


def smem():
    return pl.BlockSpec(memory_space=pltpu.SMEM)


def params(mib):
    return pltpu.CompilerParams(vmem_limit_bytes=mib * 1024 * 1024)


def sublanes(shape):
    return lax.broadcasted_iota(jnp.int32, shape, len(shape) - 2)


def pack_kernel(x_ref, q_ref, kv_ref, out_ref, rows):
    sources = ((x_ref, HALF), (q_ref, QUARTER), (kv_ref, HEAD_SIZE))
    for step in range(STEPS):
        for group in range(0, REQS, 16):
            for half in range(2):
                first = half * STEPS + step
                places = [
                    pl.ds((group + part * 8) * ROWS + first, 8, stride=ROWS) for part in range(2)
                ]
                tile = 0
                for ref, width in sources:
                    block = ref[step, group : group + 16, half * width : (half + 1) * width]
                    block = block.astype(F32)
                    for column in range(0, width, LANES):
                        rows[tile, places[0], :] = block[0:8, column : column + LANES]
                        rows[tile, places[1], :] = block[8:16, column : column + LANES]
                        tile += 1
    for req in range(REQS):
        for tile in range(SEND // LANES):
            out_ref[req, :, tile * LANES : (tile + 1) * LANES] = rows[
                tile, req * ROWS : (req + 1) * ROWS, :
            ].astype(BF16)


def pack(mamba_x, queries, new_kv):
    return pl.pallas_call(
        pack_kernel,
        out_shape=jax.ShapeDtypeStruct((REQS, ROWS, SEND), BF16),
        in_specs=[vmem()] * 3,
        out_specs=vmem(),
        scratch_shapes=[pltpu.VMEM((SEND // LANES, REQS * ROWS, LANES), F32)],
        compiler_params=params(24),
        name="pack",
    )(mamba_x, queries, new_kv)


def halves(ref, row, width):
    low = jnp.broadcast_to(ref[row : row + 1, 0:width], (STEPS, width))
    high = jnp.broadcast_to(ref[row : row + 1, width : 2 * width], (STEPS, width))
    return jnp.concatenate([low, high], axis=0)


def conv_kernel(
    order_ref,
    core_ref,
    rows_ref,
    past_ref,
    weight_ref,
    bias_ref,
    proj_ref,
    act_ref,
    mine_ref,
    other_ref,
    taps,
    part,
):
    for tap in range(4):
        taps[tap] = halves(weight_ref, tap, HALF)
    taps[4] = halves(bias_ref, 0, HALF)
    step_of = lax.rem(sublanes((ROWS, HALF)), STEPS)
    blank = jnp.zeros((1, HALF), F32)

    def one(req):
        now = rows_ref[req, :, 0:HALF].astype(F32)
        past = past_ref[order_ref[req]].astype(F32)
        past = jnp.concatenate([blank, past[:, HALF:], blank, past[:, :HALF]], axis=0)
        total = taps[4] + taps[3] * now
        for back in range(1, 4):
            mixed = jnp.where(step_of >= STEPS - back, past, now)
            total = total + taps[3 - back] * pltpu.roll(mixed, back, 0)
        return total * jax.nn.sigmoid(total)

    def pair(index, carry):
        both = jnp.concatenate([one(2 * index), one(2 * index + 1)], axis=0)
        act_ref[pl.ds(pl.multiple_of(index * 16, 16), 16), :] = both.astype(BF16)
        return carry

    lax.fori_loop(0, REQS // 2, pair, 0)
    act = act_ref[...]
    low = jnp.dot(act, proj_ref[0:HALF, :], preferred_element_type=F32)
    high = jnp.dot(act, proj_ref[HALF : 2 * HALF, :], preferred_element_type=F32)
    upper = sublanes((ROWS, PROJ)) < STEPS
    for index in range(REQS // 2):
        even = slice(index * 16, index * 16 + 8)
        odd = slice(index * 16 + 8, index * 16 + 16)
        own = jnp.where(upper, low[even], high[odd])
        cross = jnp.where(upper, low[odd], high[even])
        part[index * 8 : index * 8 + 8, :] = own + pltpu.roll(cross, STEPS, 0)
    core = core_ref[0]
    size = REQS * STEPS // 2
    mine_ref[...] = part[pl.ds(pl.multiple_of(core * size, size), size), :]
    other_ref[...] = part[pl.ds(pl.multiple_of((1 - core) * size, size), size), :]


def convolve(order, core, arrived, conv_state, conv_weight, conv_bias, x_proj):
    half_rows = jax.ShapeDtypeStruct((REQS * STEPS // 2, PROJ), F32)
    return pl.pallas_call(
        conv_kernel,
        out_shape=(jax.ShapeDtypeStruct((REQS * ROWS, HALF), BF16), half_rows, half_rows),
        in_specs=[smem(), smem()] + [vmem()] * 5,
        out_specs=(vmem(), vmem(), vmem()),
        scratch_shapes=[
            pltpu.VMEM((5, ROWS, HALF), F32),
            pltpu.VMEM((REQS * STEPS, PROJ), F32),
        ],
        compiler_params=params(24),
        name="convolve",
    )(order, core, arrived, conv_state, conv_weight, conv_bias, x_proj)


def norm_kernel(sum_ref, one_ref, two_ref, three_ref, gain_ref, out_ref):
    total = (
        sum_ref[...]
        + one_ref[...].astype(F32)
        + two_ref[...].astype(F32)
        + three_ref[...].astype(F32)
    )
    low = total[:, :RANK]
    spread = lax.rsqrt(jnp.mean(low * low, axis=-1, keepdims=True) + EPSILON)
    out_ref[:, 0:RANK] = (low * spread * gain_ref[...]).astype(BF16)
    coef = total[:, RANK:]
    coef = jnp.concatenate([coef, jnp.zeros((coef.shape[0], LANES - 2 * STATE), F32)], axis=1)
    coef_high = coef.astype(BF16)
    out_ref[:, RANK : RANK + LANES] = coef_high
    out_ref[:, RANK + LANES :] = (coef - coef_high.astype(F32)).astype(BF16)


def normalise(chip_sum, ring, gain):
    return pl.pallas_call(
        norm_kernel,
        out_shape=jax.ShapeDtypeStruct((REQS * STEPS // 2, RANK + 2 * LANES), BF16),
        in_specs=[vmem()] * 5,
        out_specs=vmem(),
        compiler_params=params(8),
        name="normalise",
    )(chip_sum, *ring, gain)


def attend_kernel(order_ref, table_ref, length_ref, rows_ref, pool_ref, out_ref):
    scale = 1.0 / math.sqrt(HEAD_SIZE)
    wide = (4 * ROWS, 2 * LANES)
    lane = lax.broadcasted_iota(jnp.int32, wide, 1)
    step_of = lax.rem(lax.broadcasted_iota(jnp.int32, wide, 0), STEPS)
    fresh_ok = (lane >= LANES) & (lane - LANES <= step_of)
    pad = jnp.zeros((LANES - PAGE_TOKENS, HEAD_SIZE), BF16)
    blank = jnp.zeros((ROWS, HEAD_SIZE), F32)

    def one(req):
        source = order_ref[req]
        pages = [table_ref[source, page] for page in range(PAGES)]
        length = length_ref[source]
        query = rows_ref[req, :, HALF : HALF + QUARTER].astype(F32)
        query = jnp.concatenate(
            [query[:, h * HEAD_SIZE : (h + 1) * HEAD_SIZE] for h in range(4)], axis=0
        ).astype(BF16)
        fresh = rows_ref[req, :, HALF + QUARTER : SEND].astype(F32)
        fresh_keys = jnp.concatenate([fresh, blank], axis=0).astype(BF16)
        fresh_values = jnp.concatenate([pltpu.roll(fresh, STEPS, 0), blank], axis=0).astype(BF16)
        keys = jnp.concatenate([pool_ref[p, 0] for p in pages] + [fresh_keys, pad], axis=0)
        values = jnp.concatenate([pool_ref[p, 1] for p in pages] + [fresh_values, pad], axis=0)
        scores = (
            lax.dot_general(query, keys, (((1,), (1,)), ((), ())), preferred_element_type=F32)
            * scale
        )
        scores = jnp.where((lane < length) & (lane < LANES) | fresh_ok, scores, -jnp.inf)
        weights = jnp.exp(scores - jnp.max(scores, axis=1, keepdims=True))
        total = jnp.sum(weights, axis=1, keepdims=True)
        mixed = jnp.dot(weights.astype(BF16), values, preferred_element_type=F32) / total
        for h in range(4):
            out_ref[req, :, h * HEAD_SIZE : (h + 1) * HEAD_SIZE] = mixed[
                h * ROWS : (h + 1) * ROWS
            ].astype(BF16)

    def some(index, carry):
        for offset in range(4):
            one(4 * index + offset)
        return carry

    lax.fori_loop(0, REQS // 4, some, 0)


def attend(order, page_table, prompt_len, arrived, pool):
    return pl.pallas_call(
        attend_kernel,
        out_shape=jax.ShapeDtypeStruct((REQS, ROWS, QUARTER), BF16),
        in_specs=[smem()] * 3 + [vmem()] * 2,
        out_specs=vmem(),
        compiler_params=params(16),
        cost_estimate=pl.CostEstimate(
            flops=300_000_000, bytes_accessed=6_000_000, transcendentals=300_000
        ),
        name="attend",
    )(order, page_table, prompt_len, arrived, pool)


def gather_rows(parts, sub):
    four = sub < 4
    parts = [
        jnp.where(four, parts[s], parts[s + 4])
        + pltpu.roll(jnp.where(four, parts[s + 4], parts[s]), 4, 0)
        for s in range(4)
    ]
    two = lax.rem(sub, 4) < 2
    parts = [
        jnp.where(
            two,
            parts[s] + pltpu.roll(parts[s], 6, 0),
            parts[s + 2] + pltpu.roll(parts[s + 2], 2, 0),
        )
        for s in range(2)
    ]
    return jnp.where(
        lax.rem(sub, 2) < 1,
        parts[0] + pltpu.roll(parts[0], 7, 0),
        parts[1] + pltpu.roll(parts[1], 1, 0),
    )


def scan_kernel(
    order_ref,
    core_ref,
    ours_ref,
    theirs_ref,
    act_ref,
    attended_ref,
    state_ref,
    dt_proj_ref,
    dt_bias_ref,
    a_log_ref,
    skip_ref,
    out_ref,
    packed,
    rate,
    fed,
    decay,
    skip,
    coef,
):
    core = core_ref[0]
    size = REQS * STEPS // 2
    packed[pl.ds(pl.multiple_of(core * size, size), size), :] = ours_ref[...]
    packed[pl.ds(pl.multiple_of((1 - core) * size, size), size), :] = theirs_ref[...]
    skip[...] = halves(skip_ref, 0, HALF)
    decay[...] = jnp.exp(a_log_ref[...]) * (-1.0 / math.log(2.0))
    coef[...] = jnp.transpose(
        packed[:, RANK : RANK + LANES].astype(F32) + packed[:, RANK + LANES :].astype(F32)
    )
    upper = sublanes((ROWS, HALF)) < STEPS
    normed = packed[:, 0:RANK]
    low = jnp.dot(normed, dt_proj_ref[:, 0:HALF], preferred_element_type=F32)
    low = jax.nn.softplus(low + dt_bias_ref[:, 0:HALF])
    high = jnp.dot(normed, dt_proj_ref[:, HALF:], preferred_element_type=F32)
    high = jax.nn.softplus(high + dt_bias_ref[:, HALF:])
    for index in range(REQS // 2):
        rows = slice(index * 8, index * 8 + 8)
        even = jnp.where(upper, low[rows], pltpu.roll(high[rows], STEPS, 0))
        odd = jnp.where(upper, pltpu.roll(low[rows], STEPS, 0), high[rows])
        both = jnp.concatenate([even, odd], axis=0)
        span = slice(index * 16, index * 16 + 16)
        both_fed = both * act_ref[span, :].astype(F32)
        rate[2 * index] = even
        rate[2 * index + 1] = odd
        fed[2 * index] = both_fed[0:8]
        fed[2 * index + 1] = both_fed[8:16]
    sub = sublanes((ROWS, LANES))

    def one(req, act):
        source = order_ref[req]
        turned = pltpu.roll(coef[0 : 2 * STATE, :], lax.rem(LANES - STEPS * req, LANES), 1)
        into = [
            jnp.broadcast_to(turned[0:STATE, s : s + 1], (STATE, LANES)) for s in range(STEPS)
        ]
        read = [
            jnp.broadcast_to(turned[STATE : 2 * STATE, s : s + 1], (STATE, LANES))
            for s in range(STEPS)
        ]
        for tile in range(HALF // LANES):
            place = slice(tile * LANES, (tile + 1) * LANES)
            parts = []
            for half in range(2):
                columns = slice(half * HALF + tile * LANES, half * HALF + (tile + 1) * LANES)
                hidden = state_ref[source, :, columns]
                slope = decay[:, columns]
                for step in range(STEPS):
                    row = slice(half * STEPS + step, half * STEPS + step + 1)
                    hidden = (
                        jnp.exp2(jnp.broadcast_to(rate[req, row, place], (STATE, LANES)) * slope) * hidden
                        + jnp.broadcast_to(fed[req, row, place], (STATE, LANES)) * into[step]
                    )
                    seen = hidden * read[step]
                    parts.append(seen[0:8] + seen[8:16])
            summed = gather_rows(parts, sub) + skip[:, place] * act[:, place]
            out_ref[req, :, place] = summed.astype(BF16)
        out_ref[req, :, HALF:BACK] = attended_ref[req]

    def pair(index, carry):
        act = act_ref[pl.ds(pl.multiple_of(index * 16, 16), 16), :].astype(F32)
        one(2 * index, act[0:8])
        one(2 * index + 1, act[8:16])
        return carry

    lax.fori_loop(0, REQS // 2, pair, 0)


def scan(order, core, ours, theirs, act, attended, ssm_state, dt_proj, dt_bias, a_log, skip_d):
    return pl.pallas_call(
        scan_kernel,
        out_shape=jax.ShapeDtypeStruct((REQS, ROWS, BACK), BF16),
        in_specs=[smem(), smem()] + [vmem()] * 9,
        out_specs=vmem(),
        scratch_shapes=[
            pltpu.VMEM((REQS * STEPS, RANK + 2 * LANES), BF16),
            pltpu.VMEM((REQS, ROWS, HALF), F32),
            pltpu.VMEM((REQS, ROWS, HALF), F32),
            pltpu.VMEM((STATE, 2 * HALF), F32),
            pltpu.VMEM((ROWS, HALF), F32),
            pltpu.VMEM((LANES, LANES), F32),
        ],
        compiler_params=params(32),
        name="scan",
    )(order, core, ours, theirs, act, attended, ssm_state, dt_proj, dt_bias, a_log, skip_d)


def unpack_kernel(back_ref, z_ref, attn_ref, mamba_ref, rows):
    for req in range(REQS):
        for tile in range(BACK // LANES):
            rows[tile, req * ROWS : (req + 1) * ROWS, :] = back_ref[
                req, :, tile * LANES : (tile + 1) * LANES
            ].astype(F32)
    for step in range(STEPS):
        for group in range(0, REQS, 16):
            for half in range(2):
                first = half * STEPS + step
                places = [
                    pl.ds((group + part * 8) * ROWS + first, 8, stride=ROWS) for part in range(2)
                ]
                for tile in range(BACK // LANES):
                    block = jnp.concatenate([rows[tile, place, :] for place in places], axis=0)
                    if tile < HALF // LANES:
                        first_column = half * HALF + tile * LANES
                        columns = slice(first_column, first_column + LANES)
                        z = z_ref[step, group : group + 16, columns].astype(F32)
                        block = block * (z * jax.nn.sigmoid(z))
                        mamba_ref[step, group : group + 16, columns] = block.astype(BF16)
                    else:
                        first_column = half * QUARTER + tile * LANES - HALF
                        columns = slice(first_column, first_column + LANES)
                        attn_ref[step, group : group + 16, columns] = block.astype(BF16)


def unpack(back, mamba_z):
    return pl.pallas_call(
        unpack_kernel,
        out_shape=(
            jax.ShapeDtypeStruct((STEPS, REQS, 2 * QUARTER), BF16),
            jax.ShapeDtypeStruct((STEPS, REQS, 2 * HALF), BF16),
        ),
        in_specs=[vmem()] * 2,
        out_specs=(vmem(), vmem()),
        scratch_shapes=[pltpu.VMEM((BACK // LANES, REQS * ROWS, LANES), F32)],
        compiler_params=params(24),
        name="unpack",
    )(back, mamba_z)


def per_device(
    queries,
    new_kv,
    prefill_page_pool,
    page_table,
    prompt_len,
    dest_device,
    ssm_state,
    conv_state,
    mamba_x,
    mamba_z,
    conv_weight,
    conv_bias,
    x_proj,
    dt_gain,
    dt_proj,
    dt_bias,
    a_log,
    skip_d,
):
    slots = jnp.arange(REQS, dtype=jnp.int32)
    order = jnp.sum(
        jnp.where(dest_device[None, :] == slots[:, None], slots[None, :], 0), axis=1
    )
    core = (lax.axis_index("tp") % 2).astype(jnp.int32).reshape(1)
    swap = [(j, j ^ 1) for j in range(8)]

    outgoing = pack(mamba_x, queries, new_kv.reshape(STEPS, REQS, 2 * HEAD_SIZE))
    arrived = lax.all_to_all(outgoing, "req", split_axis=0, concat_axis=0, tiled=True)
    act, mine, other = convolve(
        order, core, arrived, conv_state, conv_weight, conv_bias[None], x_proj
    )
    chip_sum = mine + lax.ppermute(other, "tp", swap)
    small = chip_sum.astype(BF16)
    ring = [
        lax.ppermute(small, "tp", [(j, (j + hop) % 8) for j in range(8)]) for hop in (2, 6, 4)
    ]
    attended = attend(order, page_table, prompt_len, arrived, prefill_page_pool)
    ours = normalise(chip_sum, ring, dt_gain[None])
    theirs = lax.ppermute(ours, "tp", swap)
    returning = scan(
        order,
        core,
        ours,
        theirs,
        act,
        attended,
        ssm_state,
        dt_proj,
        dt_bias[None],
        a_log,
        skip_d[None],
    )
    back = lax.all_to_all(returning, "req", split_axis=0, concat_axis=0, tiled=True)
    return unpack(back, mamba_z)


def solution(mesh):
    return jax.shard_map(
        per_device,
        mesh=mesh,
        in_specs=(
            P(None, "req", "tp"),
            P(None, "req", None, "tp"),
            P("req", None, None, "tp"),
            P("req", None),
            P("req"),
            P("req"),
            P("req", None, "tp"),
            P("req", None, "tp"),
            P(None, "req", "tp"),
            P(None, "req", "tp"),
            P(None, "tp"),
            P("tp"),
            P("tp", None),
            P(),
            P(None, "tp"),
            P("tp"),
            P(None, "tp"),
            P("tp"),
        ),
        out_specs=(P(None, "req", "tp"), P(None, "req", "tp")),
        check_vma=False,
    )
```

time: 127 us -> 109 us (0.86)
  other arithmetic: 26.3 us -> 0.13 us
  Pallas kernels: 0 us -> 23.9 us
  local copies, waits for them, and re-layouts: 34.6 us -> 14.6 us
  waiting for transfers between devices: 10.6 us -> 24.5 us
  matrix products: 8.76 us -> 0 us
    pallas_call x0 -> x6, Pallas kernels: none -> 23.9 us  [the longest x1 9.48 us: attend(): pl.pallas_call(attend_kernel, out_shape=jax.ShapeDtypeStruct((REQS, ROWS,...]
    all_to_all x1, waiting for transfers between devices: 4.97 us -> 19.1 us  [per_device(): lax.all_to_all(outgoing, 'req', split_axis=0, concat_axis=0, tiled=True)]
    gather x5 -> x0, local copies, waits for them, and re-layouts: 11.8 us -> none  [the longest x1 4.95 us: per_device(): hidden = ssm_state[order]]
    dot_general x6 -> x0, matrix products: 8.76 us -> none  [the longest x1 3.56 us: per_device(): jnp.dot(normed, dt_proj, preferred_element_type=jnp.float32) + dt_bias]
    reduce_sum x4 -> x0, other arithmetic: 8.18 us -> none  [the longest x1 7.66 us: per_device(): jnp.sum(coef[:, step, state_size:, None] * hidden, axis=1)]
    slice x7 -> x0, local copies, waits for them, and re-layouts: 7.75 us -> none  [the longest x1 3.57 us: per_device(): values = picked[:, :, 1].reshape(reqs, cache_len, HEAD_SIZE)]
    unnamed x59 -> x39, local copies, waits for them, and re-layouts: 6.08 us -> 13.7 us
    convert_element_type x6 -> x1, other arithmetic: 6.58 us -> 0.02 us  [per_device(): small = chip_sum.astype(BF16)]
  transfers between devices with their start and end apart: 6 -> 6, of which waited for: 4 -> 5; matrix products, arithmetic and copies ran while one was open for 20% -> 5% of each run, Pallas kernels for 0% -> 9%
where the time goes in v2:
time: 109 us
  blocking collectives  28.1 us (26%)
  waiting for transfers between devices  24.5 us (22%)
  Pallas kernels  23.9 us (22%)
  starting transfers between devices  16.7 us (15%)
  local copies, waits for them, and re-layouts  14.6 us (13%)
    all_to_all x1, blocking collectives, per_device(): lax.all_to_all(returning, 'req', split_axis=0, concat_axis=0, tiled=True)  28.1 us
    all_to_all x1, waiting for transfers between devices, per_device(): lax.all_to_all(outgoing, 'req', split_axis=0, concat_axis=0, tiled=True)  19.1 us
    unnamed x39, local copies, waits for them, and re-layouts  13.7 us
    all_to_all x1, starting transfers between devices, per_device(): lax.all_to_all(outgoing, 'req', split_axis=0, concat_axis=0, tiled=True)  11.2 us
    pallas_call x1, Pallas kernels, attend(): pl.pallas_call(attend_kernel, out_shape=jax.ShapeDtypeStruct((REQS, ROWS,...  9.48 us
    pallas_call x1, Pallas kernels, scan(): pl.pallas_call(scan_kernel, out_shape=jax.ShapeDtypeStruct((REQS, ROWS, B...  8.7 us
    ppermute x3, starting transfers between devices, per_device(): lax.ppermute(small, 'tp', [(j, (j + hop) % 8) for j in range(8)])  5.29 us
    ppermute x3, waiting for transfers between devices, per_device(): lax.ppermute(small, 'tp', [(j, (j + hop) % 8) for j in range(8)])  3.97 us
  transfers between devices with their start and end apart: 6, of which 5 were waited for; matrix products, arithmetic and copies ran while one was open for 5% of the time, Pallas kernels for 9%

profile of v2, /device:TPU:32, one launch (start us, length us, event | category | flops | bytes accessed | tf_op | source)
XLA Modules:
  0.0 108.8 jit_solution(610998727440835278)
XLA Ops:
  0.6 0.9 reshape.12.kv_ref
  1.5 1.0 copy-done.6
  2.6 0.9 copy-done.8
  3.5 1.4 %pack.1 = bf16[32,8,1664]{2,1,0:T(8,128)(2,1)} custom-call(bf16[4,32,2048]{2,1,0:T(8,128)(2,1)S(1)} %copy-done.6, bf16[4,32,1024]{2,1,0:T(8,128)(2,1)S(1)} %copy-done.8, bf16[4,32,256]{2,1,0:T(8,128)(2,1)S(1)} %reshape.12.kv_ref), custom_call_target="tpu_custom_call" | custom-call | tf_op jit(solution)/shard_map/pack/pallas_call | solution.py:70
  5.0 11.2 %all-to-all-start = ((bf16[32,8,1664]{2,1,0:T(8,128)(2,1)}), bf16[32,8,1664]{2,1,0:T(8,128)(2,1)S(1)}, u32[]{:S(2)}, u32[]{:S(2)}) async-start(bf16[32,8,1664]{2,1,0:T(8,128)(2,1)} %pack.1), calls=%async_computation | async-start | bytes 1703936 | tf_op jit(solution)/shard_map/all_to_all | solution.py:438
  16.2 3.1 %copy.24.proj_ref = bf16[2048,544]{1,0:T(8,128)(2,1)S(1)} copy(bf16[2048,544]{0,1:T(8,128)(2,1)} %param.30) | data formatting | bytes 4456448 | tf_op args[12]
  19.3 2.1 %copy.23.past_ref = bf16[32,3,2048]{2,1,0:T(4,128)(2,1)} copy(bf16[32,3,2048]{2,0,1:T(8,128)(2,1)} %param.25) | data formatting | bytes 786432 | tf_op args[7]
  21.5 19.1 %all-to-all-done.rows_ref = bf16[32,8,1664]{2,1,0:T(8,128)(2,1)S(1)} async-done(((bf16[32,8,1664]{2,1,0:T(8,128)(2,1)}), bf16[32,8,1664]{2,1,0:T(8,128)(2,1)S(1)}, u32[]{:S(2)}, u32[]{:S(2)}) %all-to-all-start) | async-done | bytes 852000 | tf_op jit(solution)/shard_map/all_to_all | solution.py:438
  40.7 1.0 copy-done.1
  41.7 2.6 %convolve.1 = (bf16[256,1024]{1,0:T(8,128)(2,1)S(1)}, f32[64,544]{1,0:T(8,128)S(1)}, f32[64,544]{1,0:T(8,128)S(1)}) custom-call(s32[32]{0:T(128)S(1)} %select_reduce_fusion.order_ref, s32[1]{0:T(128)} %bitcast.core_ref, bf16[32,8,1664]{2,1,0:T(8,128)(2,1)S(1)} %all-to-all-done.rows_ref, bf16[32,3,2048]{2,1,0:T(4,128)(2,1)S(1)} %copy-done.1, ...), custom_call_target="tpu_custom_call" | custom-call | tf_op jit(solution)/shard_map/convolve/pallas_call | solution.py:141
  44.5 1.4 %collective-permute-done = f32[64,544]{1,0:T(8,128)S(1)} collective-permute-done((f32[64,544]{1,0:T(8,128)S(1)}, f32[64,544]{1,0:T(8,128)S(1)}, u32[]{:S(2)}, u32[]{:S(2)}) %collective-permute-start) | collective-permute-done | bytes 139296 | tf_op jit(solution)/shard_map/ppermute | solution.py:442
  45.9 1.7 %collective-permute-start.1 = (bf16[64,544]{1,0:T(8,128)(2,1)S(1)}, bf16[64,544]{1,0:T(8,128)(2,1)S(1)}, u32[]{:S(2)}, u32[]{:S(2)}) collective-permute-start(bf16[64,544]{1,0:T(8,128)(2,1)S(1)} %get-tuple-element.8), channel_id=1, source_target_pairs={{0,2},{1,3},{2,4},{3,5},{4,6},{5,7},{6,0},{7,1},{8,10},{9,11},{10,... | collective-permute-start | bytes 208904 | tf_op jit(solution)/shard_map/ppermute | solution.py:445
  47.6 1.7 %collective-permute-start.2 = (bf16[64,544]{1,0:T(8,128)(2,1)S(1)}, bf16[64,544]{1,0:T(8,128)(2,1)S(1)}, u32[]{:S(2)}, u32[]{:S(2)}) collective-permute-start(bf16[64,544]{1,0:T(8,128)(2,1)S(1)} %get-tuple-element.8), channel_id=1, source_target_pairs={{0,6},{1,7},{2,0},{3,1},{4,2},{5,3},{6,4},{7,5},{8,14},{9,15},{10,... | collective-permute-start | bytes 208904 | tf_op jit(solution)/shard_map/ppermute | solution.py:445
  49.2 2.0 %collective-permute-start.3 = (bf16[64,544]{1,0:T(8,128)(2,1)S(1)}, bf16[64,544]{1,0:T(8,128)(2,1)S(1)}, u32[]{:S(2)}, u32[]{:S(2)}) collective-permute-start(bf16[64,544]{1,0:T(8,128)(2,1)S(1)} %get-tuple-element.8), channel_id=1, source_target_pairs={{0,4},{1,5},{2,6},{3,7},{4,0},{5,1},{6,2},{7,3},{8,12},{9,13},{10,... | collective-permute-start | bytes 208904 | tf_op jit(solution)/shard_map/ppermute | solution.py:445
  51.2 0.5 collective-permute-done.1.one_ref
  51.8 0.3 collective-permute-done.2.two_ref
  52.0 3.2 %collective-permute-done.3.three_ref = bf16[64,544]{1,0:T(8,128)(2,1)S(1)} collective-permute-done((bf16[64,544]{1,0:T(8,128)(2,1)S(1)}, bf16[64,544]{1,0:T(8,128)(2,1)S(1)}, u32[]{:S(2)}, u32[]{:S(2)}) %collective-permute-start.3) | collective-permute-done | bytes 69664 | tf_op jit(solution)/shard_map/ppermute | solution.py:445
  55.5 1.6 %copy-done.2 = bf16[256,2,16,128]{3,2,1,0:T(8,128)(2,1)S(1)} copy-done((bf16[256,2,16,128]{3,2,1,0:T(8,128)(2,1)S(1)}, bf16[256,2,16,128]{3,2,1,0:T(8,128)(2,1)}, u32[]{:S(2)}) %copy-start.2) | copy-done | bytes 2097176
  57.1 9.5 %attend.1.attended_ref = bf16[32,8,512]{2,1,0:T(8,128)(2,1)S(1)} custom-call(s32[32]{0:T(128)S(1)} %select_reduce_fusion.order_ref, s32[32,8]{1,0:T(8,128)S(1)} %copy.25.table_ref, s32[32]{0:T(128)S(1)} %copy-done.15, bf16[32,8,1664]{2,1,0:T(8,128)(2,1)S(1)} %all-to-all-done.rows_ref, bf16[256,2,16,128]{3,2,1,0:T(8,128)(2,1)S(1)} %copy-done.2), custom_call_target="tpu_custom_call" | custom-call | flops 300000000 | bytes 6000000 | tf_op jit(solution)/shard_map/attend/pallas_call | solution.py:227
  66.7 2.2 %copy-done = f32[32,16,2048]{2,1,0:T(8,128)S(1)} copy-done((f32[32,16,2048]{2,1,0:T(8,128)S(1)}, f32[32,16,2048]{2,1,0:T(8,128)}, u32[]{:S(2)}) %copy-start) | copy-done | bytes 4194328
  68.9 1.6 %copy-done.3 = bf16[512,2048]{1,0:T(8,128)(2,1)S(1)} copy-done((bf16[512,2048]{1,0:T(8,128)(2,1)S(1)}, bf16[512,2048]{1,0:T(8,128)(2,1)}, u32[]{:S(2)}) %copy-start.3) | copy-done | bytes 2097176
  70.4 8.7 %scan.1 = bf16[32,8,1536]{2,1,0:T(8,128)(2,1)S(1)} custom-call(s32[32]{0:T(128)S(1)} %select_reduce_fusion.order_ref, s32[1]{0:T(128)} %bitcast.core_ref, bf16[64,768]{1,0:T(8,128)(2,1)S(1)} %normalise.1.ours_ref, bf16[64,768]{1,0:T(8,128)(2,1)S(1)} %collective-permute-done.4.theirs_ref, bf16[256,1024]{1,0:T(8,128)(2,1)S(1)} %copy-done.5, ...), custom_call_target="tpu_custom_call" | custom-call | tf_op jit(solution)/shard_map/scan/pallas_call | solution.py:350
  79.2 28.1 %all_to_all.10.back_ref = bf16[32,8,1536]{2,1,0:T(8,128)(2,1)S(1)} all-to-all(bf16[32,8,1536]{2,1,0:T(8,128)(2,1)S(1)} %scan.1), channel_id=1, replica_groups=mesh['req'=32,'tp'=8] {'req'}, dimensions={0} | all-to-all | bytes 1572864 | tf_op jit(solution)/shard_map/all_to_all | solution.py:463
  107.3 1.5 %unpack.1 = (bf16[4,32,1024]{2,1,0:T(8,128)(2,1)}, bf16[4,32,2048]{2,1,0:T(8,128)(2,1)}) custom-call(bf16[32,8,1536]{2,1,0:T(8,128)(2,1)S(1)} %all_to_all.10.back_ref, bf16[4,32,2048]{2,1,0:T(8,128)(2,1)S(1)} %copy-done.7), custom_call_target="tpu_custom_call" | custom-call | tf_op jit(solution)/shard_map/unpack/pallas_call | solution.py:396
  (37 shorter events, 0.6 us)
Async XLA Ops:
  1.5 1.0 copy-start.6
  2.6 0.9 copy-start.8
  5.0 35.7 %all-to-all-start = ((bf16[32,8,1664]{2,1,0:T(8,128)(2,1)}), bf16[32,8,1664]{2,1,0:T(8,128)(2,1)S(1)}, u32[]{:S(2)}, u32[]{:S(2)}) async-start(bf16[32,8,1664]{2,1,0:T(8,128)(2,1)} %pack.1), calls=%async_computation | async-start | bytes 1703936 | tf_op jit(solution)/shard_map/all_to_all | solution.py:438
  16.2 5.3 %copy-start.17 = (s32[32]{0:T(128)S(1)}, s32[32]{0:T(128)}, u32[]{:S(2)}) copy-start(s32[32]{0:T(128)} %param.23) | copy-start | bytes 388
  16.2 24.5 %copy-start.10 = (f32[4,2048]{1,0:T(4,128)S(1)}, f32[4,2048]{1,0:T(4,128)}, u32[]{:S(2)}) copy-start(f32[4,2048]{1,0:T(4,128)} %weight_ref.1) | copy-start | bytes 98308
  16.2 24.5 %copy-start.11 = (f32[2048]{0:T(1024)S(1)}, f32[2048]{0:T(1024)}, u32[]{:S(2)}) copy-start(f32[2048]{0:T(1024)} %param.29) | copy-start | bytes 24580
  40.7 1.0 copy-start.1
  41.7 13.5 %copy-start.14 = (f32[512]{0:T(512)S(1)}, f32[512]{0:T(512)}, u32[]{:S(2)}) copy-start(f32[512]{0:T(512)} %param.31) | copy-start | bytes 6148
  41.7 13.7 %copy-start.16 = (s32[32,8]{0,1:T(8,128)S(1)}, s32[32,8]{0,1:T(8,128)}, u32[]{:S(2)}) copy-start(s32[32,8]{0,1:T(8,128)} %param.21) | copy-start | bytes 3076
  41.7 13.8 %copy-start.15 = (s32[32]{0:T(128)S(1)}, s32[32]{0:T(128)}, u32[]{:S(2)}) copy-start(s32[32]{0:T(128)} %length_ref.1) | copy-start | bytes 388
  44.4 11.0 %copy-start.4 = (bf16[256,1024]{1,0:T(8,128)(2,1)}, bf16[256,1024]{1,0:T(8,128)(2,1)S(1)}, u32[]{:S(2)}) copy-start(bf16[256,1024]{1,0:T(8,128)(2,1)S(1)} %get-tuple-element.7.act_ref) | copy-start | bytes 1572868
  44.4 22.2 %copy-start.9 = (f32[16,2048]{1,0:T(8,128)S(1)}, f32[16,2048]{1,0:T(8,128)}, u32[]{:S(2)}) copy-start(f32[16,2048]{1,0:T(8,128)} %a_log_ref.1) | copy-start | bytes 393220
  44.4 22.2 %copy-start.12 = (f32[2048]{0:T(1024)S(1)}, f32[2048]{0:T(1024)}, u32[]{:S(2)}) copy-start(f32[2048]{0:T(1024)} %param.33) | copy-start | bytes 24580
  44.4 22.2 %copy-start.13 = (f32[2048]{0:T(1024)S(1)}, f32[2048]{0:T(1024)}, u32[]{:S(2)}) copy-start(f32[2048]{0:T(1024)} %param.35) | copy-start | bytes 24580
  44.4 1.5 %collective-permute-start = (f32[64,544]{1,0:T(8,128)S(1)}, f32[64,544]{1,0:T(8,128)S(1)}, u32[]{:S(2)}, u32[]{:S(2)}) collective-permute-start(f32[64,544]{1,0:T(8,128)S(1)} %get-tuple-element.6), channel_id=1, source_target_pairs={{0,1},{1,0},{2,3},{3,2},{4,5},{5,4},{6,7},{7,6},{8,9},{9,8},{10,11... | collective-permute-start | bytes 417800 | tf_op jit(solution)/shard_map/ppermute | solution.py:442
  45.9 5.8 %collective-permute-start.1 = (bf16[64,544]{1,0:T(8,128)(2,1)S(1)}, bf16[64,544]{1,0:T(8,128)(2,1)S(1)}, u32[]{:S(2)}, u32[]{:S(2)}) collective-permute-start(bf16[64,544]{1,0:T(8,128)(2,1)S(1)} %get-tuple-element.8), channel_id=1, source_target_pairs={{0,2},{1,3},{2,4},{3,5},{4,6},{5,7},{6,0},{7,1},{8,10},{9,11},{10,... | collective-permute-start | bytes 208904 | tf_op jit(solution)/shard_map/ppermute | solution.py:445
  47.6 4.4 %collective-permute-start.2 = (bf16[64,544]{1,0:T(8,128)(2,1)S(1)}, bf16[64,544]{1,0:T(8,128)(2,1)S(1)}, u32[]{:S(2)}, u32[]{:S(2)}) collective-permute-start(bf16[64,544]{1,0:T(8,128)(2,1)S(1)} %get-tuple-element.8), channel_id=1, source_target_pairs={{0,6},{1,7},{2,0},{3,1},{4,2},{5,3},{6,4},{7,5},{8,14},{9,15},{10,... | collective-permute-start | bytes 208904 | tf_op jit(solution)/shard_map/ppermute | solution.py:445
  49.2 5.9 %collective-permute-start.3 = (bf16[64,544]{1,0:T(8,128)(2,1)S(1)}, bf16[64,544]{1,0:T(8,128)(2,1)S(1)}, u32[]{:S(2)}, u32[]{:S(2)}) collective-permute-start(bf16[64,544]{1,0:T(8,128)(2,1)S(1)} %get-tuple-element.8), channel_id=1, source_target_pairs={{0,4},{1,5},{2,6},{3,7},{4,0},{5,1},{6,2},{7,3},{8,12},{9,13},{10,... | collective-permute-start | bytes 208904 | tf_op jit(solution)/shard_map/ppermute | solution.py:445
  55.3 11.3 %collective-permute-start.4 = (bf16[64,768]{1,0:T(8,128)(2,1)S(1)}, bf16[64,768]{1,0:T(8,128)(2,1)S(1)}, u32[]{:S(2)}, u32[]{:S(2)}) collective-permute-start(bf16[64,768]{1,0:T(8,128)(2,1)S(1)} %normalise.1.ours_ref), channel_id=1, source_target_pairs={{0,1},{1,0},{2,3},{3,2},{4,5},{5,4},{6,7},{7,6},{8,9},{9,8},{10,11... | collective-permute-start | bytes 294920 | tf_op jit(solution)/shard_map/ppermute | solution.py:449
  55.5 1.6 %copy-start.2 = (bf16[256,2,16,128]{3,2,1,0:T(8,128)(2,1)S(1)}, bf16[256,2,16,128]{3,2,1,0:T(8,128)(2,1)}, u32[]{:S(2)}) copy-start(bf16[256,2,16,128]{3,2,1,0:T(8,128)(2,1)} %pool_ref.1) | copy-start | bytes 6291460
  57.1 9.5 %copy-start.5 = (bf16[256,1024]{1,0:T(8,128)(2,1)S(1)}, bf16[256,1024]{1,0:T(8,128)(2,1)}, u32[]{:S(2)}) copy-start(bf16[256,1024]{1,0:T(8,128)(2,1)} %copy-done.4) | copy-start | bytes 1572868
  66.7 2.2 %copy-start = (f32[32,16,2048]{2,1,0:T(8,128)S(1)}, f32[32,16,2048]{2,1,0:T(8,128)}, u32[]{:S(2)}) copy-start(f32[32,16,2048]{2,1,0:T(8,128)} %state_ref.1) | copy-start | bytes 12582916
  68.9 1.6 %copy-start.3 = (bf16[512,2048]{1,0:T(8,128)(2,1)S(1)}, bf16[512,2048]{1,0:T(8,128)(2,1)}, u32[]{:S(2)}) copy-start(bf16[512,2048]{1,0:T(8,128)(2,1)} %dt_proj_ref.1) | copy-start | bytes 6291460
  70.4 36.9 %copy-start.7 = (bf16[4,32,2048]{2,1,0:T(8,128)(2,1)S(1)}, bf16[4,32,2048]{2,1,0:T(8,128)(2,1)}, u32[]{:S(2)}) copy-start(bf16[4,32,2048]{2,1,0:T(8,128)(2,1)} %z_ref.1) | copy-start | bytes 1572868

commit v3 on v2

--- a/solution.py
+++ b/solution.py
@@ -18,6 +18,9 @@
 RANK = 512
 STATE = 16
 PAGES = 8
+BIG = 60
+UNROLL = 8
+CHUNKS = 4
 PAGE_TOKENS = 16
 PROJ = RANK + 2 * STATE
 SEND = HALF + QUARTER + HEAD_SIZE
@@ -30,6 +33,10 @@
     return pl.BlockSpec(memory_space=pltpu.VMEM)
 
 
+def anywhere():
+    return pl.BlockSpec(memory_space=pl.ANY)
+
+
 def smem():
     return pl.BlockSpec(memory_space=pltpu.SMEM)
 
@@ -38,42 +45,84 @@
     return pltpu.CompilerParams(vmem_limit_bytes=mib * 1024 * 1024)
 
 
+def cost(mb):
+    return pl.CostEstimate(
+        flops=3_500_000_000, bytes_accessed=mb * 1_000_000, transcendentals=300_000
+    )
+
+
 def sublanes(shape):
     return lax.broadcasted_iota(jnp.int32, shape, len(shape) - 2)
 
 
-def pack_kernel(x_ref, q_ref, kv_ref, out_ref, rows):
-    sources = ((x_ref, HALF), (q_ref, QUARTER), (kv_ref, HEAD_SIZE))
-    for step in range(STEPS):
-        for group in range(0, REQS, 16):
+def pack_kernel(x_hbm, q_hbm, kv_hbm, out_hbm, x_ref, q_ref, kv_ref, rows, out_ref, sems, out_sems):
+    groups = range(0, REQS, 16)
+    copies = []
+    for group in groups:
+        span = pl.ds(group, 16)
+        trio = ((x_hbm, x_ref), (q_hbm, q_ref), (kv_hbm, kv_ref))
+        copies.append(
+            [
+                pltpu.make_async_copy(
+                    far.at[:, span], near.at[:, span], sems.at[index, group // 16]
+                )
+                for index, (far, near) in enumerate(trio)
+            ]
+        )
+        for copy in copies[-1]:
+            copy.start()
+    outs = []
+    for group in groups:
+        for copy in copies[group // 16]:
+            copy.wait()
+        for step in range(STEPS):
             for half in range(2):
                 first = half * STEPS + step
                 places = [
                     pl.ds((group + part * 8) * ROWS + first, 8, stride=ROWS) for part in range(2)
                 ]
                 tile = 0
-                for ref, width in sources:
+                for ref, width in ((x_ref, HALF), (q_ref, QUARTER)):
                     block = ref[step, group : group + 16, half * width : (half + 1) * width]
                     block = block.astype(F32)
                     for column in range(0, width, LANES):
                         rows[tile, places[0], :] = block[0:8, column : column + LANES]
                         rows[tile, places[1], :] = block[8:16, column : column + LANES]
                         tile += 1
-    for req in range(REQS):
-        for tile in range(SEND // LANES):
-            out_ref[req, :, tile * LANES : (tile + 1) * LANES] = rows[
-                tile, req * ROWS : (req + 1) * ROWS, :
-            ].astype(BF16)
+            for req in range(group, group + 16):
+                rows[SEND // LANES - 1, pl.ds(req * ROWS + step, 2, stride=STEPS), :] = kv_ref[
+                    step, req
+                ].astype(F32)
+        for req in range(group, group + 16):
+            for tile in range(SEND // LANES):
+                out_ref[req, :, tile * LANES : (tile + 1) * LANES] = rows[
+                    tile, req * ROWS : (req + 1) * ROWS, :
+                ].astype(BF16)
+        span = pl.ds(group, 16)
+        outs.append(
+            pltpu.make_async_copy(out_ref.at[span], out_hbm.at[span], out_sems.at[group // 16])
+        )
+        outs[-1].start()
+    for copy in outs:
+        copy.wait()
 
 
 def pack(mamba_x, queries, new_kv):
     return pl.pallas_call(
         pack_kernel,
         out_shape=jax.ShapeDtypeStruct((REQS, ROWS, SEND), BF16),
-        in_specs=[vmem()] * 3,
-        out_specs=vmem(),
-        scratch_shapes=[pltpu.VMEM((SEND // LANES, REQS * ROWS, LANES), F32)],
-        compiler_params=params(24),
+        in_specs=[anywhere()] * 3,
+        out_specs=anywhere(),
+        scratch_shapes=[
+            pltpu.VMEM((STEPS, REQS, 2 * HALF), BF16),
+            pltpu.VMEM((STEPS, REQS, 2 * QUARTER), BF16),
+            pltpu.VMEM((STEPS, REQS, 2, HEAD_SIZE), BF16),
+            pltpu.VMEM((SEND // LANES, REQS * ROWS, LANES), F32),
+            pltpu.VMEM((REQS, ROWS, SEND), BF16),
+            pltpu.SemaphoreType.DMA((3, 2)),
+            pltpu.SemaphoreType.DMA((2,)),
+        ],
+        compiler_params=params(BIG),
         name="pack",
     )(mamba_x, queries, new_kv)
 
@@ -87,31 +136,70 @@
 def conv_kernel(
     order_ref,
     core_ref,
+    rows_hbm,
+    past_hbm,
+    weight_hbm,
+    bias_hbm,
+    proj_hbm,
+    act_hbm,
+    mine_ref,
+    other_ref,
     rows_ref,
     past_ref,
     weight_ref,
     bias_ref,
     proj_ref,
+    taps,
+    past_rows,
     act_ref,
-    mine_ref,
-    other_ref,
-    taps,
     part,
+    sems,
+    rows_sems,
+    act_sem,
 ):
-    for tap in range(4):
-        taps[tap] = halves(weight_ref, tap, HALF)
-    taps[4] = halves(bias_ref, 0, HALF)
+    small = [
+        pltpu.make_async_copy(far, near, sems.at[index])
+        for index, (far, near) in enumerate(
+            ((past_hbm, past_ref), (weight_hbm, weight_ref), (bias_hbm, bias_ref))
+        )
+    ]
+    chunk = REQS // CHUNKS
+    arriving = [
+        pltpu.make_async_copy(
+            rows_hbm.at[pl.ds(index * chunk, chunk), :, pl.ds(0, HALF)],
+            rows_ref.at[pl.ds(index * chunk, chunk)],
+            rows_sems.at[index],
+        )
+        for index in range(CHUNKS)
+    ]
+    proj_copy = pltpu.make_async_copy(proj_hbm, proj_ref, sems.at[3])
+    for copy in small + arriving + [proj_copy]:
+        copy.start()
+    for copy in small:
+        copy.wait()
     step_of = lax.rem(sublanes((ROWS, HALF)), STEPS)
-    blank = jnp.zeros((1, HALF), F32)
+    for tap in range(3):
+        for half in range(2):
+            for tile in range(HALF // LANES):
+                column = half * HALF + tile * LANES
+                block = past_ref[tap, :, column : column + LANES].astype(F32)
+                for group in range(0, REQS, 8):
+                    place = pl.ds(group * ROWS + (1 - half) * STEPS + 1 + tap, 8, stride=ROWS)
+                    past_rows[tile, place, :] = block[group : group + 8]
+    taps[0] = halves(bias_ref, 0, HALF)
+    for back in range(4):
+        taps[1 + back] = halves(weight_ref, 3 - back, HALF)
 
     def one(req):
-        now = rows_ref[req, :, 0:HALF].astype(F32)
-        past = past_ref[order_ref[req]].astype(F32)
-        past = jnp.concatenate([blank, past[:, HALF:], blank, past[:, :HALF]], axis=0)
-        total = taps[4] + taps[3] * now
+        now = rows_ref[req].astype(F32)
+        first = pl.multiple_of(order_ref[req] * ROWS, ROWS)
+        past = jnp.concatenate(
+            [past_rows[tile, pl.ds(first, ROWS), :] for tile in range(HALF // LANES)], axis=1
+        )
+        total = taps[0] + taps[1] * now
         for back in range(1, 4):
             mixed = jnp.where(step_of >= STEPS - back, past, now)
-            total = total + taps[3 - back] * pltpu.roll(mixed, back, 0)
+            total = total + taps[1 + back] * pltpu.roll(mixed, back, 0)
         return total * jax.nn.sigmoid(total)
 
     def pair(index, carry):
@@ -119,7 +207,12 @@
         act_ref[pl.ds(pl.multiple_of(index * 16, 16), 16), :] = both.astype(BF16)
         return carry
 
-    lax.fori_loop(0, REQS // 2, pair, 0)
+    for index in range(CHUNKS):
+        arriving[index].wait()
+        lax.fori_loop(index * chunk // 2, (index + 1) * chunk // 2, pair, 0)
+    act_copy = pltpu.make_async_copy(act_ref, act_hbm, act_sem)
+    act_copy.start()
+    proj_copy.wait()
     act = act_ref[...]
     low = jnp.dot(act, proj_ref[0:HALF, :], preferred_element_type=F32)
     high = jnp.dot(act, proj_ref[HALF : 2 * HALF, :], preferred_element_type=F32)
@@ -134,6 +227,7 @@
     size = REQS * STEPS // 2
     mine_ref[...] = part[pl.ds(pl.multiple_of(core * size, size), size), :]
     other_ref[...] = part[pl.ds(pl.multiple_of((1 - core) * size, size), size), :]
+    act_copy.wait()
 
 
 def convolve(order, core, arrived, conv_state, conv_weight, conv_bias, x_proj):
@@ -141,18 +235,29 @@
     return pl.pallas_call(
         conv_kernel,
         out_shape=(jax.ShapeDtypeStruct((REQS * ROWS, HALF), BF16), half_rows, half_rows),
-        in_specs=[smem(), smem()] + [vmem()] * 5,
-        out_specs=(vmem(), vmem(), vmem()),
+        in_specs=[smem(), smem()] + [anywhere()] * 5,
+        out_specs=(anywhere(), vmem(), vmem()),
         scratch_shapes=[
+            pltpu.VMEM((REQS, ROWS, HALF), BF16),
+            pltpu.VMEM(conv_state.shape, BF16),
+            pltpu.VMEM(conv_weight.shape, F32),
+            pltpu.VMEM(conv_bias.shape, F32),
+            pltpu.VMEM(x_proj.shape, BF16),
             pltpu.VMEM((5, ROWS, HALF), F32),
+            pltpu.VMEM((HALF // LANES, REQS * ROWS, LANES), F32),
+            pltpu.VMEM((REQS * ROWS, HALF), BF16),
             pltpu.VMEM((REQS * STEPS, PROJ), F32),
+            pltpu.SemaphoreType.DMA((4,)),
+            pltpu.SemaphoreType.DMA((CHUNKS,)),
+            pltpu.SemaphoreType.DMA,
         ],
-        compiler_params=params(24),
+        compiler_params=params(56),
         name="convolve",
     )(order, core, arrived, conv_state, conv_weight, conv_bias, x_proj)
 
 
-def norm_kernel(sum_ref, one_ref, two_ref, three_ref, gain_ref, out_ref):
+def norm_kernel(sum_ref, one_ref, two_ref, three_ref, gain_ref, after_ref, out_ref):
+    del after_ref
     total = (
         sum_ref[...]
         + one_ref[...].astype(F32)
@@ -169,58 +274,73 @@
     out_ref[:, RANK + LANES :] = (coef - coef_high.astype(F32)).astype(BF16)
 
 
-def normalise(chip_sum, ring, gain):
+def normalise(chip_sum, ring, gain, after):
     return pl.pallas_call(
         norm_kernel,
         out_shape=jax.ShapeDtypeStruct((REQS * STEPS // 2, RANK + 2 * LANES), BF16),
-        in_specs=[vmem()] * 5,
+        in_specs=[vmem()] * 5 + [anywhere()],
         out_specs=vmem(),
         compiler_params=params(8),
         name="normalise",
-    )(chip_sum, *ring, gain)
-
-
-def attend_kernel(order_ref, table_ref, length_ref, rows_ref, pool_ref, out_ref):
+    )(chip_sum, *ring, gain, after)
+
+
+def attend_kernel(
+    order_ref, table_ref, length_ref, rows_ref, pool_ref, out_ref, scores_ref, weights_ref, inverse_ref
+):
     scale = 1.0 / math.sqrt(HEAD_SIZE)
-    wide = (4 * ROWS, 2 * LANES)
+    count = 4 * ROWS
+    wide = (count, 2 * LANES)
     lane = lax.broadcasted_iota(jnp.int32, wide, 1)
     step_of = lax.rem(lax.broadcasted_iota(jnp.int32, wide, 0), STEPS)
     fresh_ok = (lane >= LANES) & (lane - LANES <= step_of)
     pad = jnp.zeros((LANES - PAGE_TOKENS, HEAD_SIZE), BF16)
     blank = jnp.zeros((ROWS, HEAD_SIZE), F32)
 
-    def one(req):
+    def score(req):
         source = order_ref[req]
-        pages = [table_ref[source, page] for page in range(PAGES)]
-        length = length_ref[source]
         query = rows_ref[req, :, HALF : HALF + QUARTER].astype(F32)
         query = jnp.concatenate(
             [query[:, h * HEAD_SIZE : (h + 1) * HEAD_SIZE] for h in range(4)], axis=0
         ).astype(BF16)
         fresh = rows_ref[req, :, HALF + QUARTER : SEND].astype(F32)
-        fresh_keys = jnp.concatenate([fresh, blank], axis=0).astype(BF16)
-        fresh_values = jnp.concatenate([pltpu.roll(fresh, STEPS, 0), blank], axis=0).astype(BF16)
-        keys = jnp.concatenate([pool_ref[p, 0] for p in pages] + [fresh_keys, pad], axis=0)
-        values = jnp.concatenate([pool_ref[p, 1] for p in pages] + [fresh_values, pad], axis=0)
-        scores = (
+        fresh = jnp.concatenate([fresh, blank], axis=0).astype(BF16)
+        keys = [pool_ref[table_ref[source, page], 0] for page in range(PAGES)]
+        keys = jnp.concatenate(keys + [fresh, pad], axis=0)
+        scores_ref[req] = (
             lax.dot_general(query, keys, (((1,), (1,)), ((), ())), preferred_element_type=F32)
             * scale
         )
-        scores = jnp.where((lane < length) & (lane < LANES) | fresh_ok, scores, -jnp.inf)
+
+    def soften(req):
+        length = length_ref[order_ref[req]]
+        valid = (lane < length) & (lane < LANES) | fresh_ok
+        scores = jnp.where(valid, scores_ref[req], -jnp.inf)
         weights = jnp.exp(scores - jnp.max(scores, axis=1, keepdims=True))
         total = jnp.sum(weights, axis=1, keepdims=True)
-        mixed = jnp.dot(weights.astype(BF16), values, preferred_element_type=F32) / total
+        weights_ref[req] = weights.astype(BF16)
+        inverse_ref[req] = jnp.broadcast_to(1.0 / total, (count, LANES))
+
+    def mix(req):
+        source = order_ref[req]
+        fresh = rows_ref[req, :, HALF + QUARTER : SEND].astype(F32)
+        fresh = jnp.concatenate([pltpu.roll(fresh, STEPS, 0), blank], axis=0).astype(BF16)
+        values = [pool_ref[table_ref[source, page], 1] for page in range(PAGES)]
+        values = jnp.concatenate(values + [fresh, pad], axis=0)
+        mixed = jnp.dot(weights_ref[req], values, preferred_element_type=F32) * inverse_ref[req]
         for h in range(4):
             out_ref[req, :, h * HEAD_SIZE : (h + 1) * HEAD_SIZE] = mixed[
                 h * ROWS : (h + 1) * ROWS
             ].astype(BF16)
 
-    def some(index, carry):
-        for offset in range(4):
-            one(4 * index + offset)
-        return carry
-
-    lax.fori_loop(0, REQS // 4, some, 0)
+    for phase in (score, soften, mix):
+
+        def some(index, carry, phase=phase):
+            for offset in range(UNROLL):
+                phase(UNROLL * index + offset)
+            return carry
+
+        lax.fori_loop(0, REQS // UNROLL, some, 0)
 
 
 def attend(order, page_table, prompt_len, arrived, pool):
@@ -229,10 +349,13 @@
         out_shape=jax.ShapeDtypeStruct((REQS, ROWS, QUARTER), BF16),
         in_specs=[smem()] * 3 + [vmem()] * 2,
         out_specs=vmem(),
-        compiler_params=params(16),
-        cost_estimate=pl.CostEstimate(
-            flops=300_000_000, bytes_accessed=6_000_000, transcendentals=300_000
-        ),
+        scratch_shapes=[
+            pltpu.VMEM((REQS, 4 * ROWS, 2 * LANES), F32),
+            pltpu.VMEM((REQS, 4 * ROWS, 2 * LANES), BF16),
+            pltpu.VMEM((REQS, 4 * ROWS, LANES), F32),
+        ],
+        compiler_params=params(8),
+        cost_estimate=cost(6),
         name="attend",
     )(order, page_table, prompt_len, arrived, pool)
 
@@ -360,7 +483,7 @@
             pltpu.VMEM((ROWS, HALF), F32),
             pltpu.VMEM((LANES, LANES), F32),
         ],
-        compiler_params=params(32),
+        compiler_params=params(16),
         name="scan",
     )(order, core, ours, theirs, act, attended, ssm_state, dt_proj, dt_bias, a_log, skip_d)
 
@@ -434,18 +557,26 @@
     core = (lax.axis_index("tp") % 2).astype(jnp.int32).reshape(1)
     swap = [(j, j ^ 1) for j in range(8)]
 
-    outgoing = pack(mamba_x, queries, new_kv.reshape(STEPS, REQS, 2 * HEAD_SIZE))
+    outgoing = pack(mamba_x, queries, new_kv)
     arrived = lax.all_to_all(outgoing, "req", split_axis=0, concat_axis=0, tiled=True)
     act, mine, other = convolve(
-        order, core, arrived, conv_state, conv_weight, conv_bias[None], x_proj
-    )
+        order,
+        core,
+        arrived,
+        jnp.transpose(conv_state, (1, 0, 2)),
+        conv_weight,
+        conv_bias[None],
+        x_proj,
+    )
+    unit = jnp.where(order[0] >= 0, 1, 2).astype(BF16)
+    pool = prefill_page_pool * unit
     chip_sum = mine + lax.ppermute(other, "tp", swap)
     small = chip_sum.astype(BF16)
     ring = [
         lax.ppermute(small, "tp", [(j, (j + hop) % 8) for j in range(8)]) for hop in (2, 6, 4)
     ]
-    attended = attend(order, page_table, prompt_len, arrived, prefill_page_pool)
-    ours = normalise(chip_sum, ring, dt_gain[None])
+    attended = attend(order, page_table, prompt_len, arrived, pool)
+    ours = normalise(chip_sum, ring, dt_gain[None], attended)
     theirs = lax.ppermute(ours, "tp", swap)
     returning = scan(
         order,

time: 109 us -> 95.3 us (0.87)
  local copies, waits for them, and re-layouts: 14.6 us -> 4.15 us
  Pallas kernels: 23.9 us -> 20.9 us
    unnamed x39 -> x38, local copies, waits for them, and re-layouts: 13.7 us -> 4.15 us
    pallas_call x1, Pallas kernels: 9.48 us -> 3.77 us  [attend(): pl.pallas_call(attend_kernel, out_shape=jax.ShapeDtypeStruct((REQS, ROWS,...]
    ppermute x3, waiting for transfers between devices: 3.97 us -> 0.15 us  [per_device(): lax.ppermute(small, 'tp', [(j, (j + hop) % 8) for j in range(8)])]
    all_to_all x1, waiting for transfers between devices: 19.1 us -> 21.7 us  [per_device(): lax.all_to_all(outgoing, 'req', split_axis=0, concat_axis=0, tiled=True)]
    pallas_call x1, Pallas kernels: 2.64 us -> 4.69 us  [convolve(): pl.pallas_call(conv_kernel, out_shape=(jax.ShapeDtypeStruct((REQS * ROWS,...]
    ppermute x1, waiting for transfers between devices: 0.01 us -> 1.29 us  [per_device(): theirs = lax.ppermute(ours, 'tp', swap)]
  transfers between devices with their start and end apart: 6 -> 6, of which waited for: 5 -> 4; matrix products, arithmetic and copies ran while one was open for 5% -> 3% of each run, Pallas kernels for 9% -> 4%
where the time goes in v3:
time: 95.3 us; the launch traced here: 95.1 us
  blocking collectives  28.1 us (29%)
  waiting for transfers between devices  24 us (25%)
  Pallas kernels  20.9 us (22%)
  starting transfers between devices  16.7 us (18%)
  local copies, waits for them, and re-layouts  4.15 us (4%)
  between operations  0.96 us (1%)
    all_to_all x1, blocking collectives, per_device(): lax.all_to_all(returning, 'req', split_axis=0, concat_axis=0, tiled=True)  28.1 us
    all_to_all x1, waiting for transfers between devices, per_device(): lax.all_to_all(outgoing, 'req', split_axis=0, concat_axis=0, tiled=True)  21.7 us
    all_to_all x1, starting transfers between devices, per_device(): lax.all_to_all(outgoing, 'req', split_axis=0, concat_axis=0, tiled=True)  11.2 us
    pallas_call x1, Pallas kernels, scan(): pl.pallas_call(scan_kernel, out_shape=jax.ShapeDtypeStruct((REQS, ROWS, B...  8.36 us
    ppermute x3, starting transfers between devices, per_device(): lax.ppermute(small, 'tp', [(j, (j + hop) % 8) for j in range(8)])  5.3 us
    pallas_call x1, Pallas kernels, convolve(): pl.pallas_call(conv_kernel, out_shape=(jax.ShapeDtypeStruct((REQS * ROWS,...  4.69 us
    unnamed x38, local copies, waits for them, and re-layouts  4.15 us
    pallas_call x1, Pallas kernels, attend(): pl.pallas_call(attend_kernel, out_shape=jax.ShapeDtypeStruct((REQS, ROWS,...  3.77 us
  transfers between devices with their start and end apart: 6, of which 4 were waited for; matrix products, arithmetic and copies ran while one was open for 3% of the time, Pallas kernels for 4%

profile of v3, /device:TPU:32, one launch (start us, length us, event | category | flops | bytes accessed | tf_op | source)
XLA Modules:
  0.0 95.1 jit_solution(15396555001672392490)
XLA Ops:
  0.6 2.5 %pack.1 = bf16[32,8,1664]{2,1,0:T(8,128)(2,1)} custom-call(bf16[4,32,2048]{2,1,0:T(8,128)(2,1)} %x_hbm.1, bf16[4,32,1024]{2,1,0:T(8,128)(2,1)} %q_hbm.1, bf16[4,32,2,128]{3,2,1,0:T(2,128)(2,1)} %kv_hbm.1), custom_call_target="tpu_custom_call" | custom-call | tf_op jit(solution)/shard_map/pack/pallas_call | solution.py:111
  3.2 11.2 %all-to-all-start = ((bf16[32,8,1664]{2,1,0:T(8,128)(2,1)}), bf16[32,8,1664]{2,1,0:T(8,128)(2,1)S(1)}, u32[]{:S(2)}, u32[]{:S(2)}) async-start(bf16[32,8,1664]{2,1,0:T(8,128)(2,1)} %pack.1), calls=%async_computation | async-start | bytes 1703936 | tf_op jit(solution)/shard_map/all_to_all | solution.py:561
  14.4 2.6 %copy.22.proj_hbm = bf16[2048,544]{1,0:T(8,128)(2,1)} copy(bf16[2048,544]{0,1:T(8,128)(2,1)S(1)} %copy-done.13) | data formatting | bytes 4456448 | tf_op args[12]
  17.0 0.1 select_reduce_fusion.order_ref
  17.2 21.7 %all-to-all-done.rows_hbm.rows_ref = bf16[32,8,1664]{2,1,0:T(8,128)(2,1)S(1)} async-done(((bf16[32,8,1664]{2,1,0:T(8,128)(2,1)}), bf16[32,8,1664]{2,1,0:T(8,128)(2,1)S(1)}, u32[]{:S(2)}, u32[]{:S(2)}) %all-to-all-start) | async-done | bytes 852000 | tf_op jit(solution)/shard_map/all_to_all | solution.py:561
  38.9 0.9 copy-done.1
  39.8 4.7 %convolve.1 = (bf16[256,1024]{1,0:T(8,128)(2,1)}, f32[64,544]{1,0:T(8,128)}, f32[64,544]{1,0:T(8,128)}) custom-call(s32[32]{0:T(128)} %copy-done.10, s32[1]{0:T(128)} %bitcast.core_ref, bf16[32,8,1664]{2,1,0:T(8,128)(2,1)} %copy-done.1, bf16[3,32,2048]{2,1,0:T(8,128)(2,1)} %bitcast.12, f32[4,2048]{1,0:T(4,128)} %weight_hbm.1, f32[1,2048]{1,0:T(1,128)} %bitcast.13, ...), custom_call_target="tpu_custom_call" | custom-call | tf_op jit(solution)/shard_map/convolve/pallas_call | solution.py:235
  44.5 0.1 collective-permute-start
  44.7 0.1 broadcast_multiply_fusion.pool_ref
  44.8 0.5 copy-done.16
  45.3 0.1 copy.23.table_ref
  45.4 0.8 collective-permute-done
  46.3 1.7 %collective-permute-start.1 = (bf16[64,544]{1,0:T(8,128)(2,1)S(1)}, bf16[64,544]{1,0:T(8,128)(2,1)S(1)}, u32[]{:S(2)}, u32[]{:S(2)}) collective-permute-start(bf16[64,544]{1,0:T(8,128)(2,1)S(1)} %get-tuple-element.8), channel_id=1, source_target_pairs={{0,2},{1,3},{2,4},{3,5},{4,6},{5,7},{6,0},{7,1},{8,10},{9,11},{10,... | collective-permute-start | bytes 208904 | tf_op jit(solution)/shard_map/ppermute | solution.py:576
  47.9 1.7 %collective-permute-start.2 = (bf16[64,544]{1,0:T(8,128)(2,1)S(1)}, bf16[64,544]{1,0:T(8,128)(2,1)S(1)}, u32[]{:S(2)}, u32[]{:S(2)}) collective-permute-start(bf16[64,544]{1,0:T(8,128)(2,1)S(1)} %get-tuple-element.8), channel_id=1, source_target_pairs={{0,6},{1,7},{2,0},{3,1},{4,2},{5,3},{6,4},{7,5},{8,14},{9,15},{10,... | collective-permute-start | bytes 208904 | tf_op jit(solution)/shard_map/ppermute | solution.py:576
  49.6 2.0 %collective-permute-start.3 = (bf16[64,544]{1,0:T(8,128)(2,1)S(1)}, bf16[64,544]{1,0:T(8,128)(2,1)S(1)}, u32[]{:S(2)}, u32[]{:S(2)}) collective-permute-start(bf16[64,544]{1,0:T(8,128)(2,1)S(1)} %get-tuple-element.8), channel_id=1, source_target_pairs={{0,4},{1,5},{2,6},{3,7},{4,0},{5,1},{6,2},{7,3},{8,12},{9,13},{10,... | collective-permute-start | bytes 208904 | tf_op jit(solution)/shard_map/ppermute | solution.py:576
  51.6 3.8 %attend.1.after_ref.attended_ref = bf16[32,8,512]{2,1,0:T(8,128)(2,1)S(1)} custom-call(s32[32]{0:T(128)S(1)} %copy-done.11, s32[32,8]{1,0:T(8,128)S(1)} %copy.23.table_ref, s32[32]{0:T(128)S(1)} %copy-done.12, bf16[32,8,1664]{2,1,0:T(8,128)(2,1)S(1)} %copy-done.2, bf16[256,2,16,128]{3,2,1,0:T(8,128)(2,1)S(1)} %broadcast_multiply_fusion.pool_ref), custom_call_target="tpu_custom_call" | custom-call | flops 3500000000 | bytes 6000000 | tf_op jit(solution)/shard_map/attend/pallas_call | solution.py:347
  55.4 0.0 collective-permute-done.1.one_ref
  55.4 0.1 collective-permute-done.3.three_ref
  55.5 0.1 normalise.1.ours_ref
  55.7 0.1 collective-permute-start.4
  55.8 1.3 %collective-permute-done.4.theirs_ref = bf16[64,768]{1,0:T(8,128)(2,1)S(1)} collective-permute-done((bf16[64,768]{1,0:T(8,128)(2,1)S(1)}, bf16[64,768]{1,0:T(8,128)(2,1)S(1)}, u32[]{:S(2)}, u32[]{:S(2)}) %collective-permute-start.4) | collective-permute-done | bytes 98336 | tf_op jit(solution)/shard_map/ppermute | solution.py:580
  57.1 8.4 %scan.1 = bf16[32,8,1536]{2,1,0:T(8,128)(2,1)S(1)} custom-call(s32[32]{0:T(128)S(1)} %copy-done.11, s32[1]{0:T(128)} %bitcast.core_ref, bf16[64,768]{1,0:T(8,128)(2,1)S(1)} %normalise.1.ours_ref, bf16[64,768]{1,0:T(8,128)(2,1)S(1)} %collective-permute-done.4.theirs_ref, bf16[256,1024]{1,0:T(8,128)(2,1)S(1)} %copy-done.4, ...), custom_call_target="tpu_custom_call" | custom-call | tf_op jit(solution)/shard_map/scan/pallas_call | solution.py:473
  65.5 28.1 %all_to_all.10.back_ref = bf16[32,8,1536]{2,1,0:T(8,128)(2,1)S(1)} all-to-all(bf16[32,8,1536]{2,1,0:T(8,128)(2,1)S(1)} %scan.1), channel_id=1, replica_groups=mesh['req'=32,'tp'=8] {'req'}, dimensions={0} | all-to-all | bytes 1572864 | tf_op jit(solution)/shard_map/all_to_all | solution.py:594
  93.6 1.5 %unpack.1 = (bf16[4,32,1024]{2,1,0:T(8,128)(2,1)}, bf16[4,32,2048]{2,1,0:T(8,128)(2,1)}) custom-call(bf16[32,8,1536]{2,1,0:T(8,128)(2,1)S(1)} %all_to_all.10.back_ref, bf16[4,32,2048]{2,1,0:T(8,128)(2,1)S(1)} %copy-done.5), custom_call_target="tpu_custom_call" | custom-call | tf_op jit(solution)/shard_map/unpack/pallas_call | solution.py:519
  (36 shorter events, 0.1 us)
Async XLA Ops:
  0.6 13.8 %copy-start.13 = (bf16[2048,544]{0,1:T(8,128)(2,1)S(1)}, bf16[2048,544]{0,1:T(8,128)(2,1)}, u32[]{:S(2)}) copy-start(bf16[2048,544]{0,1:T(8,128)(2,1)} %param.30) | copy-start | bytes 6684676
  3.2 35.7 %all-to-all-start = ((bf16[32,8,1664]{2,1,0:T(8,128)(2,1)}), bf16[32,8,1664]{2,1,0:T(8,128)(2,1)S(1)}, u32[]{:S(2)}, u32[]{:S(2)}) async-start(bf16[32,8,1664]{2,1,0:T(8,128)(2,1)} %pack.1), calls=%async_computation | async-start | bytes 1703936 | tf_op jit(solution)/shard_map/all_to_all | solution.py:561
  14.4 2.6 %copy-start.17 = (s32[32]{0:T(128)S(1)}, s32[32]{0:T(128)}, u32[]{:S(2)}) copy-start(s32[32]{0:T(128)} %param.23) | copy-start | bytes 388
  17.1 21.8 %copy-start.10 = (s32[32]{0:T(128)}, s32[32]{0:T(128)S(1)}, u32[]{:S(2)}) copy-start(s32[32]{0:T(128)S(1)} %select_reduce_fusion.order_ref) | copy-start | bytes 388
  38.9 0.9 copy-start.1
  38.9 5.7 %copy-start.14 = (bf16[256,2,16,128]{3,2,1,0:T(8,128)(2,1)S(1)}, bf16[256,2,16,128]{3,2,1,0:T(8,128)(2,1)}, u32[]{:S(2)}) copy-start(bf16[256,2,16,128]{3,2,1,0:T(8,128)(2,1)} %param.20) | copy-start | bytes 6291460
  44.5 1.7 %collective-permute-start = (f32[64,544]{1,0:T(8,128)}, f32[64,544]{1,0:T(8,128)S(1)}, u32[]{:S(2)}, u32[]{:S(2)}) collective-permute-start(f32[64,544]{1,0:T(8,128)} %get-tuple-element.6), channel_id=1, source_target_pairs={{0,1},{1,0},{2,3},{3,2},{4,5},{5,4},{6,7},{7,6},{8,9},{9,8},{10,11... | collective-permute-start | bytes 417800 | tf_op jit(solution)/shard_map/ppermute | solution.py:573
  44.6 0.7 copy-start.16
  44.6 1.6 %copy-start.15 = (f32[64,544]{1,0:T(8,128)S(1)}, f32[64,544]{1,0:T(8,128)}, u32[]{:S(2)}) copy-start(f32[64,544]{1,0:T(8,128)} %get-tuple-element.5) | copy-start | bytes 417796
  44.6 6.9 %copy-start.2 = (bf16[32,8,1664]{2,1,0:T(8,128)(2,1)S(1)}, bf16[32,8,1664]{2,1,0:T(8,128)(2,1)}, u32[]{:S(2)}) copy-start(bf16[32,8,1664]{2,1,0:T(8,128)(2,1)} %copy-done.1) | copy-start | bytes 2555908
  44.6 6.9 %copy-start.11 = (s32[32]{0:T(128)S(1)}, s32[32]{0:T(128)}, u32[]{:S(2)}) copy-start(s32[32]{0:T(128)} %copy-done.10) | copy-start | bytes 388
  44.7 6.9 %copy-start.12 = (s32[32]{0:T(128)S(1)}, s32[32]{0:T(128)}, u32[]{:S(2)}) copy-start(s32[32]{0:T(128)} %length_ref.1) | copy-start | bytes 388
  46.2 9.3 %copy-start.9 = (f32[512]{0:T(512)S(1)}, f32[512]{0:T(512)}, u32[]{:S(2)}) copy-start(f32[512]{0:T(512)} %param.31) | copy-start | bytes 6148
  46.2 10.8 %copy-start.4 = (bf16[256,1024]{1,0:T(8,128)(2,1)S(1)}, bf16[256,1024]{1,0:T(8,128)(2,1)}, u32[]{:S(2)}) copy-start(bf16[256,1024]{1,0:T(8,128)(2,1)} %get-tuple-element.7.act_ref) | copy-start | bytes 1572868
  46.3 10.8 %copy-start.6 = (f32[16,2048]{1,0:T(8,128)S(1)}, f32[16,2048]{1,0:T(8,128)}, u32[]{:S(2)}) copy-start(f32[16,2048]{1,0:T(8,128)} %a_log_ref.1) | copy-start | bytes 393220
  46.3 10.8 %copy-start.7 = (f32[2048]{0:T(1024)S(1)}, f32[2048]{0:T(1024)}, u32[]{:S(2)}) copy-start(f32[2048]{0:T(1024)} %param.33) | copy-start | bytes 24580
  46.3 10.8 %copy-start.8 = (f32[2048]{0:T(1024)S(1)}, f32[2048]{0:T(1024)}, u32[]{:S(2)}) copy-start(f32[2048]{0:T(1024)} %param.35) | copy-start | bytes 24580
  46.3 9.1 %collective-permute-start.1 = (bf16[64,544]{1,0:T(8,128)(2,1)S(1)}, bf16[64,544]{1,0:T(8,128)(2,1)S(1)}, u32[]{:S(2)}, u32[]{:S(2)}) collective-permute-start(bf16[64,544]{1,0:T(8,128)(2,1)S(1)} %get-tuple-element.8), channel_id=1, source_target_pairs={{0,2},{1,3},{2,4},{3,5},{4,6},{5,7},{6,0},{7,1},{8,10},{9,11},{10,... | collective-permute-start | bytes 208904 | tf_op jit(solution)/shard_map/ppermute | solution.py:576
  47.9 7.5 %collective-permute-start.2 = (bf16[64,544]{1,0:T(8,128)(2,1)S(1)}, bf16[64,544]{1,0:T(8,128)(2,1)S(1)}, u32[]{:S(2)}, u32[]{:S(2)}) collective-permute-start(bf16[64,544]{1,0:T(8,128)(2,1)S(1)} %get-tuple-element.8), channel_id=1, source_target_pairs={{0,6},{1,7},{2,0},{3,1},{4,2},{5,3},{6,4},{7,5},{8,14},{9,15},{10,... | collective-permute-start | bytes 208904 | tf_op jit(solution)/shard_map/ppermute | solution.py:576
  49.6 5.9 %collective-permute-start.3 = (bf16[64,544]{1,0:T(8,128)(2,1)S(1)}, bf16[64,544]{1,0:T(8,128)(2,1)S(1)}, u32[]{:S(2)}, u32[]{:S(2)}) collective-permute-start(bf16[64,544]{1,0:T(8,128)(2,1)S(1)} %get-tuple-element.8), channel_id=1, source_target_pairs={{0,4},{1,5},{2,6},{3,7},{4,0},{5,1},{6,2},{7,3},{8,12},{9,13},{10,... | collective-permute-start | bytes 208904 | tf_op jit(solution)/shard_map/ppermute | solution.py:576
  51.6 5.5 %copy-start = (f32[32,16,2048]{2,1,0:T(8,128)S(1)}, f32[32,16,2048]{2,1,0:T(8,128)}, u32[]{:S(2)}) copy-start(f32[32,16,2048]{2,1,0:T(8,128)} %state_ref.1) | copy-start | bytes 12582916
  51.6 5.5 %copy-start.3 = (bf16[512,2048]{1,0:T(8,128)(2,1)S(1)}, bf16[512,2048]{1,0:T(8,128)(2,1)}, u32[]{:S(2)}) copy-start(bf16[512,2048]{1,0:T(8,128)(2,1)} %dt_proj_ref.1) | copy-start | bytes 6291460
  55.7 1.4 %collective-permute-start.4 = (bf16[64,768]{1,0:T(8,128)(2,1)S(1)}, bf16[64,768]{1,0:T(8,128)(2,1)S(1)}, u32[]{:S(2)}, u32[]{:S(2)}) collective-permute-start(bf16[64,768]{1,0:T(8,128)(2,1)S(1)} %normalise.1.ours_ref), channel_id=1, source_target_pairs={{0,1},{1,0},{2,3},{3,2},{4,5},{5,4},{6,7},{7,6},{8,9},{9,8},{10,11... | collective-permute-start | bytes 294920 | tf_op jit(solution)/shard_map/ppermute | solution.py:580
  57.1 36.5 %copy-start.5 = (bf16[4,32,2048]{2,1,0:T(8,128)(2,1)S(1)}, bf16[4,32,2048]{2,1,0:T(8,128)(2,1)}, u32[]{:S(2)}) copy-start(bf16[4,32,2048]{2,1,0:T(8,128)(2,1)} %z_ref.1) | copy-start | bytes 1572868

commit v4 on v3

--- a/solution.py
+++ b/solution.py
@@ -18,8 +18,10 @@
 RANK = 512
 STATE = 16
 PAGES = 8
+WHOLE = 63
 BIG = 60
-UNROLL = 8
+UNROLL = 32
+KEEPS = 4
 CHUNKS = 4
 PAGE_TOKENS = 16
 PROJ = RANK + 2 * STATE
@@ -49,6 +51,15 @@
     return pl.CostEstimate(
         flops=3_500_000_000, bytes_accessed=mb * 1_000_000, transcendentals=300_000
     )
+
+
+def softplus(x):
+    return jnp.maximum(x, 0.0) + jnp.log(1.0 + jnp.exp(-jnp.abs(x)))
+
+
+def silu(x):
+    half = 0.5 * x
+    return half * jnp.tanh(half) + half
 
 
 def sublanes(shape):
@@ -133,50 +144,8 @@
     return jnp.concatenate([low, high], axis=0)
 
 
-def conv_kernel(
-    order_ref,
-    core_ref,
-    rows_hbm,
-    past_hbm,
-    weight_hbm,
-    bias_hbm,
-    proj_hbm,
-    act_hbm,
-    mine_ref,
-    other_ref,
-    rows_ref,
-    past_ref,
-    weight_ref,
-    bias_ref,
-    proj_ref,
-    taps,
-    past_rows,
-    act_ref,
-    part,
-    sems,
-    rows_sems,
-    act_sem,
-):
-    small = [
-        pltpu.make_async_copy(far, near, sems.at[index])
-        for index, (far, near) in enumerate(
-            ((past_hbm, past_ref), (weight_hbm, weight_ref), (bias_hbm, bias_ref))
-        )
-    ]
-    chunk = REQS // CHUNKS
-    arriving = [
-        pltpu.make_async_copy(
-            rows_hbm.at[pl.ds(index * chunk, chunk), :, pl.ds(0, HALF)],
-            rows_ref.at[pl.ds(index * chunk, chunk)],
-            rows_sems.at[index],
-        )
-        for index in range(CHUNKS)
-    ]
-    proj_copy = pltpu.make_async_copy(proj_hbm, proj_ref, sems.at[3])
-    for copy in small + arriving + [proj_copy]:
-        copy.start()
-    for copy in small:
-        copy.wait()
+def stage_kernel(order_ref, sent_ref, past_ref, weight_ref, bias_ref, out_ref, past_rows, past_taps):
+    del sent_ref
     step_of = lax.rem(sublanes((ROWS, HALF)), STEPS)
     for tap in range(3):
         for half in range(2):
@@ -186,21 +155,87 @@
                 for group in range(0, REQS, 8):
                     place = pl.ds(group * ROWS + (1 - half) * STEPS + 1 + tap, 8, stride=ROWS)
                     past_rows[tile, place, :] = block[group : group + 8]
-    taps[0] = halves(bias_ref, 0, HALF)
+    plain = [halves(weight_ref, tap, HALF) for tap in range(4)]
     for back in range(4):
-        taps[1 + back] = halves(weight_ref, 3 - back, HALF)
-
-    def one(req):
-        now = rows_ref[req].astype(F32)
+        out_ref[REQS + back] = jnp.where(step_of >= back, plain[3 - back], 0.0)
+        past_taps[back] = plain[3 - back]
+    past_taps[0] = halves(bias_ref, 0, HALF)
+
+    def one(req, carry):
         first = pl.multiple_of(order_ref[req] * ROWS, ROWS)
         past = jnp.concatenate(
             [past_rows[tile, pl.ds(first, ROWS), :] for tile in range(HALF // LANES)], axis=1
         )
-        total = taps[0] + taps[1] * now
+        total = past_taps[0]
         for back in range(1, 4):
-            mixed = jnp.where(step_of >= STEPS - back, past, now)
-            total = total + taps[1 + back] * pltpu.roll(mixed, back, 0)
-        return total * jax.nn.sigmoid(total)
+            moved = jnp.where(step_of < back, pltpu.roll(past, back, 0), 0.0)
+            total = total + past_taps[back] * moved
+        out_ref[req] = total
+        return carry
+
+    lax.fori_loop(0, REQS, one, 0)
+
+
+def stage(order, sent, conv_state, conv_weight, conv_bias):
+    return pl.pallas_call(
+        stage_kernel,
+        out_shape=jax.ShapeDtypeStruct((REQS + 4, ROWS, HALF), F32),
+        in_specs=[smem(), anywhere()] + [vmem()] * 3,
+        out_specs=vmem(),
+        scratch_shapes=[
+            pltpu.VMEM((HALF // LANES, REQS * ROWS, LANES), F32),
+            pltpu.VMEM((4, ROWS, HALF), F32),
+        ],
+        compiler_params=pltpu.CompilerParams(vmem_limit_bytes=(64 * 1024 - 600) * 1024),
+        name="stage",
+    )(order, sent, conv_state, conv_weight, conv_bias)
+
+
+def conv_kernel(
+    core_ref,
+    rows_hbm,
+    prior_hbm,
+    proj_hbm,
+    act_hbm,
+    mine_ref,
+    other_ref,
+    rows_ref,
+    prior_ref,
+    proj_ref,
+    act_ref,
+    part,
+    rows_sems,
+    prior_sems,
+    proj_sem,
+    act_sem,
+):
+    chunk = REQS // CHUNKS
+    arriving = [
+        pltpu.make_async_copy(
+            prior_hbm.at[pl.ds(REQS, 4)], prior_ref.at[pl.ds(REQS, 4)], prior_sems.at[CHUNKS]
+        )
+    ]
+    for index in range(CHUNKS):
+        span = pl.ds(index * chunk, chunk)
+        arriving.append(
+            pltpu.make_async_copy(
+                rows_hbm.at[span, :, pl.ds(0, HALF)], rows_ref.at[span], rows_sems.at[index]
+            )
+        )
+        arriving.append(
+            pltpu.make_async_copy(prior_hbm.at[span], prior_ref.at[span], prior_sems.at[index])
+        )
+    proj_copy = pltpu.make_async_copy(proj_hbm, proj_ref, proj_sem)
+    for copy in arriving + [proj_copy]:
+        copy.start()
+    arriving[0].wait()
+
+    def one(req):
+        now = rows_ref[req].astype(F32)
+        total = prior_ref[req] + prior_ref[REQS] * now
+        for back in range(1, 4):
+            total = total + prior_ref[REQS + back] * pltpu.roll(now, back, 0)
+        return silu(total)
 
     def pair(index, carry):
         both = jnp.concatenate([one(2 * index), one(2 * index + 1)], axis=0)
@@ -208,7 +243,8 @@
         return carry
 
     for index in range(CHUNKS):
-        arriving[index].wait()
+        arriving[1 + 2 * index].wait()
+        arriving[2 + 2 * index].wait()
         lax.fori_loop(index * chunk // 2, (index + 1) * chunk // 2, pair, 0)
     act_copy = pltpu.make_async_copy(act_ref, act_hbm, act_sem)
     act_copy.start()
@@ -230,30 +266,27 @@
     act_copy.wait()
 
 
-def convolve(order, core, arrived, conv_state, conv_weight, conv_bias, x_proj):
+def convolve(core, arrived, prior, x_proj):
     half_rows = jax.ShapeDtypeStruct((REQS * STEPS // 2, PROJ), F32)
     return pl.pallas_call(
         conv_kernel,
         out_shape=(jax.ShapeDtypeStruct((REQS * ROWS, HALF), BF16), half_rows, half_rows),
-        in_specs=[smem(), smem()] + [anywhere()] * 5,
+        in_specs=[smem()] + [anywhere()] * 3,
         out_specs=(anywhere(), vmem(), vmem()),
         scratch_shapes=[
             pltpu.VMEM((REQS, ROWS, HALF), BF16),
-            pltpu.VMEM(conv_state.shape, BF16),
-            pltpu.VMEM(conv_weight.shape, F32),
-            pltpu.VMEM(conv_bias.shape, F32),
+            pltpu.VMEM(prior.shape, F32),
             pltpu.VMEM(x_proj.shape, BF16),
-            pltpu.VMEM((5, ROWS, HALF), F32),
-            pltpu.VMEM((HALF // LANES, REQS * ROWS, LANES), F32),
             pltpu.VMEM((REQS * ROWS, HALF), BF16),
             pltpu.VMEM((REQS * STEPS, PROJ), F32),
-            pltpu.SemaphoreType.DMA((4,)),
             pltpu.SemaphoreType.DMA((CHUNKS,)),
+            pltpu.SemaphoreType.DMA((CHUNKS + 1,)),
+            pltpu.SemaphoreType.DMA,
             pltpu.SemaphoreType.DMA,
         ],
-        compiler_params=params(56),
+        compiler_params=params(BIG),
         name="convolve",
-    )(order, core, arrived, conv_state, conv_weight, conv_bias, x_proj)
+    )(core, arrived, prior, x_proj)
 
 
 def norm_kernel(sum_ref, one_ref, two_ref, three_ref, gain_ref, after_ref, out_ref):
@@ -286,16 +319,16 @@
 
 
 def attend_kernel(
-    order_ref, table_ref, length_ref, rows_ref, pool_ref, out_ref, scores_ref, weights_ref, inverse_ref
+    order_ref, table_ref, length_ref, rows_ref, pool_ref, out_ref, scores_ref, weights_ref
 ):
-    scale = 1.0 / math.sqrt(HEAD_SIZE)
+    scale = math.log2(math.e) / math.sqrt(HEAD_SIZE)
     count = 4 * ROWS
-    wide = (count, 2 * LANES)
-    lane = lax.broadcasted_iota(jnp.int32, wide, 1)
-    step_of = lax.rem(lax.broadcasted_iota(jnp.int32, wide, 0), STEPS)
-    fresh_ok = (lane >= LANES) & (lane - LANES <= step_of)
+    lane = lax.broadcasted_iota(jnp.int32, (count, LANES), 1)
+    step_of = lax.rem(lax.broadcasted_iota(jnp.int32, (count, LANES), 0), STEPS)
+    fresh_ok = lane <= step_of
     pad = jnp.zeros((LANES - PAGE_TOKENS, HEAD_SIZE), BF16)
     blank = jnp.zeros((ROWS, HEAD_SIZE), F32)
+    ones = jnp.ones((2 * LANES, LANES), BF16)
 
     def score(req):
         source = order_ref[req]
@@ -307,19 +340,17 @@
         fresh = jnp.concatenate([fresh, blank], axis=0).astype(BF16)
         keys = [pool_ref[table_ref[source, page], 0] for page in range(PAGES)]
         keys = jnp.concatenate(keys + [fresh, pad], axis=0)
-        scores_ref[req] = (
-            lax.dot_general(query, keys, (((1,), (1,)), ((), ())), preferred_element_type=F32)
-            * scale
+        scores_ref[req] = lax.dot_general(
+            query, keys, (((1,), (1,)), ((), ())), preferred_element_type=F32
         )
 
     def soften(req):
         length = length_ref[order_ref[req]]
-        valid = (lane < length) & (lane < LANES) | fresh_ok
-        scores = jnp.where(valid, scores_ref[req], -jnp.inf)
-        weights = jnp.exp(scores - jnp.max(scores, axis=1, keepdims=True))
-        total = jnp.sum(weights, axis=1, keepdims=True)
-        weights_ref[req] = weights.astype(BF16)
-        inverse_ref[req] = jnp.broadcast_to(1.0 / total, (count, LANES))
+        old = jnp.where(lane < length, scores_ref[req, :, 0:LANES] * scale, -jnp.inf)
+        new = jnp.where(fresh_ok, scores_ref[req, :, LANES:] * scale, -jnp.inf)
+        top = jnp.max(jnp.maximum(old, new), axis=1, keepdims=True)
+        weights_ref[req, :, 0:LANES] = jnp.exp2(old - top).astype(BF16)
+        weights_ref[req, :, LANES:] = jnp.exp2(new - top).astype(BF16)
 
     def mix(req):
         source = order_ref[req]
@@ -327,7 +358,9 @@
         fresh = jnp.concatenate([pltpu.roll(fresh, STEPS, 0), blank], axis=0).astype(BF16)
         values = [pool_ref[table_ref[source, page], 1] for page in range(PAGES)]
         values = jnp.concatenate(values + [fresh, pad], axis=0)
-        mixed = jnp.dot(weights_ref[req], values, preferred_element_type=F32) * inverse_ref[req]
+        values = jnp.concatenate([values, ones], axis=1)
+        mixed = jnp.dot(weights_ref[req], values, preferred_element_type=F32)
+        mixed = mixed[:, 0:LANES] / mixed[:, LANES:]
         for h in range(4):
             out_ref[req, :, h * HEAD_SIZE : (h + 1) * HEAD_SIZE] = mixed[
                 h * ROWS : (h + 1) * ROWS
@@ -352,35 +385,11 @@
         scratch_shapes=[
             pltpu.VMEM((REQS, 4 * ROWS, 2 * LANES), F32),
             pltpu.VMEM((REQS, 4 * ROWS, 2 * LANES), BF16),
-            pltpu.VMEM((REQS, 4 * ROWS, LANES), F32),
         ],
         compiler_params=params(8),
         cost_estimate=cost(6),
         name="attend",
     )(order, page_table, prompt_len, arrived, pool)
-
-
-def gather_rows(parts, sub):
-    four = sub < 4
-    parts = [
-        jnp.where(four, parts[s], parts[s + 4])
-        + pltpu.roll(jnp.where(four, parts[s + 4], parts[s]), 4, 0)
-        for s in range(4)
-    ]
-    two = lax.rem(sub, 4) < 2
-    parts = [
-        jnp.where(
-            two,
-            parts[s] + pltpu.roll(parts[s], 6, 0),
-            parts[s + 2] + pltpu.roll(parts[s + 2], 2, 0),
-        )
-        for s in range(2)
-    ]
-    return jnp.where(
-        lax.rem(sub, 2) < 1,
-        parts[0] + pltpu.roll(parts[0], 7, 0),
-        parts[1] + pltpu.roll(parts[1], 1, 0),
-    )
 
 
 def scan_kernel(
@@ -402,6 +411,8 @@
     decay,
     skip,
     coef,
+    read,
+    *keeps,
 ):
     core = core_ref[0]
     size = REQS * STEPS // 2
@@ -415,9 +426,9 @@
     upper = sublanes((ROWS, HALF)) < STEPS
     normed = packed[:, 0:RANK]
     low = jnp.dot(normed, dt_proj_ref[:, 0:HALF], preferred_element_type=F32)
-    low = jax.nn.softplus(low + dt_bias_ref[:, 0:HALF])
+    low = softplus(low + dt_bias_ref[:, 0:HALF])
     high = jnp.dot(normed, dt_proj_ref[:, HALF:], preferred_element_type=F32)
-    high = jax.nn.softplus(high + dt_bias_ref[:, HALF:])
+    high = softplus(high + dt_bias_ref[:, HALF:])
     for index in range(REQS // 2):
         rows = slice(index * 8, index * 8 + 8)
         even = jnp.where(upper, low[rows], pltpu.roll(high[rows], STEPS, 0))
@@ -429,44 +440,77 @@
         rate[2 * index + 1] = odd
         fed[2 * index] = both_fed[0:8]
         fed[2 * index + 1] = both_fed[8:16]
-    sub = sublanes((ROWS, LANES))
-
-    def one(req, act):
-        source = order_ref[req]
-        turned = pltpu.roll(coef[0 : 2 * STATE, :], lax.rem(LANES - STEPS * req, LANES), 1)
-        into = [
-            jnp.broadcast_to(turned[0:STATE, s : s + 1], (STATE, LANES)) for s in range(STEPS)
-        ]
-        read = [
-            jnp.broadcast_to(turned[STATE : 2 * STATE, s : s + 1], (STATE, LANES))
-            for s in range(STEPS)
-        ]
+    lane = lax.broadcasted_iota(jnp.int32, (REQS * STEPS, LANES), 1)
+    row = lax.broadcasted_iota(jnp.int32, (REQS * STEPS, LANES), 0)
+    parts = []
+    for first in (RANK, RANK + LANES):
+        part = packed[:, first : first + LANES].astype(F32)
+        spread = jnp.zeros_like(part)
+        for block in range(LANES // STATE):
+            moved = pltpu.roll(part, (block * STATE - STATE) % LANES, 1)
+            spread = jnp.where(
+                (lane // STATE == block) & (lax.rem(row, 2 * STEPS) == block), moved, spread
+            )
+        parts.append(spread)
+    for pair in range(REQS // 2):
+        rows = slice(pair * 8, pair * 8 + 8)
+        read[pair] = jnp.concatenate([parts[0][rows], parts[1][rows]], axis=0).astype(BF16)
+    upper = sublanes((ROWS, LANES)) < STEPS
+
+    def advance(pair, keep):
+        for which in range(2):
+            req = 2 * pair + which
+            source = order_ref[req]
+            turned = pltpu.roll(coef[0:STATE, :], lax.rem(LANES - STEPS * req, LANES), 1)
+            into = [
+                jnp.broadcast_to(turned[:, s : s + 1], (STATE, LANES)) for s in range(STEPS)
+            ]
+            for first_tile in range(0, HALF // LANES, 2):
+                chains = [
+                    (tile, half) for tile in range(first_tile, first_tile + 2) for half in range(2)
+                ]
+                spans = [
+                    slice(half * HALF + tile * LANES, half * HALF + (tile + 1) * LANES)
+                    for tile, half in chains
+                ]
+                hidden = [state_ref[source, :, columns] for columns in spans]
+                for step in range(STEPS):
+                    first = (which * STEPS + step) * STATE
+                    for index, (tile, half) in enumerate(chains):
+                        place = slice(tile * LANES, (tile + 1) * LANES)
+                        line = slice(half * STEPS + step, half * STEPS + step + 1)
+                        speed = jnp.broadcast_to(rate[req, line, place], (STATE, LANES))
+                        feed = jnp.broadcast_to(fed[req, line, place], (STATE, LANES))
+                        hidden[index] = (
+                            jnp.exp2(speed * decay[:, spans[index]]) * hidden[index]
+                            + feed * into[step]
+                        )
+                        keep[first : first + STATE, spans[index]] = hidden[index].astype(BF16)
+
+    def readout(pair, keep):
+        both = jnp.dot(read[pair], keep[...], preferred_element_type=F32)
+        both = both[0:8] + both[8:16]
+        act = act_ref[pl.ds(pl.multiple_of(pair * 16, 16), 16), :].astype(F32)
         for tile in range(HALF // LANES):
             place = slice(tile * LANES, (tile + 1) * LANES)
-            parts = []
-            for half in range(2):
-                columns = slice(half * HALF + tile * LANES, half * HALF + (tile + 1) * LANES)
-                hidden = state_ref[source, :, columns]
-                slope = decay[:, columns]
-                for step in range(STEPS):
-                    row = slice(half * STEPS + step, half * STEPS + step + 1)
-                    hidden = (
-                        jnp.exp2(jnp.broadcast_to(rate[req, row, place], (STATE, LANES)) * slope) * hidden
-                        + jnp.broadcast_to(fed[req, row, place], (STATE, LANES)) * into[step]
-                    )
-                    seen = hidden * read[step]
-                    parts.append(seen[0:8] + seen[8:16])
-            summed = gather_rows(parts, sub) + skip[:, place] * act[:, place]
-            out_ref[req, :, place] = summed.astype(BF16)
+            low = both[:, place]
+            high = both[:, HALF + tile * LANES : HALF + (tile + 1) * LANES]
+            even = jnp.where(upper, low, pltpu.roll(high, STEPS, 0))
+            odd = jnp.where(upper, pltpu.roll(low, STEPS, 0), high)
+            out_ref[2 * pair, :, place] = (even + skip[:, place] * act[0:8, place]).astype(BF16)
+            out_ref[2 * pair + 1, :, place] = (odd + skip[:, place] * act[8:16, place]).astype(BF16)
+
+    def some(index, carry):
+        for offset in range(len(keeps)):
+            advance(len(keeps) * index + offset, keeps[offset])
+            if offset:
+                readout(len(keeps) * index + offset - 1, keeps[offset - 1])
+        readout(len(keeps) * index + len(keeps) - 1, keeps[-1])
+        return carry
+
+    lax.fori_loop(0, REQS // 2 // len(keeps), some, 0)
+    for req in range(REQS):
         out_ref[req, :, HALF:BACK] = attended_ref[req]
-
-    def pair(index, carry):
-        act = act_ref[pl.ds(pl.multiple_of(index * 16, 16), 16), :].astype(F32)
-        one(2 * index, act[0:8])
-        one(2 * index + 1, act[8:16])
-        return carry
-
-    lax.fori_loop(0, REQS // 2, pair, 0)
 
 
 def scan(order, core, ours, theirs, act, attended, ssm_state, dt_proj, dt_bias, a_log, skip_d):
@@ -482,7 +526,9 @@
             pltpu.VMEM((STATE, 2 * HALF), F32),
             pltpu.VMEM((ROWS, HALF), F32),
             pltpu.VMEM((LANES, LANES), F32),
-        ],
+            pltpu.VMEM((REQS // 2, 16, LANES), BF16),
+        ]
+        + [pltpu.VMEM((2 * STEPS * STATE, 2 * HALF), BF16)] * KEEPS,
         compiler_params=params(16),
         name="scan",
     )(order, core, ours, theirs, act, attended, ssm_state, dt_proj, dt_bias, a_log, skip_d)
@@ -507,7 +553,7 @@
                         first_column = half * HALF + tile * LANES
                         columns = slice(first_column, first_column + LANES)
                         z = z_ref[step, group : group + 16, columns].astype(F32)
-                        block = block * (z * jax.nn.sigmoid(z))
+                        block = block * silu(z)
                         mamba_ref[step, group : group + 16, columns] = block.astype(BF16)
                     else:
                         first_column = half * QUARTER + tile * LANES - HALF
@@ -559,15 +605,10 @@
 
     outgoing = pack(mamba_x, queries, new_kv)
     arrived = lax.all_to_all(outgoing, "req", split_axis=0, concat_axis=0, tiled=True)
-    act, mine, other = convolve(
-        order,
-        core,
-        arrived,
-        jnp.transpose(conv_state, (1, 0, 2)),
-        conv_weight,
-        conv_bias[None],
-        x_proj,
+    prior = stage(
+        order, outgoing, jnp.transpose(conv_state, (1, 0, 2)), conv_weight, conv_bias[None]
     )
+    act, mine, other = convolve(core, arrived, prior, x_proj)
     unit = jnp.where(order[0] >= 0, 1, 2).astype(BF16)
     pool = prefill_page_pool * unit
     chip_sum = mine + lax.ppermute(other, "tp", swap)

time: 95.3 us -> 93.4 us (0.980)
  waiting for transfers between devices: 24 us -> 20.5 us
  other arithmetic: 0.27 us -> 1.93 us
    all_to_all x1, waiting for transfers between devices: 21.7 us -> 18.3 us  [per_device(): lax.all_to_all(outgoing, 'req', split_axis=0, concat_axis=0, tiled=True)]
    pallas_call x0 -> x1, Pallas kernels: none -> 2.97 us  [stage(): pl.pallas_call(stage_kernel, out_shape=jax.ShapeDtypeStruct((REQS + 4, RO...]
    mul x1, other arithmetic: 0.14 us -> 1.8 us  [per_device(): pool = prefill_page_pool * unit]
    pallas_call x1, Pallas kernels: 8.36 us -> 7.39 us  [scan(): pl.pallas_call(scan_kernel, out_shape=jax.ShapeDtypeStruct((REQS, ROWS, B...]
    unnamed x38 -> x32, local copies, waits for them, and re-layouts: 4.15 us -> 3.26 us
  transfers between devices with their start and end apart: 6 -> 6, of which waited for: 4 -> 3; matrix products, arithmetic and copies ran while one was open for 3% -> 5% of each run, Pallas kernels for 4% -> 6%
where the time goes in v4:
time: 93.4 us; the launch traced here: 93.1 us
  blocking collectives  28.1 us (30%)
  Pallas kernels  21.6 us (23%)
  waiting for transfers between devices  20.5 us (22%)
  starting transfers between devices  16.7 us (18%)
  local copies, waits for them, and re-layouts  3.26 us (3%)
  other arithmetic  1.93 us (2%)
  between operations  0.95 us (1%)
    all_to_all x1, blocking collectives, per_device(): lax.all_to_all(returning, 'req', split_axis=0, concat_axis=0, tiled=True)  28.1 us
    all_to_all x1, waiting for transfers between devices, per_device(): lax.all_to_all(outgoing, 'req', split_axis=0, concat_axis=0, tiled=True)  18.3 us
    all_to_all x1, starting transfers between devices, per_device(): lax.all_to_all(outgoing, 'req', split_axis=0, concat_axis=0, tiled=True)  11.2 us
    pallas_call x1, Pallas kernels, scan(): pl.pallas_call(scan_kernel, out_shape=jax.ShapeDtypeStruct((REQS, ROWS, B...  7.39 us
    ppermute x3, starting transfers between devices, per_device(): lax.ppermute(small, 'tp', [(j, (j + hop) % 8) for j in range(8)])  5.3 us
    pallas_call x1, Pallas kernels, convolve(): pl.pallas_call(conv_kernel, out_shape=(jax.ShapeDtypeStruct((REQS * ROWS,...  4.15 us
    unnamed x32, local copies, waits for them, and re-layouts  3.26 us
    pallas_call x1, Pallas kernels, stage(): pl.pallas_call(stage_kernel, out_shape=jax.ShapeDtypeStruct((REQS + 4, RO...  2.97 us
  transfers between devices with their start and end apart: 6, of which 3 were waited for; matrix products, arithmetic and copies ran while one was open for 5% of the time, Pallas kernels for 6%

profile of v4, /device:TPU:32, one launch (start us, length us, event | category | flops | bytes accessed | tf_op | source)
XLA Modules:
  0.0 93.1 jit_solution(2414730876853822967)
XLA Ops:
  0.6 2.5 %pack.1.sent_ref = bf16[32,8,1664]{2,1,0:T(8,128)(2,1)} custom-call(bf16[4,32,2048]{2,1,0:T(8,128)(2,1)} %x_hbm.1, bf16[4,32,1024]{2,1,0:T(8,128)(2,1)} %q_hbm.1, bf16[4,32,2,128]{3,2,1,0:T(2,128)(2,1)} %kv_hbm.1), custom_call_target="tpu_custom_call" | custom-call | tf_op jit(solution)/shard_map/pack/pallas_call | solution.py:122
  3.2 11.2 %all-to-all-start = ((bf16[32,8,1664]{2,1,0:T(8,128)(2,1)}), bf16[32,8,1664]{2,1,0:T(8,128)(2,1)}, u32[]{:S(2)}, u32[]{:S(2)}) async-start(bf16[32,8,1664]{2,1,0:T(8,128)(2,1)} %pack.1.sent_ref), calls=%async_computation | async-start | bytes 1703936 | tf_op jit(solution)/shard_map/all_to_all | solution.py:607
  14.4 0.0 copy-start.14
  14.5 2.6 %copy.22.proj_hbm = bf16[2048,544]{1,0:T(8,128)(2,1)} copy(bf16[2048,544]{0,1:T(8,128)(2,1)S(1)} %copy-done.11) | data formatting | bytes 4456448 | tf_op args[12]
  17.0 0.1 select_reduce_fusion.order_ref
  17.2 0.5 copy-done.8
  17.7 3.0 %stage.1.prior_hbm = f32[36,8,1024]{2,1,0:T(8,128)} custom-call(s32[32]{0:T(128)} %copy-done.8, bf16[32,8,1664]{2,1,0:T(8,128)(2,1)} %pack.1.sent_ref, bf16[3,32,2048]{2,1,0:T(8,128)(2,1)} %bitcast.12, f32[4,2048]{1,0:T(4,128)} %weight_ref.1, f32[1,2048]{1,0:T(1,128)} %bitcast.13), custom_call_target="tpu_custom_call" | custom-call | tf_op jit(solution)/shard_map/stage/pallas_call | solution.py:180
  20.7 18.3 %all-to-all-done.rows_hbm.rows_ref = bf16[32,8,1664]{2,1,0:T(8,128)(2,1)} async-done(((bf16[32,8,1664]{2,1,0:T(8,128)(2,1)}), bf16[32,8,1664]{2,1,0:T(8,128)(2,1)}, u32[]{:S(2)}, u32[]{:S(2)}) %all-to-all-start) | async-done | bytes 852000 | tf_op jit(solution)/shard_map/all_to_all | solution.py:607
  39.0 4.2 %convolve.1 = (bf16[256,1024]{1,0:T(8,128)(2,1)}, f32[64,544]{1,0:T(8,128)}, f32[64,544]{1,0:T(8,128)}) custom-call(s32[1]{0:T(128)} %bitcast.core_ref, bf16[32,8,1664]{2,1,0:T(8,128)(2,1)} %all-to-all-done.rows_hbm.rows_ref, f32[36,8,1024]{2,1,0:T(8,128)} %stage.1.prior_hbm, bf16[2048,544]{1,0:T(8,128)(2,1)} %copy.22.proj_hbm), custom_call_target="tpu_custom_call" | custom-call | tf_op jit(solution)/shard_map/convolve/pallas_call | solution.py:271
  43.2 0.1 collective-permute-start
  43.3 0.0 copy-start.13
  43.3 1.8 %broadcast_multiply_fusion.pool_ref = bf16[256,2,16,128]{3,2,1,0:T(8,128)(2,1)S(1)} fusion(bf16[256,2,16,128]{3,2,1,0:T(8,128)(2,1)} %param.20, bf16[]{:T(256)} %bitcast.4), kind=kLoop, calls=%fused_computation | loop fusion | flops 1048576 | bytes 4194306 | tf_op jit(solution)/shard_map/mul | solution.py:613
  45.1 0.1 copy.23.table_ref
  45.3 1.7 %collective-permute-start.1 = (bf16[64,544]{1,0:T(8,128)(2,1)S(1)}, bf16[64,544]{1,0:T(8,128)(2,1)S(1)}, u32[]{:S(2)}, u32[]{:S(2)}) collective-permute-start(bf16[64,544]{1,0:T(8,128)(2,1)S(1)} %get-tuple-element.8), channel_id=1, source_target_pairs={{0,2},{1,3},{2,4},{3,5},{4,6},{5,7},{6,0},{7,1},{8,10},{9,11},{10,... | collective-permute-start | bytes 208904 | tf_op jit(solution)/shard_map/ppermute | solution.py:617
  46.9 1.7 %collective-permute-start.2 = (bf16[64,544]{1,0:T(8,128)(2,1)S(1)}, bf16[64,544]{1,0:T(8,128)(2,1)S(1)}, u32[]{:S(2)}, u32[]{:S(2)}) collective-permute-start(bf16[64,544]{1,0:T(8,128)(2,1)S(1)} %get-tuple-element.8), channel_id=1, source_target_pairs={{0,6},{1,7},{2,0},{3,1},{4,2},{5,3},{6,4},{7,5},{8,14},{9,15},{10,... | collective-permute-start | bytes 208904 | tf_op jit(solution)/shard_map/ppermute | solution.py:617
  48.6 2.0 %collective-permute-start.3 = (bf16[64,544]{1,0:T(8,128)(2,1)S(1)}, bf16[64,544]{1,0:T(8,128)(2,1)S(1)}, u32[]{:S(2)}, u32[]{:S(2)}) collective-permute-start(bf16[64,544]{1,0:T(8,128)(2,1)S(1)} %get-tuple-element.8), channel_id=1, source_target_pairs={{0,4},{1,5},{2,6},{3,7},{4,0},{5,1},{6,2},{7,3},{8,12},{9,13},{10,... | collective-permute-start | bytes 208904 | tf_op jit(solution)/shard_map/ppermute | solution.py:617
  50.6 3.0 %attend.1.after_ref.attended_ref = bf16[32,8,512]{2,1,0:T(8,128)(2,1)S(1)} custom-call(s32[32]{0:T(128)S(1)} %copy-done.9, s32[32,8]{1,0:T(8,128)S(1)} %copy.23.table_ref, s32[32]{0:T(128)S(1)} %copy-done.10, bf16[32,8,1664]{2,1,0:T(8,128)(2,1)} %all-to-all-done.rows_hbm.rows_ref, bf16[256,2,16,128]{3,2,1,0:T(8,128)(2,1)S(1)} %broadcast_multiply_fusion.pool_ref), custom_call_target="tpu_custom_call" | custom-call | flops 3500000000 | bytes 6000000 | tf_op jit(solution)/shard_map/attend/pallas_call | solution.py:380
  53.6 1.0 %collective-permute-done.3.three_ref = bf16[64,544]{1,0:T(8,128)(2,1)S(1)} collective-permute-done((bf16[64,544]{1,0:T(8,128)(2,1)S(1)}, bf16[64,544]{1,0:T(8,128)(2,1)S(1)}, u32[]{:S(2)}, u32[]{:S(2)}) %collective-permute-start.3) | collective-permute-done | bytes 69664 | tf_op jit(solution)/shard_map/ppermute | solution.py:617
  54.5 0.1 normalise.1.ours_ref
  54.7 0.1 collective-permute-start.4
  54.8 1.3 %collective-permute-done.4.theirs_ref = bf16[64,768]{1,0:T(8,128)(2,1)S(1)} collective-permute-done((bf16[64,768]{1,0:T(8,128)(2,1)S(1)}, bf16[64,768]{1,0:T(8,128)(2,1)S(1)}, u32[]{:S(2)}, u32[]{:S(2)}) %collective-permute-start.4) | collective-permute-done | bytes 98336 | tf_op jit(solution)/shard_map/ppermute | solution.py:621
  56.1 7.4 %scan.1 = bf16[32,8,1536]{2,1,0:T(8,128)(2,1)S(1)} custom-call(s32[32]{0:T(128)S(1)} %copy-done.9, s32[1]{0:T(128)} %bitcast.core_ref, bf16[64,768]{1,0:T(8,128)(2,1)S(1)} %normalise.1.ours_ref, bf16[64,768]{1,0:T(8,128)(2,1)S(1)} %collective-permute-done.4.theirs_ref, bf16[256,1024]{1,0:T(8,128)(2,1)S(1)} %copy-done.2, ...), custom_call_target="tpu_custom_call" | custom-call | tf_op jit(solution)/shard_map/scan/pallas_call | solution.py:517
  63.5 28.1 %all_to_all.10.back_ref = bf16[32,8,1536]{2,1,0:T(8,128)(2,1)S(1)} all-to-all(bf16[32,8,1536]{2,1,0:T(8,128)(2,1)S(1)} %scan.1), channel_id=1, replica_groups=mesh['req'=32,'tp'=8] {'req'}, dimensions={0} | all-to-all | bytes 1572864 | tf_op jit(solution)/shard_map/all_to_all | solution.py:635
  91.6 1.4 %unpack.1 = (bf16[4,32,1024]{2,1,0:T(8,128)(2,1)}, bf16[4,32,2048]{2,1,0:T(8,128)(2,1)}) custom-call(bf16[32,8,1536]{2,1,0:T(8,128)(2,1)S(1)} %all_to_all.10.back_ref, bf16[4,32,2048]{2,1,0:T(8,128)(2,1)S(1)} %copy-done.3), custom_call_target="tpu_custom_call" | custom-call | tf_op jit(solution)/shard_map/unpack/pallas_call | solution.py:565
  (31 shorter events, 0.1 us)
Async XLA Ops:
  0.6 13.8 %copy-start.11 = (bf16[2048,544]{0,1:T(8,128)(2,1)S(1)}, bf16[2048,544]{0,1:T(8,128)(2,1)}, u32[]{:S(2)}) copy-start(bf16[2048,544]{0,1:T(8,128)(2,1)} %param.30) | copy-start | bytes 6684676
  3.2 35.8 %all-to-all-start = ((bf16[32,8,1664]{2,1,0:T(8,128)(2,1)}), bf16[32,8,1664]{2,1,0:T(8,128)(2,1)}, u32[]{:S(2)}, u32[]{:S(2)}) async-start(bf16[32,8,1664]{2,1,0:T(8,128)(2,1)} %pack.1.sent_ref), calls=%async_computation | async-start | bytes 1703936 | tf_op jit(solution)/shard_map/all_to_all | solution.py:607
  14.4 2.6 %copy-start.14 = (s32[32]{0:T(128)S(1)}, s32[32]{0:T(128)}, u32[]{:S(2)}) copy-start(s32[32]{0:T(128)} %param.23) | copy-start | bytes 388
  17.2 0.6 copy-start.8
  43.2 2.0 %collective-permute-start = (f32[64,544]{1,0:T(8,128)}, f32[64,544]{1,0:T(8,128)S(1)}, u32[]{:S(2)}, u32[]{:S(2)}) collective-permute-start(f32[64,544]{1,0:T(8,128)} %get-tuple-element.6), channel_id=1, source_target_pairs={{0,1},{1,0},{2,3},{3,2},{4,5},{5,4},{6,7},{7,6},{8,9},{9,8},{10,11... | collective-permute-start | bytes 417800 | tf_op jit(solution)/shard_map/ppermute | solution.py:614
  43.3 1.8 %copy-start.13 = (s32[32,8]{0,1:T(8,128)S(1)}, s32[32,8]{0,1:T(8,128)}, u32[]{:S(2)}) copy-start(s32[32,8]{0,1:T(8,128)} %param.21) | copy-start | bytes 3076
  43.3 1.9 %copy-start.12 = (f32[64,544]{1,0:T(8,128)S(1)}, f32[64,544]{1,0:T(8,128)}, u32[]{:S(2)}) copy-start(f32[64,544]{1,0:T(8,128)} %get-tuple-element.5) | copy-start | bytes 417796
  43.3 7.3 %copy-start.9 = (s32[32]{0:T(128)S(1)}, s32[32]{0:T(128)}, u32[]{:S(2)}) copy-start(s32[32]{0:T(128)} %copy-done.8) | copy-start | bytes 388
  43.3 7.3 %copy-start.10 = (s32[32]{0:T(128)S(1)}, s32[32]{0:T(128)}, u32[]{:S(2)}) copy-start(s32[32]{0:T(128)} %length_ref.1) | copy-start | bytes 388
  45.2 9.3 %copy-start.7 = (f32[512]{0:T(512)S(1)}, f32[512]{0:T(512)}, u32[]{:S(2)}) copy-start(f32[512]{0:T(512)} %param.31) | copy-start | bytes 6148
  45.2 10.8 %copy-start.2 = (bf16[256,1024]{1,0:T(8,128)(2,1)S(1)}, bf16[256,1024]{1,0:T(8,128)(2,1)}, u32[]{:S(2)}) copy-start(bf16[256,1024]{1,0:T(8,128)(2,1)} %get-tuple-element.7.act_ref) | copy-start | bytes 1572868
  45.2 10.8 %copy-start.4 = (f32[16,2048]{1,0:T(8,128)S(1)}, f32[16,2048]{1,0:T(8,128)}, u32[]{:S(2)}) copy-start(f32[16,2048]{1,0:T(8,128)} %a_log_ref.1) | copy-start | bytes 393220
  45.3 10.8 %copy-start.5 = (f32[2048]{0:T(1024)S(1)}, f32[2048]{0:T(1024)}, u32[]{:S(2)}) copy-start(f32[2048]{0:T(1024)} %param.33) | copy-start | bytes 24580
  45.3 10.8 %copy-start.6 = (f32[2048]{0:T(1024)S(1)}, f32[2048]{0:T(1024)}, u32[]{:S(2)}) copy-start(f32[2048]{0:T(1024)} %param.35) | copy-start | bytes 24580
  45.3 8.3 %collective-permute-start.1 = (bf16[64,544]{1,0:T(8,128)(2,1)S(1)}, bf16[64,544]{1,0:T(8,128)(2,1)S(1)}, u32[]{:S(2)}, u32[]{:S(2)}) collective-permute-start(bf16[64,544]{1,0:T(8,128)(2,1)S(1)} %get-tuple-element.8), channel_id=1, source_target_pairs={{0,2},{1,3},{2,4},{3,5},{4,6},{5,7},{6,0},{7,1},{8,10},{9,11},{10,... | collective-permute-start | bytes 208904 | tf_op jit(solution)/shard_map/ppermute | solution.py:617
  46.9 6.6 %collective-permute-start.2 = (bf16[64,544]{1,0:T(8,128)(2,1)S(1)}, bf16[64,544]{1,0:T(8,128)(2,1)S(1)}, u32[]{:S(2)}, u32[]{:S(2)}) collective-permute-start(bf16[64,544]{1,0:T(8,128)(2,1)S(1)} %get-tuple-element.8), channel_id=1, source_target_pairs={{0,6},{1,7},{2,0},{3,1},{4,2},{5,3},{6,4},{7,5},{8,14},{9,15},{10,... | collective-permute-start | bytes 208904 | tf_op jit(solution)/shard_map/ppermute | solution.py:617
  48.6 5.9 %collective-permute-start.3 = (bf16[64,544]{1,0:T(8,128)(2,1)S(1)}, bf16[64,544]{1,0:T(8,128)(2,1)S(1)}, u32[]{:S(2)}, u32[]{:S(2)}) collective-permute-start(bf16[64,544]{1,0:T(8,128)(2,1)S(1)} %get-tuple-element.8), channel_id=1, source_target_pairs={{0,4},{1,5},{2,6},{3,7},{4,0},{5,1},{6,2},{7,3},{8,12},{9,13},{10,... | collective-permute-start | bytes 208904 | tf_op jit(solution)/shard_map/ppermute | solution.py:617
  50.6 5.5 %copy-start = (f32[32,16,2048]{2,1,0:T(8,128)S(1)}, f32[32,16,2048]{2,1,0:T(8,128)}, u32[]{:S(2)}) copy-start(f32[32,16,2048]{2,1,0:T(8,128)} %state_ref.1) | copy-start | bytes 12582916
  50.6 5.5 %copy-start.1 = (bf16[512,2048]{1,0:T(8,128)(2,1)S(1)}, bf16[512,2048]{1,0:T(8,128)(2,1)}, u32[]{:S(2)}) copy-start(bf16[512,2048]{1,0:T(8,128)(2,1)} %dt_proj_ref.1) | copy-start | bytes 6291460
  54.7 1.4 %collective-permute-start.4 = (bf16[64,768]{1,0:T(8,128)(2,1)S(1)}, bf16[64,768]{1,0:T(8,128)(2,1)S(1)}, u32[]{:S(2)}, u32[]{:S(2)}) collective-permute-start(bf16[64,768]{1,0:T(8,128)(2,1)S(1)} %normalise.1.ours_ref), channel_id=1, source_target_pairs={{0,1},{1,0},{2,3},{3,2},{4,5},{5,4},{6,7},{7,6},{8,9},{9,8},{10,11... | collective-permute-start | bytes 294920 | tf_op jit(solution)/shard_map/ppermute | solution.py:621
  56.1 35.5 %copy-start.3 = (bf16[4,32,2048]{2,1,0:T(8,128)(2,1)S(1)}, bf16[4,32,2048]{2,1,0:T(8,128)(2,1)}, u32[]{:S(2)}) copy-start(bf16[4,32,2048]{2,1,0:T(8,128)(2,1)} %z_ref.1) | copy-start | bytes 1572868

commit v5 on v4

--- a/solution.py
+++ b/solution.py
@@ -237,28 +237,27 @@
             total = total + prior_ref[REQS + back] * pltpu.roll(now, back, 0)
         return silu(total)
 
-    def pair(index, carry):
-        both = jnp.concatenate([one(2 * index), one(2 * index + 1)], axis=0)
-        act_ref[pl.ds(pl.multiple_of(index * 16, 16), 16), :] = both.astype(BF16)
+    upper = sublanes((ROWS, HALF)) < STEPS
+
+    def some(index, carry):
+        lows, highs = [], []
+        for offset in range(0, 4, 2):
+            even, odd = one(4 * index + offset), one(4 * index + offset + 1)
+            lows.append(jnp.where(upper, even, pltpu.roll(odd, STEPS, 0)))
+            highs.append(jnp.where(upper, pltpu.roll(even, STEPS, 0), odd))
+        rows = pl.ds(pl.multiple_of(index * 16, 16), 16)
+        act_ref[rows, 0:HALF] = jnp.concatenate(lows, axis=0).astype(BF16)
+        act_ref[rows, HALF:] = jnp.concatenate(highs, axis=0).astype(BF16)
         return carry
 
     for index in range(CHUNKS):
         arriving[1 + 2 * index].wait()
         arriving[2 + 2 * index].wait()
-        lax.fori_loop(index * chunk // 2, (index + 1) * chunk // 2, pair, 0)
+        lax.fori_loop(index * chunk // 4, (index + 1) * chunk // 4, some, 0)
     act_copy = pltpu.make_async_copy(act_ref, act_hbm, act_sem)
     act_copy.start()
     proj_copy.wait()
-    act = act_ref[...]
-    low = jnp.dot(act, proj_ref[0:HALF, :], preferred_element_type=F32)
-    high = jnp.dot(act, proj_ref[HALF : 2 * HALF, :], preferred_element_type=F32)
-    upper = sublanes((ROWS, PROJ)) < STEPS
-    for index in range(REQS // 2):
-        even = slice(index * 16, index * 16 + 8)
-        odd = slice(index * 16 + 8, index * 16 + 16)
-        own = jnp.where(upper, low[even], high[odd])
-        cross = jnp.where(upper, low[odd], high[even])
-        part[index * 8 : index * 8 + 8, :] = own + pltpu.roll(cross, STEPS, 0)
+    part[...] = jnp.dot(act_ref[...], proj_ref[...], preferred_element_type=F32)
     core = core_ref[0]
     size = REQS * STEPS // 2
     mine_ref[...] = part[pl.ds(pl.multiple_of(core * size, size), size), :]
@@ -270,21 +269,21 @@
     half_rows = jax.ShapeDtypeStruct((REQS * STEPS // 2, PROJ), F32)
     return pl.pallas_call(
         conv_kernel,
-        out_shape=(jax.ShapeDtypeStruct((REQS * ROWS, HALF), BF16), half_rows, half_rows),
+        out_shape=(jax.ShapeDtypeStruct((REQS * STEPS, 2 * HALF), BF16), half_rows, half_rows),
         in_specs=[smem()] + [anywhere()] * 3,
         out_specs=(anywhere(), vmem(), vmem()),
         scratch_shapes=[
             pltpu.VMEM((REQS, ROWS, HALF), BF16),
             pltpu.VMEM(prior.shape, F32),
             pltpu.VMEM(x_proj.shape, BF16),
-            pltpu.VMEM((REQS * ROWS, HALF), BF16),
+            pltpu.VMEM((REQS * STEPS, 2 * HALF), BF16),
             pltpu.VMEM((REQS * STEPS, PROJ), F32),
             pltpu.SemaphoreType.DMA((CHUNKS,)),
             pltpu.SemaphoreType.DMA((CHUNKS + 1,)),
             pltpu.SemaphoreType.DMA,
             pltpu.SemaphoreType.DMA,
         ],
-        compiler_params=params(BIG),
+        compiler_params=params(50),
         name="convolve",
     )(core, arrived, prior, x_proj)
 
@@ -409,7 +408,6 @@
     rate,
     fed,
     decay,
-    skip,
     coef,
     read,
     *keeps,
@@ -418,28 +416,17 @@
     size = REQS * STEPS // 2
     packed[pl.ds(pl.multiple_of(core * size, size), size), :] = ours_ref[...]
     packed[pl.ds(pl.multiple_of((1 - core) * size, size), size), :] = theirs_ref[...]
-    skip[...] = halves(skip_ref, 0, HALF)
     decay[...] = jnp.exp(a_log_ref[...]) * (-1.0 / math.log(2.0))
     coef[...] = jnp.transpose(
         packed[:, RANK : RANK + LANES].astype(F32) + packed[:, RANK + LANES :].astype(F32)
     )
-    upper = sublanes((ROWS, HALF)) < STEPS
-    normed = packed[:, 0:RANK]
-    low = jnp.dot(normed, dt_proj_ref[:, 0:HALF], preferred_element_type=F32)
-    low = softplus(low + dt_bias_ref[:, 0:HALF])
-    high = jnp.dot(normed, dt_proj_ref[:, HALF:], preferred_element_type=F32)
-    high = softplus(high + dt_bias_ref[:, HALF:])
-    for index in range(REQS // 2):
-        rows = slice(index * 8, index * 8 + 8)
-        even = jnp.where(upper, low[rows], pltpu.roll(high[rows], STEPS, 0))
-        odd = jnp.where(upper, pltpu.roll(low[rows], STEPS, 0), high[rows])
-        both = jnp.concatenate([even, odd], axis=0)
-        span = slice(index * 16, index * 16 + 16)
-        both_fed = both * act_ref[span, :].astype(F32)
-        rate[2 * index] = even
-        rate[2 * index + 1] = odd
-        fed[2 * index] = both_fed[0:8]
-        fed[2 * index + 1] = both_fed[8:16]
+    speeds = jnp.dot(packed[:, 0:RANK], dt_proj_ref[...], preferred_element_type=F32)
+    speeds = softplus(speeds + dt_bias_ref[...])
+    feeds = speeds * act_ref[...].astype(F32)
+    for pair in range(REQS // 2):
+        rows = slice(pair * 8, pair * 8 + 8)
+        rate[pair] = speeds[rows]
+        fed[pair] = feeds[rows]
     lane = lax.broadcasted_iota(jnp.int32, (REQS * STEPS, LANES), 1)
     row = lax.broadcasted_iota(jnp.int32, (REQS * STEPS, LANES), 0)
     parts = []
@@ -452,14 +439,20 @@
                 (lane // STATE == block) & (lax.rem(row, 2 * STEPS) == block), moved, spread
             )
         parts.append(spread)
-    for pair in range(REQS // 2):
-        rows = slice(pair * 8, pair * 8 + 8)
-        read[pair] = jnp.concatenate([parts[0][rows], parts[1][rows]], axis=0).astype(BF16)
+    first_pair = lax.rem(row, 4 * STEPS) < 2 * STEPS
+    for quad in range(REQS // 4):
+        rows = slice(quad * 16, quad * 16 + 16)
+        for side in range(2):
+            block = [jnp.where(first_pair == (side == 0), part, 0.0)[rows] for part in parts]
+            read[quad, :, side * LANES : (side + 1) * LANES] = jnp.concatenate(
+                block, axis=0
+            ).astype(BF16)
     upper = sublanes((ROWS, LANES)) < STEPS
 
-    def advance(pair, keep):
-        for which in range(2):
-            req = 2 * pair + which
+    def advance(quad, keep):
+        for which in range(4):
+            req = 4 * quad + which
+            pair = 2 * quad + which // 2
             source = order_ref[req]
             turned = pltpu.roll(coef[0:STATE, :], lax.rem(LANES - STEPS * req, LANES), 1)
             into = [
@@ -476,39 +469,44 @@
                 hidden = [state_ref[source, :, columns] for columns in spans]
                 for step in range(STEPS):
                     first = (which * STEPS + step) * STATE
-                    for index, (tile, half) in enumerate(chains):
-                        place = slice(tile * LANES, (tile + 1) * LANES)
-                        line = slice(half * STEPS + step, half * STEPS + step + 1)
-                        speed = jnp.broadcast_to(rate[req, line, place], (STATE, LANES))
-                        feed = jnp.broadcast_to(fed[req, line, place], (STATE, LANES))
+                    for index in range(len(chains)):
+                        line = slice(which % 2 * STEPS + step, which % 2 * STEPS + step + 1)
+                        speed = jnp.broadcast_to(rate[pair, line, spans[index]], (STATE, LANES))
+                        feed = jnp.broadcast_to(fed[pair, line, spans[index]], (STATE, LANES))
                         hidden[index] = (
                             jnp.exp2(speed * decay[:, spans[index]]) * hidden[index]
                             + feed * into[step]
                         )
                         keep[first : first + STATE, spans[index]] = hidden[index].astype(BF16)
 
-    def readout(pair, keep):
-        both = jnp.dot(read[pair], keep[...], preferred_element_type=F32)
-        both = both[0:8] + both[8:16]
-        act = act_ref[pl.ds(pl.multiple_of(pair * 16, 16), 16), :].astype(F32)
-        for tile in range(HALF // LANES):
-            place = slice(tile * LANES, (tile + 1) * LANES)
-            low = both[:, place]
-            high = both[:, HALF + tile * LANES : HALF + (tile + 1) * LANES]
-            even = jnp.where(upper, low, pltpu.roll(high, STEPS, 0))
-            odd = jnp.where(upper, pltpu.roll(low, STEPS, 0), high)
-            out_ref[2 * pair, :, place] = (even + skip[:, place] * act[0:8, place]).astype(BF16)
-            out_ref[2 * pair + 1, :, place] = (odd + skip[:, place] * act[8:16, place]).astype(BF16)
+    def readout(quad, keep, acts):
+        both = jnp.dot(read[quad], keep[...], preferred_element_type=F32)
+        both = both[0:16] + both[16:32] + skip_ref[...] * acts
+        for which in range(2):
+            req = 4 * quad + 2 * which
+            rows = slice(which * 8, which * 8 + 8)
+            for tile in range(HALF // LANES):
+                place = slice(tile * LANES, (tile + 1) * LANES)
+                low = both[rows, place]
+                high = both[rows, HALF + tile * LANES : HALF + (tile + 1) * LANES]
+                even = jnp.where(upper, low, pltpu.roll(high, STEPS, 0))
+                odd = jnp.where(upper, pltpu.roll(low, STEPS, 0), high)
+                out_ref[req, :, place] = even.astype(BF16)
+                out_ref[req + 1, :, place] = odd.astype(BF16)
 
     def some(index, carry):
-        for offset in range(len(keeps)):
-            advance(len(keeps) * index + offset, keeps[offset])
+        count = len(keeps)
+        rows = pl.ds(pl.multiple_of(index * 16 * count, 16 * count), 16 * count)
+        acts = act_ref[rows, :].astype(F32)
+        for offset in range(count + 1):
+            if offset < count:
+                advance(count * index + offset, keeps[offset])
             if offset:
-                readout(len(keeps) * index + offset - 1, keeps[offset - 1])
-        readout(len(keeps) * index + len(keeps) - 1, keeps[-1])
+                last = offset - 1
+                readout(count * index + last, keeps[last], acts[last * 16 : last * 16 + 16])
         return carry
 
-    lax.fori_loop(0, REQS // 2 // len(keeps), some, 0)
+    lax.fori_loop(0, REQS // 4 // len(keeps), some, 0)
     for req in range(REQS):
         out_ref[req, :, HALF:BACK] = attended_ref[req]
 
@@ -521,27 +519,27 @@
         out_specs=vmem(),
         scratch_shapes=[
             pltpu.VMEM((REQS * STEPS, RANK + 2 * LANES), BF16),
-            pltpu.VMEM((REQS, ROWS, HALF), F32),
-            pltpu.VMEM((REQS, ROWS, HALF), F32),
+            pltpu.VMEM((REQS // 2, ROWS, 2 * HALF), F32),
+            pltpu.VMEM((REQS // 2, ROWS, 2 * HALF), F32),
             pltpu.VMEM((STATE, 2 * HALF), F32),
-            pltpu.VMEM((ROWS, HALF), F32),
             pltpu.VMEM((LANES, LANES), F32),
-            pltpu.VMEM((REQS // 2, 16, LANES), BF16),
+            pltpu.VMEM((REQS // 4, 32, 2 * LANES), BF16),
         ]
-        + [pltpu.VMEM((2 * STEPS * STATE, 2 * HALF), BF16)] * KEEPS,
+        + [pltpu.VMEM((4 * STEPS * STATE, 2 * HALF), BF16)] * KEEPS,
         compiler_params=params(16),
         name="scan",
     )(order, core, ours, theirs, act, attended, ssm_state, dt_proj, dt_bias, a_log, skip_d)
 
 
-def unpack_kernel(back_ref, z_ref, attn_ref, mamba_ref, rows):
-    for req in range(REQS):
-        for tile in range(BACK // LANES):
-            rows[tile, req * ROWS : (req + 1) * ROWS, :] = back_ref[
-                req, :, tile * LANES : (tile + 1) * LANES
-            ].astype(F32)
-    for step in range(STEPS):
-        for group in range(0, REQS, 16):
+def unpack_kernel(back_ref, z_ref, attn_hbm, mamba_hbm, rows, attn_ref, mamba_ref, sems):
+    outs = []
+    for group in range(0, REQS, 16):
+        for req in range(group, group + 16):
+            for tile in range(BACK // LANES):
+                rows[tile, req * ROWS : (req + 1) * ROWS, :] = back_ref[
+                    req, :, tile * LANES : (tile + 1) * LANES
+                ].astype(F32)
+        for step in range(STEPS):
             for half in range(2):
                 first = half * STEPS + step
                 places = [
@@ -559,18 +557,32 @@
                         first_column = half * QUARTER + tile * LANES - HALF
                         columns = slice(first_column, first_column + LANES)
                         attn_ref[step, group : group + 16, columns] = block.astype(BF16)
+        span = pl.ds(group, 16)
+        for index, (near, far) in enumerate(((attn_ref, attn_hbm), (mamba_ref, mamba_hbm))):
+            outs.append(
+                pltpu.make_async_copy(
+                    near.at[:, span], far.at[:, span], sems.at[index, group // 16]
+                )
+            )
+            outs[-1].start()
+    for copy in outs:
+        copy.wait()
 
 
 def unpack(back, mamba_z):
+    attn = (STEPS, REQS, 2 * QUARTER)
+    mamba = (STEPS, REQS, 2 * HALF)
     return pl.pallas_call(
         unpack_kernel,
-        out_shape=(
-            jax.ShapeDtypeStruct((STEPS, REQS, 2 * QUARTER), BF16),
-            jax.ShapeDtypeStruct((STEPS, REQS, 2 * HALF), BF16),
-        ),
+        out_shape=(jax.ShapeDtypeStruct(attn, BF16), jax.ShapeDtypeStruct(mamba, BF16)),
         in_specs=[vmem()] * 2,
-        out_specs=(vmem(), vmem()),
-        scratch_shapes=[pltpu.VMEM((BACK // LANES, REQS * ROWS, LANES), F32)],
+        out_specs=(anywhere(), anywhere()),
+        scratch_shapes=[
+            pltpu.VMEM((BACK // LANES, REQS * ROWS, LANES), F32),
+            pltpu.VMEM(attn, BF16),
+            pltpu.VMEM(mamba, BF16),
+            pltpu.SemaphoreType.DMA((2, 2)),
+        ],
         compiler_params=params(24),
         name="unpack",
     )(back, mamba_z)
@@ -609,14 +621,12 @@
         order, outgoing, jnp.transpose(conv_state, (1, 0, 2)), conv_weight, conv_bias[None]
     )
     act, mine, other = convolve(core, arrived, prior, x_proj)
-    unit = jnp.where(order[0] >= 0, 1, 2).astype(BF16)
-    pool = prefill_page_pool * unit
     chip_sum = mine + lax.ppermute(other, "tp", swap)
     small = chip_sum.astype(BF16)
     ring = [
-        lax.ppermute(small, "tp", [(j, (j + hop) % 8) for j in range(8)]) for hop in (2, 6, 4)
+        lax.ppermute(small, "tp", [(j, (j + hop) % 8) for j in range(8)]) for hop in (4, 2, 6)
     ]
-    attended = attend(order, page_table, prompt_len, arrived, pool)
+    attended = attend(order, page_table, prompt_len, arrived, prefill_page_pool)
     ours = normalise(chip_sum, ring, dt_gain[None], attended)
     theirs = lax.ppermute(ours, "tp", swap)
     returning = scan(

time: 93.4 us -> 92.7 us (level)
  Pallas kernels: 21.6 us -> 20 us
  other arithmetic: 1.93 us -> 0.65 us
  starting transfers between devices: 16.7 us -> 17.9 us
    mul x1 -> x0, other arithmetic: 1.8 us -> none  [per_device(): pool = prefill_page_pool * unit]
    ppermute x1, waiting for transfers between devices: 0.01 us -> 1.29 us  [per_device(): chip_sum = mine + lax.ppermute(other, 'tp', swap)]
    pallas_call x2, Pallas kernels: 5.59 us -> 4.35 us  [the longest x1 3.02 us: convolve(): pl.pallas_call(conv_kernel, out_shape=(jax.ShapeDtypeStruct((REQS * STEPS...]
    ppermute x3, starting transfers between devices: 5.3 us -> 6.52 us  [per_device(): lax.ppermute(small, 'tp', [(j, (j + hop) % 8) for j in range(8)])]
    ppermute x3, waiting for transfers between devices: 0.96 us -> 0.01 us  [per_device(): lax.ppermute(small, 'tp', [(j, (j + hop) % 8) for j in range(8)])]
    unnamed x32 -> x30, local copies, waits for them, and re-layouts: 3.26 us -> 3.99 us
  transfers between devices with their start and end apart: 6 -> 6, of which waited for: 3 -> 3; matrix products, arithmetic and copies ran while one was open for 5% -> 4% of each run, Pallas kernels for 6% -> 6%
where the time goes in v5:
time: 92.7 us; the launch traced here: 92.4 us
  blocking collectives  28.1 us (30%)
  waiting for transfers between devices  21 us (23%)
  Pallas kernels  20 us (22%)
  starting transfers between devices  17.9 us (19%)
  local copies, waits for them, and re-layouts  3.99 us (4%)
    all_to_all x1, blocking collectives, per_device(): lax.all_to_all(returning, 'req', split_axis=0, concat_axis=0, tiled=True)  28.1 us
    all_to_all x1, waiting for transfers between devices, per_device(): lax.all_to_all(outgoing, 'req', split_axis=0, concat_axis=0, tiled=True)  18.4 us
    all_to_all x1, starting transfers between devices, per_device(): lax.all_to_all(outgoing, 'req', split_axis=0, concat_axis=0, tiled=True)  11.2 us
    pallas_call x1, Pallas kernels, scan(): pl.pallas_call(scan_kernel, out_shape=jax.ShapeDtypeStruct((REQS, ROWS, B...  7.02 us
    ppermute x3, starting transfers between devices, per_device(): lax.ppermute(small, 'tp', [(j, (j + hop) % 8) for j in range(8)])  6.52 us
    unnamed x30, local copies, waits for them, and re-layouts  3.99 us
    pallas_call x1, Pallas kernels, convolve(): pl.pallas_call(conv_kernel, out_shape=(jax.ShapeDtypeStruct((REQS * STEPS...  3.02 us
    pallas_call x1, Pallas kernels, attend(): pl.pallas_call(attend_kernel, out_shape=jax.ShapeDtypeStruct((REQS, ROWS,...  2.97 us
  transfers between devices with their start and end apart: 6, of which 3 were waited for; matrix products, arithmetic and copies ran while one was open for 4% of the time, Pallas kernels for 6%

profile of v5, /device:TPU:32, one launch (start us, length us, event | category | flops | bytes accessed | tf_op | source)
XLA Modules:
  0.0 92.4 jit_solution(2300795002173634880)
XLA Ops:
  0.6 2.5 %pack.1.sent_ref = bf16[32,8,1664]{2,1,0:T(8,128)(2,1)} custom-call(bf16[4,32,2048]{2,1,0:T(8,128)(2,1)} %x_hbm.1, bf16[4,32,1024]{2,1,0:T(8,128)(2,1)} %q_hbm.1, bf16[4,32,2,128]{3,2,1,0:T(2,128)(2,1)} %kv_hbm.1), custom_call_target="tpu_custom_call" | custom-call | tf_op jit(solution)/shard_map/pack/pallas_call | solution.py:122
  3.2 11.2 %all-to-all-start = ((bf16[32,8,1664]{2,1,0:T(8,128)(2,1)}), bf16[32,8,1664]{2,1,0:T(8,128)(2,1)}, u32[]{:S(2)}, u32[]{:S(2)}) async-start(bf16[32,8,1664]{2,1,0:T(8,128)(2,1)} %pack.1.sent_ref), calls=%async_computation | async-start | bytes 1703936 | tf_op jit(solution)/shard_map/all_to_all | solution.py:619
  14.5 2.6 %copy.22.proj_hbm = bf16[2048,544]{1,0:T(8,128)(2,1)} copy(bf16[2048,544]{0,1:T(8,128)(2,1)S(1)} %copy-done.11) | data formatting | bytes 4456448 | tf_op args[12]
  17.0 0.6 select_reduce_fusion.order_ref
  17.7 3.0 %stage.1.prior_hbm = f32[36,8,1024]{2,1,0:T(8,128)} custom-call(s32[32]{0:T(128)} %select_reduce_fusion.order_ref, bf16[32,8,1664]{2,1,0:T(8,128)(2,1)} %pack.1.sent_ref, bf16[3,32,2048]{2,1,0:T(8,128)(2,1)} %bitcast.9, f32[4,2048]{1,0:T(4,128)} %weight_ref.1, f32[1,2048]{1,0:T(1,128)} %bitcast.10), custom_call_target="tpu_custom_call" | custom-call | tf_op jit(solution)/shard_map/stage/pallas_call | solution.py:180
  20.6 18.4 %all-to-all-done.rows_hbm.rows_ref = bf16[32,8,1664]{2,1,0:T(8,128)(2,1)} async-done(((bf16[32,8,1664]{2,1,0:T(8,128)(2,1)}), bf16[32,8,1664]{2,1,0:T(8,128)(2,1)}, u32[]{:S(2)}, u32[]{:S(2)}) %all-to-all-start) | async-done | bytes 852000 | tf_op jit(solution)/shard_map/all_to_all | solution.py:619
  39.0 1.3 %copy-done = f32[36,8,1024]{2,1,0:T(8,128)S(1)} copy-done((f32[36,8,1024]{2,1,0:T(8,128)S(1)}, f32[36,8,1024]{2,1,0:T(8,128)}, u32[]{:S(2)}) %copy-start) | copy-done | bytes 1179672
  40.3 3.0 %convolve.1 = (bf16[128,2048]{1,0:T(8,128)(2,1)S(1)}, f32[64,544]{1,0:T(8,128)S(1)}, f32[64,544]{1,0:T(8,128)S(1)}) custom-call(s32[1]{0:T(128)} %bitcast.core_ref, bf16[32,8,1664]{2,1,0:T(8,128)(2,1)} %all-to-all-done.rows_hbm.rows_ref, f32[36,8,1024]{2,1,0:T(8,128)S(1)} %copy-done, bf16[2048,544]{1,0:T(8,128)(2,1)} %copy.22.proj_hbm), custom_call_target="tpu_custom_call" | custom-call | tf_op jit(solution)/shard_map/convolve/pallas_call | solution.py:270
  43.3 0.1 collective-permute-start
  43.4 0.1 copy.23.table_ref
  43.5 1.3 %collective-permute-done = f32[64,544]{1,0:T(8,128)S(1)} collective-permute-done((f32[64,544]{1,0:T(8,128)S(1)}, f32[64,544]{1,0:T(8,128)S(1)}, u32[]{:S(2)}, u32[]{:S(2)}) %collective-permute-start) | collective-permute-done | bytes 139296 | tf_op jit(solution)/shard_map/ppermute | solution.py:624
  44.8 0.0 copy-start.7
  44.8 0.0 copy-start.2
  44.9 0.0 copy-start.5
  44.9 3.3 %collective-permute-start.1 = (bf16[64,544]{1,0:T(8,128)(2,1)S(1)}, bf16[64,544]{1,0:T(8,128)(2,1)S(1)}, u32[]{:S(2)}, u32[]{:S(2)}) collective-permute-start(bf16[64,544]{1,0:T(8,128)(2,1)S(1)} %get-tuple-element.8), channel_id=1, source_target_pairs={{0,4},{1,5},{2,6},{3,7},{4,0},{5,1},{6,2},{7,3},{8,12},{9,13},{10,... | collective-permute-start | bytes 208904 | tf_op jit(solution)/shard_map/ppermute | solution.py:627
  48.2 0.7 collective-permute-start.2
  48.8 2.6 %collective-permute-start.3 = (bf16[64,544]{1,0:T(8,128)(2,1)S(1)}, bf16[64,544]{1,0:T(8,128)(2,1)S(1)}, u32[]{:S(2)}, u32[]{:S(2)}) collective-permute-start(bf16[64,544]{1,0:T(8,128)(2,1)S(1)} %get-tuple-element.8), channel_id=1, source_target_pairs={{0,6},{1,7},{2,0},{3,1},{4,2},{5,3},{6,4},{7,5},{8,14},{9,15},{10,... | collective-permute-start | bytes 208904 | tf_op jit(solution)/shard_map/ppermute | solution.py:627
  51.4 3.0 %attend.1.after_ref.attended_ref = bf16[32,8,512]{2,1,0:T(8,128)(2,1)S(1)} custom-call(s32[32]{0:T(128)S(1)} %copy-done.8, s32[32,8]{1,0:T(8,128)S(1)} %copy.23.table_ref, s32[32]{0:T(128)S(1)} %copy-done.10, bf16[32,8,1664]{2,1,0:T(8,128)(2,1)} %all-to-all-done.rows_hbm.rows_ref, bf16[256,2,16,128]{3,2,1,0:T(8,128)(2,1)S(1)} %copy-done.9), custom_call_target="tpu_custom_call" | custom-call | flops 3500000000 | bytes 6000000 | tf_op jit(solution)/shard_map/attend/pallas_call | solution.py:379
  54.4 0.1 normalise.1.ours_ref
  54.6 0.1 collective-permute-start.4
  54.7 1.3 %collective-permute-done.4.theirs_ref = bf16[64,768]{1,0:T(8,128)(2,1)S(1)} collective-permute-done((bf16[64,768]{1,0:T(8,128)(2,1)S(1)}, bf16[64,768]{1,0:T(8,128)(2,1)S(1)}, u32[]{:S(2)}, u32[]{:S(2)}) %collective-permute-start.4) | collective-permute-done | bytes 98336 | tf_op jit(solution)/shard_map/ppermute | solution.py:631
  56.0 7.0 %scan.1 = bf16[32,8,1536]{2,1,0:T(8,128)(2,1)S(1)} custom-call(s32[32]{0:T(128)S(1)} %copy-done.8, s32[1]{0:T(128)} %bitcast.core_ref, bf16[64,768]{1,0:T(8,128)(2,1)S(1)} %normalise.1.ours_ref, bf16[64,768]{1,0:T(8,128)(2,1)S(1)} %collective-permute-done.4.theirs_ref, bf16[128,2048]{1,0:T(8,128)(2,1)S(1)} %get-tuple-element.7.act_ref, ...), custom_call_target="tpu_custom_call" | custom-call | tf_op jit(solution)/shard_map/scan/pallas_call | solution.py:515
  63.0 28.1 %all_to_all.10.back_ref = bf16[32,8,1536]{2,1,0:T(8,128)(2,1)S(1)} all-to-all(bf16[32,8,1536]{2,1,0:T(8,128)(2,1)S(1)} %scan.1), channel_id=1, replica_groups=mesh['req'=32,'tp'=8] {'req'}, dimensions={0} | all-to-all | bytes 1572864 | tf_op jit(solution)/shard_map/all_to_all | solution.py:645
  91.1 1.3 %unpack.1 = (bf16[4,32,1024]{2,1,0:T(8,128)(2,1)}, bf16[4,32,2048]{2,1,0:T(8,128)(2,1)}) custom-call(bf16[32,8,1536]{2,1,0:T(8,128)(2,1)S(1)} %all_to_all.10.back_ref, bf16[4,32,2048]{2,1,0:T(8,128)(2,1)S(1)} %copy-done.3), custom_call_target="tpu_custom_call" | custom-call | tf_op jit(solution)/shard_map/unpack/pallas_call | solution.py:575
  (28 shorter events, 0.1 us)
Async XLA Ops:
  0.6 13.8 %copy-start.11 = (bf16[2048,544]{0,1:T(8,128)(2,1)S(1)}, bf16[2048,544]{0,1:T(8,128)(2,1)}, u32[]{:S(2)}) copy-start(bf16[2048,544]{0,1:T(8,128)(2,1)} %param.30) | copy-start | bytes 6684676
  3.2 35.8 %all-to-all-start = ((bf16[32,8,1664]{2,1,0:T(8,128)(2,1)}), bf16[32,8,1664]{2,1,0:T(8,128)(2,1)}, u32[]{:S(2)}, u32[]{:S(2)}) async-start(bf16[32,8,1664]{2,1,0:T(8,128)(2,1)} %pack.1.sent_ref), calls=%async_computation | async-start | bytes 1703936 | tf_op jit(solution)/shard_map/all_to_all | solution.py:619
  14.5 2.6 %copy-start.13 = (s32[32]{0:T(128)S(1)}, s32[32]{0:T(128)}, u32[]{:S(2)}) copy-start(s32[32]{0:T(128)} %param.23) | copy-start | bytes 388
  39.0 1.3 %copy-start = (f32[36,8,1024]{2,1,0:T(8,128)S(1)}, f32[36,8,1024]{2,1,0:T(8,128)}, u32[]{:S(2)}) copy-start(f32[36,8,1024]{2,1,0:T(8,128)} %stage.1.prior_hbm) | copy-start | bytes 3538948
  40.3 3.1 %copy-start.12 = (s32[32,8]{0,1:T(8,128)S(1)}, s32[32,8]{0,1:T(8,128)}, u32[]{:S(2)}) copy-start(s32[32,8]{0,1:T(8,128)} %param.21) | copy-start | bytes 3076
  40.3 11.1 %copy-start.8 = (s32[32]{0:T(128)S(1)}, s32[32]{0:T(128)}, u32[]{:S(2)}) copy-start(s32[32]{0:T(128)} %select_reduce_fusion.order_ref) | copy-start | bytes 388
  40.3 11.1 %copy-start.9 = (bf16[256,2,16,128]{3,2,1,0:T(8,128)(2,1)S(1)}, bf16[256,2,16,128]{3,2,1,0:T(8,128)(2,1)}, u32[]{:S(2)}) copy-start(bf16[256,2,16,128]{3,2,1,0:T(8,128)(2,1)} %pool_ref.1) | copy-start | bytes 6291460
  40.3 11.1 %copy-start.10 = (s32[32]{0:T(128)S(1)}, s32[32]{0:T(128)}, u32[]{:S(2)}) copy-start(s32[32]{0:T(128)} %length_ref.1) | copy-start | bytes 388
  43.3 1.5 %collective-permute-start = (f32[64,544]{1,0:T(8,128)S(1)}, f32[64,544]{1,0:T(8,128)S(1)}, u32[]{:S(2)}, u32[]{:S(2)}) collective-permute-start(f32[64,544]{1,0:T(8,128)S(1)} %get-tuple-element.6), channel_id=1, source_target_pairs={{0,1},{1,0},{2,3},{3,2},{4,5},{5,4},{6,7},{7,6},{8,9},{9,8},{10,11... | collective-permute-start | bytes 417800 | tf_op jit(solution)/shard_map/ppermute | solution.py:624
  44.8 9.6 %copy-start.7 = (f32[512]{0:T(512)S(1)}, f32[512]{0:T(512)}, u32[]{:S(2)}) copy-start(f32[512]{0:T(512)} %param.31) | copy-start | bytes 6148
  44.8 11.1 %copy-start.2 = (bf16[512,2048]{1,0:T(8,128)(2,1)S(1)}, bf16[512,2048]{1,0:T(8,128)(2,1)}, u32[]{:S(2)}) copy-start(bf16[512,2048]{1,0:T(8,128)(2,1)} %dt_proj_ref.1) | copy-start | bytes 6291460
  44.8 11.1 %copy-start.4 = (f32[16,2048]{1,0:T(8,128)S(1)}, f32[16,2048]{1,0:T(8,128)}, u32[]{:S(2)}) copy-start(f32[16,2048]{1,0:T(8,128)} %a_log_ref.1) | copy-start | bytes 393220
  44.9 11.1 %copy-start.5 = (f32[2048]{0:T(1024)S(1)}, f32[2048]{0:T(1024)}, u32[]{:S(2)}) copy-start(f32[2048]{0:T(1024)} %param.33) | copy-start | bytes 24580
  44.9 11.1 %copy-start.6 = (f32[2048]{0:T(1024)S(1)}, f32[2048]{0:T(1024)}, u32[]{:S(2)}) copy-start(f32[2048]{0:T(1024)} %param.35) | copy-start | bytes 24580
  44.9 9.5 %collective-permute-start.1 = (bf16[64,544]{1,0:T(8,128)(2,1)S(1)}, bf16[64,544]{1,0:T(8,128)(2,1)S(1)}, u32[]{:S(2)}, u32[]{:S(2)}) collective-permute-start(bf16[64,544]{1,0:T(8,128)(2,1)S(1)} %get-tuple-element.8), channel_id=1, source_target_pairs={{0,4},{1,5},{2,6},{3,7},{4,0},{5,1},{6,2},{7,3},{8,12},{9,13},{10,... | collective-permute-start | bytes 208904 | tf_op jit(solution)/shard_map/ppermute | solution.py:627
  48.2 6.2 %collective-permute-start.2 = (bf16[64,544]{1,0:T(8,128)(2,1)S(1)}, bf16[64,544]{1,0:T(8,128)(2,1)S(1)}, u32[]{:S(2)}, u32[]{:S(2)}) collective-permute-start(bf16[64,544]{1,0:T(8,128)(2,1)S(1)} %get-tuple-element.8), channel_id=1, source_target_pairs={{0,2},{1,3},{2,4},{3,5},{4,6},{5,7},{6,0},{7,1},{8,10},{9,11},{10,... | collective-permute-start | bytes 208904 | tf_op jit(solution)/shard_map/ppermute | solution.py:627
  48.8 5.6 %collective-permute-start.3 = (bf16[64,544]{1,0:T(8,128)(2,1)S(1)}, bf16[64,544]{1,0:T(8,128)(2,1)S(1)}, u32[]{:S(2)}, u32[]{:S(2)}) collective-permute-start(bf16[64,544]{1,0:T(8,128)(2,1)S(1)} %get-tuple-element.8), channel_id=1, source_target_pairs={{0,6},{1,7},{2,0},{3,1},{4,2},{5,3},{6,4},{7,5},{8,14},{9,15},{10,... | collective-permute-start | bytes 208904 | tf_op jit(solution)/shard_map/ppermute | solution.py:627
  51.4 4.6 %copy-start.1 = (f32[32,16,2048]{2,1,0:T(8,128)S(1)}, f32[32,16,2048]{2,1,0:T(8,128)}, u32[]{:S(2)}) copy-start(f32[32,16,2048]{2,1,0:T(8,128)} %state_ref.1) | copy-start | bytes 12582916
  54.6 1.4 %collective-permute-start.4 = (bf16[64,768]{1,0:T(8,128)(2,1)S(1)}, bf16[64,768]{1,0:T(8,128)(2,1)S(1)}, u32[]{:S(2)}, u32[]{:S(2)}) collective-permute-start(bf16[64,768]{1,0:T(8,128)(2,1)S(1)} %normalise.1.ours_ref), channel_id=1, source_target_pairs={{0,1},{1,0},{2,3},{3,2},{4,5},{5,4},{6,7},{7,6},{8,9},{9,8},{10,11... | collective-permute-start | bytes 294920 | tf_op jit(solution)/shard_map/ppermute | solution.py:631
  56.0 35.1 %copy-start.3 = (bf16[4,32,2048]{2,1,0:T(8,128)(2,1)S(1)}, bf16[4,32,2048]{2,1,0:T(8,128)(2,1)}, u32[]{:S(2)}) copy-start(bf16[4,32,2048]{2,1,0:T(8,128)(2,1)} %z_ref.1) | copy-start | bytes 1572868

commit v6 on v5

--- a/solution.py
+++ b/solution.py
@@ -283,7 +283,7 @@
             pltpu.SemaphoreType.DMA,
             pltpu.SemaphoreType.DMA,
         ],
-        compiler_params=params(50),
+        compiler_params=params(52),
         name="convolve",
     )(core, arrived, prior, x_proj)
 

time: 92.7 us -> 91.6 us (0.988)
  local copies, waits for them, and re-layouts: 3.99 us -> 2.73 us
    unnamed x30 -> x28, local copies, waits for them, and re-layouts: 3.99 us -> 2.73 us
where the time goes in v6:
time: 91.6 us; the launch traced here: 91.3 us
  blocking collectives  28.1 us (31%)
  waiting for transfers between devices  21 us (23%)
  Pallas kernels  20.1 us (22%)
  starting transfers between devices  17.9 us (20%)
  local copies, waits for them, and re-layouts  2.73 us (3%)
    all_to_all x1, blocking collectives, per_device(): lax.all_to_all(returning, 'req', split_axis=0, concat_axis=0, tiled=True)  28.1 us
    all_to_all x1, waiting for transfers between devices, per_device(): lax.all_to_all(outgoing, 'req', split_axis=0, concat_axis=0, tiled=True)  18.4 us
    all_to_all x1, starting transfers between devices, per_device(): lax.all_to_all(outgoing, 'req', split_axis=0, concat_axis=0, tiled=True)  11.2 us
    pallas_call x1, Pallas kernels, scan(): pl.pallas_call(scan_kernel, out_shape=jax.ShapeDtypeStruct((REQS, ROWS, B...  7.02 us
    ppermute x3, starting transfers between devices, per_device(): lax.ppermute(small, 'tp', [(j, (j + hop) % 8) for j in range(8)])  6.51 us
    pallas_call x1, Pallas kernels, convolve(): pl.pallas_call(conv_kernel, out_shape=(jax.ShapeDtypeStruct((REQS * STEPS...  3.17 us
    pallas_call x1, Pallas kernels, attend(): pl.pallas_call(attend_kernel, out_shape=jax.ShapeDtypeStruct((REQS, ROWS,...  2.96 us
    pallas_call x1, Pallas kernels, stage(): pl.pallas_call(stage_kernel, out_shape=jax.ShapeDtypeStruct((REQS + 4, RO...  2.96 us
  transfers between devices with their start and end apart: 6, of which 3 were waited for; matrix products, arithmetic and copies ran while one was open for 4% of the time, Pallas kernels for 6%

profile of v6, /device:TPU:32, one launch (start us, length us, event | category | flops | bytes accessed | tf_op | source)
XLA Modules:
  0.0 91.3 jit_solution(16336707713092702880)
XLA Ops:
  0.6 2.5 %pack.1.sent_ref = bf16[32,8,1664]{2,1,0:T(8,128)(2,1)} custom-call(bf16[4,32,2048]{2,1,0:T(8,128)(2,1)} %x_hbm.1, bf16[4,32,1024]{2,1,0:T(8,128)(2,1)} %q_hbm.1, bf16[4,32,2,128]{3,2,1,0:T(2,128)(2,1)} %kv_hbm.1), custom_call_target="tpu_custom_call" | custom-call | tf_op jit(solution)/shard_map/pack/pallas_call | solution.py:122
  3.2 11.2 %all-to-all-start = ((bf16[32,8,1664]{2,1,0:T(8,128)(2,1)}), bf16[32,8,1664]{2,1,0:T(8,128)(2,1)}, u32[]{:S(2)}, u32[]{:S(2)}) async-start(bf16[32,8,1664]{2,1,0:T(8,128)(2,1)} %pack.1.sent_ref), calls=%async_computation | async-start | bytes 1703936 | tf_op jit(solution)/shard_map/all_to_all | solution.py:619
  14.5 0.0 copy-start.12
  14.5 2.6 %copy.22.proj_hbm = bf16[2048,544]{1,0:T(8,128)(2,1)} copy(bf16[2048,544]{0,1:T(8,128)(2,1)S(1)} %copy-done.10) | data formatting | bytes 4456448 | tf_op args[12]
  17.1 0.6 select_reduce_fusion.order_ref
  17.7 3.0 %stage.1.prior_hbm = f32[36,8,1024]{2,1,0:T(8,128)} custom-call(s32[32]{0:T(128)} %select_reduce_fusion.order_ref, bf16[32,8,1664]{2,1,0:T(8,128)(2,1)} %pack.1.sent_ref, bf16[3,32,2048]{2,1,0:T(8,128)(2,1)} %bitcast.9, f32[4,2048]{1,0:T(4,128)} %weight_ref.1, f32[1,2048]{1,0:T(1,128)} %bitcast.10), custom_call_target="tpu_custom_call" | custom-call | tf_op jit(solution)/shard_map/stage/pallas_call | solution.py:180
  20.6 18.4 %all-to-all-done.rows_hbm.rows_ref = bf16[32,8,1664]{2,1,0:T(8,128)(2,1)} async-done(((bf16[32,8,1664]{2,1,0:T(8,128)(2,1)}), bf16[32,8,1664]{2,1,0:T(8,128)(2,1)}, u32[]{:S(2)}, u32[]{:S(2)}) %all-to-all-start) | async-done | bytes 852000 | tf_op jit(solution)/shard_map/all_to_all | solution.py:619
  39.0 3.2 %convolve.1 = (bf16[128,2048]{1,0:T(8,128)(2,1)S(1)}, f32[64,544]{1,0:T(8,128)S(1)}, f32[64,544]{1,0:T(8,128)S(1)}) custom-call(s32[1]{0:T(128)} %bitcast.core_ref, bf16[32,8,1664]{2,1,0:T(8,128)(2,1)} %all-to-all-done.rows_hbm.rows_ref, f32[36,8,1024]{2,1,0:T(8,128)} %stage.1.prior_hbm, bf16[2048,544]{1,0:T(8,128)(2,1)} %copy.22.proj_hbm), custom_call_target="tpu_custom_call" | custom-call | tf_op jit(solution)/shard_map/convolve/pallas_call | solution.py:270
  42.2 0.1 collective-permute-start
  42.3 0.1 copy.23.table_ref
  42.4 1.3 %collective-permute-done = f32[64,544]{1,0:T(8,128)S(1)} collective-permute-done((f32[64,544]{1,0:T(8,128)S(1)}, f32[64,544]{1,0:T(8,128)S(1)}, u32[]{:S(2)}, u32[]{:S(2)}) %collective-permute-start) | collective-permute-done | bytes 139296 | tf_op jit(solution)/shard_map/ppermute | solution.py:624
  43.7 0.0 copy-start.6
  43.7 0.0 copy-start.1
  43.8 0.0 copy-start.5
  43.8 3.3 %collective-permute-start.1 = (bf16[64,544]{1,0:T(8,128)(2,1)S(1)}, bf16[64,544]{1,0:T(8,128)(2,1)S(1)}, u32[]{:S(2)}, u32[]{:S(2)}) collective-permute-start(bf16[64,544]{1,0:T(8,128)(2,1)S(1)} %get-tuple-element.8), channel_id=1, source_target_pairs={{0,4},{1,5},{2,6},{3,7},{4,0},{5,1},{6,2},{7,3},{8,12},{9,13},{10,... | collective-permute-start | bytes 208904 | tf_op jit(solution)/shard_map/ppermute | solution.py:627
  47.0 0.7 collective-permute-start.2
  47.7 2.6 %collective-permute-start.3 = (bf16[64,544]{1,0:T(8,128)(2,1)S(1)}, bf16[64,544]{1,0:T(8,128)(2,1)S(1)}, u32[]{:S(2)}, u32[]{:S(2)}) collective-permute-start(bf16[64,544]{1,0:T(8,128)(2,1)S(1)} %get-tuple-element.8), channel_id=1, source_target_pairs={{0,6},{1,7},{2,0},{3,1},{4,2},{5,3},{6,4},{7,5},{8,14},{9,15},{10,... | collective-permute-start | bytes 208904 | tf_op jit(solution)/shard_map/ppermute | solution.py:627
  50.3 3.0 %attend.1.after_ref.attended_ref = bf16[32,8,512]{2,1,0:T(8,128)(2,1)S(1)} custom-call(s32[32]{0:T(128)S(1)} %copy-done.7, s32[32,8]{1,0:T(8,128)S(1)} %copy.23.table_ref, s32[32]{0:T(128)S(1)} %copy-done.9, bf16[32,8,1664]{2,1,0:T(8,128)(2,1)} %all-to-all-done.rows_hbm.rows_ref, bf16[256,2,16,128]{3,2,1,0:T(8,128)(2,1)S(1)} %copy-done.8), custom_call_target="tpu_custom_call" | custom-call | flops 3500000000 | bytes 6000000 | tf_op jit(solution)/shard_map/attend/pallas_call | solution.py:379
  53.3 0.1 normalise.1.ours_ref
  53.4 0.1 collective-permute-start.4
  53.5 1.3 %collective-permute-done.4.theirs_ref = bf16[64,768]{1,0:T(8,128)(2,1)S(1)} collective-permute-done((bf16[64,768]{1,0:T(8,128)(2,1)S(1)}, bf16[64,768]{1,0:T(8,128)(2,1)S(1)}, u32[]{:S(2)}, u32[]{:S(2)}) %collective-permute-start.4) | collective-permute-done | bytes 98336 | tf_op jit(solution)/shard_map/ppermute | solution.py:631
  54.9 7.0 %scan.1 = bf16[32,8,1536]{2,1,0:T(8,128)(2,1)S(1)} custom-call(s32[32]{0:T(128)S(1)} %copy-done.7, s32[1]{0:T(128)} %bitcast.core_ref, bf16[64,768]{1,0:T(8,128)(2,1)S(1)} %normalise.1.ours_ref, bf16[64,768]{1,0:T(8,128)(2,1)S(1)} %collective-permute-done.4.theirs_ref, bf16[128,2048]{1,0:T(8,128)(2,1)S(1)} %get-tuple-element.7.act_ref, ...), custom_call_target="tpu_custom_call" | custom-call | tf_op jit(solution)/shard_map/scan/pallas_call | solution.py:515
  61.9 28.1 %all_to_all.10.back_ref = bf16[32,8,1536]{2,1,0:T(8,128)(2,1)S(1)} all-to-all(bf16[32,8,1536]{2,1,0:T(8,128)(2,1)S(1)} %scan.1), channel_id=1, replica_groups=mesh['req'=32,'tp'=8] {'req'}, dimensions={0} | all-to-all | bytes 1572864 | tf_op jit(solution)/shard_map/all_to_all | solution.py:645
  90.0 1.3 %unpack.1 = (bf16[4,32,1024]{2,1,0:T(8,128)(2,1)}, bf16[4,32,2048]{2,1,0:T(8,128)(2,1)}) custom-call(bf16[32,8,1536]{2,1,0:T(8,128)(2,1)S(1)} %all_to_all.10.back_ref, bf16[4,32,2048]{2,1,0:T(8,128)(2,1)S(1)} %copy-done.2), custom_call_target="tpu_custom_call" | custom-call | tf_op jit(solution)/shard_map/unpack/pallas_call | solution.py:575
  (26 shorter events, 0.1 us)
Async XLA Ops:
  0.6 13.8 %copy-start.10 = (bf16[2048,544]{0,1:T(8,128)(2,1)S(1)}, bf16[2048,544]{0,1:T(8,128)(2,1)}, u32[]{:S(2)}) copy-start(bf16[2048,544]{0,1:T(8,128)(2,1)} %param.30) | copy-start | bytes 6684676
  3.2 35.8 %all-to-all-start = ((bf16[32,8,1664]{2,1,0:T(8,128)(2,1)}), bf16[32,8,1664]{2,1,0:T(8,128)(2,1)}, u32[]{:S(2)}, u32[]{:S(2)}) async-start(bf16[32,8,1664]{2,1,0:T(8,128)(2,1)} %pack.1.sent_ref), calls=%async_computation | async-start | bytes 1703936 | tf_op jit(solution)/shard_map/all_to_all | solution.py:619
  14.5 2.6 %copy-start.12 = (s32[32]{0:T(128)S(1)}, s32[32]{0:T(128)}, u32[]{:S(2)}) copy-start(s32[32]{0:T(128)} %param.23) | copy-start | bytes 388
  39.0 3.3 %copy-start.11 = (s32[32,8]{0,1:T(8,128)S(1)}, s32[32,8]{0,1:T(8,128)}, u32[]{:S(2)}) copy-start(s32[32,8]{0,1:T(8,128)} %param.21) | copy-start | bytes 3076
  39.0 11.3 %copy-start.7 = (s32[32]{0:T(128)S(1)}, s32[32]{0:T(128)}, u32[]{:S(2)}) copy-start(s32[32]{0:T(128)} %select_reduce_fusion.order_ref) | copy-start | bytes 388
  39.0 11.3 %copy-start.8 = (bf16[256,2,16,128]{3,2,1,0:T(8,128)(2,1)S(1)}, bf16[256,2,16,128]{3,2,1,0:T(8,128)(2,1)}, u32[]{:S(2)}) copy-start(bf16[256,2,16,128]{3,2,1,0:T(8,128)(2,1)} %pool_ref.1) | copy-start | bytes 6291460
  39.0 11.3 %copy-start.9 = (s32[32]{0:T(128)S(1)}, s32[32]{0:T(128)}, u32[]{:S(2)}) copy-start(s32[32]{0:T(128)} %length_ref.1) | copy-start | bytes 388
  42.2 1.5 %collective-permute-start = (f32[64,544]{1,0:T(8,128)S(1)}, f32[64,544]{1,0:T(8,128)S(1)}, u32[]{:S(2)}, u32[]{:S(2)}) collective-permute-start(f32[64,544]{1,0:T(8,128)S(1)} %get-tuple-element.6), channel_id=1, source_target_pairs={{0,1},{1,0},{2,3},{3,2},{4,5},{5,4},{6,7},{7,6},{8,9},{9,8},{10,11... | collective-permute-start | bytes 417800 | tf_op jit(solution)/shard_map/ppermute | solution.py:624
  43.7 9.6 %copy-start.6 = (f32[512]{0:T(512)S(1)}, f32[512]{0:T(512)}, u32[]{:S(2)}) copy-start(f32[512]{0:T(512)} %param.31) | copy-start | bytes 6148
  43.7 11.1 %copy-start.1 = (bf16[512,2048]{1,0:T(8,128)(2,1)S(1)}, bf16[512,2048]{1,0:T(8,128)(2,1)}, u32[]{:S(2)}) copy-start(bf16[512,2048]{1,0:T(8,128)(2,1)} %dt_proj_ref.1) | copy-start | bytes 6291460
  43.7 11.1 %copy-start.3 = (f32[16,2048]{1,0:T(8,128)S(1)}, f32[16,2048]{1,0:T(8,128)}, u32[]{:S(2)}) copy-start(f32[16,2048]{1,0:T(8,128)} %a_log_ref.1) | copy-start | bytes 393220
  43.7 11.1 %copy-start.4 = (f32[2048]{0:T(1024)S(1)}, f32[2048]{0:T(1024)}, u32[]{:S(2)}) copy-start(f32[2048]{0:T(1024)} %param.33) | copy-start | bytes 24580
  43.8 11.1 %copy-start.5 = (f32[2048]{0:T(1024)S(1)}, f32[2048]{0:T(1024)}, u32[]{:S(2)}) copy-start(f32[2048]{0:T(1024)} %param.35) | copy-start | bytes 24580
  43.8 9.5 %collective-permute-start.1 = (bf16[64,544]{1,0:T(8,128)(2,1)S(1)}, bf16[64,544]{1,0:T(8,128)(2,1)S(1)}, u32[]{:S(2)}, u32[]{:S(2)}) collective-permute-start(bf16[64,544]{1,0:T(8,128)(2,1)S(1)} %get-tuple-element.8), channel_id=1, source_target_pairs={{0,4},{1,5},{2,6},{3,7},{4,0},{5,1},{6,2},{7,3},{8,12},{9,13},{10,... | collective-permute-start | bytes 208904 | tf_op jit(solution)/shard_map/ppermute | solution.py:627
  47.0 6.2 %collective-permute-start.2 = (bf16[64,544]{1,0:T(8,128)(2,1)S(1)}, bf16[64,544]{1,0:T(8,128)(2,1)S(1)}, u32[]{:S(2)}, u32[]{:S(2)}) collective-permute-start(bf16[64,544]{1,0:T(8,128)(2,1)S(1)} %get-tuple-element.8), channel_id=1, source_target_pairs={{0,2},{1,3},{2,4},{3,5},{4,6},{5,7},{6,0},{7,1},{8,10},{9,11},{10,... | collective-permute-start | bytes 208904 | tf_op jit(solution)/shard_map/ppermute | solution.py:627
  47.7 5.6 %collective-permute-start.3 = (bf16[64,544]{1,0:T(8,128)(2,1)S(1)}, bf16[64,544]{1,0:T(8,128)(2,1)S(1)}, u32[]{:S(2)}, u32[]{:S(2)}) collective-permute-start(bf16[64,544]{1,0:T(8,128)(2,1)S(1)} %get-tuple-element.8), channel_id=1, source_target_pairs={{0,6},{1,7},{2,0},{3,1},{4,2},{5,3},{6,4},{7,5},{8,14},{9,15},{10,... | collective-permute-start | bytes 208904 | tf_op jit(solution)/shard_map/ppermute | solution.py:627
  50.3 4.6 %copy-start = (f32[32,16,2048]{2,1,0:T(8,128)S(1)}, f32[32,16,2048]{2,1,0:T(8,128)}, u32[]{:S(2)}) copy-start(f32[32,16,2048]{2,1,0:T(8,128)} %state_ref.1) | copy-start | bytes 12582916
  53.4 1.4 %collective-permute-start.4 = (bf16[64,768]{1,0:T(8,128)(2,1)S(1)}, bf16[64,768]{1,0:T(8,128)(2,1)S(1)}, u32[]{:S(2)}, u32[]{:S(2)}) collective-permute-start(bf16[64,768]{1,0:T(8,128)(2,1)S(1)} %normalise.1.ours_ref), channel_id=1, source_target_pairs={{0,1},{1,0},{2,3},{3,2},{4,5},{5,4},{6,7},{7,6},{8,9},{9,8},{10,11... | collective-permute-start | bytes 294920 | tf_op jit(solution)/shard_map/ppermute | solution.py:631
  54.9 35.1 %copy-start.2 = (bf16[4,32,2048]{2,1,0:T(8,128)(2,1)S(1)}, bf16[4,32,2048]{2,1,0:T(8,128)(2,1)}, u32[]{:S(2)}) copy-start(bf16[4,32,2048]{2,1,0:T(8,128)(2,1)} %z_ref.1) | copy-start | bytes 1572868

commit v7 on v6

--- a/solution.py
+++ b/solution.py
@@ -21,7 +21,7 @@
 WHOLE = 63
 BIG = 60
 UNROLL = 32
-KEEPS = 4
+KEEPS = 8
 CHUNKS = 4
 PAGE_TOKENS = 16
 PROJ = RANK + 2 * STATE
@@ -526,7 +526,7 @@
             pltpu.VMEM((REQS // 4, 32, 2 * LANES), BF16),
         ]
         + [pltpu.VMEM((4 * STEPS * STATE, 2 * HALF), BF16)] * KEEPS,
-        compiler_params=params(16),
+        compiler_params=params(40),
         name="scan",
     )(order, core, ours, theirs, act, attended, ssm_state, dt_proj, dt_bias, a_log, skip_d)
 

time: 91.6 us -> 92.4 us (level)
  no operation moved by 1% of the time
where the time goes in v7:
time: 92.4 us; the launch traced here: 92.1 us
  blocking collectives  28.1 us (30%)
  waiting for transfers between devices  21 us (23%)
  Pallas kernels  20.6 us (22%)
  starting transfers between devices  18.1 us (20%)
  local copies, waits for them, and re-layouts  2.73 us (3%)
  between operations  1.01 us (1%)
    all_to_all x1, blocking collectives, per_device(): lax.all_to_all(returning, 'req', split_axis=0, concat_axis=0, tiled=True)  28.1 us
    all_to_all x1, waiting for transfers between devices, per_device(): lax.all_to_all(outgoing, 'req', split_axis=0, concat_axis=0, tiled=True)  18.4 us
    all_to_all x1, starting transfers between devices, per_device(): lax.all_to_all(outgoing, 'req', split_axis=0, concat_axis=0, tiled=True)  11.2 us
    pallas_call x1, Pallas kernels, scan(): pl.pallas_call(scan_kernel, out_shape=jax.ShapeDtypeStruct((REQS, ROWS, B...  7.46 us
    ppermute x3, starting transfers between devices, per_device(): lax.ppermute(small, 'tp', [(j, (j + hop) % 8) for j in range(8)])  6.52 us
    pallas_call x1, Pallas kernels, convolve(): pl.pallas_call(conv_kernel, out_shape=(jax.ShapeDtypeStruct((REQS * STEPS...  3.16 us
    pallas_call x1, Pallas kernels, stage(): pl.pallas_call(stage_kernel, out_shape=jax.ShapeDtypeStruct((REQS + 4, RO...  2.96 us
    pallas_call x1, Pallas kernels, attend(): pl.pallas_call(attend_kernel, out_shape=jax.ShapeDtypeStruct((REQS, ROWS,...  2.96 us
  transfers between devices with their start and end apart: 6, of which 3 were waited for; matrix products, arithmetic and copies ran while one was open for 4% of the time, Pallas kernels for 6%

profile of v7, /device:TPU:32, one launch (start us, length us, event | category | flops | bytes accessed | tf_op | source)
XLA Modules:
  0.0 92.1 jit_solution(2327522447050021657)
XLA Ops:
  0.6 2.5 %pack.1.sent_ref = bf16[32,8,1664]{2,1,0:T(8,128)(2,1)} custom-call(bf16[4,32,2048]{2,1,0:T(8,128)(2,1)} %x_hbm.1, bf16[4,32,1024]{2,1,0:T(8,128)(2,1)} %q_hbm.1, bf16[4,32,2,128]{3,2,1,0:T(2,128)(2,1)} %kv_hbm.1), custom_call_target="tpu_custom_call" | custom-call | tf_op jit(solution)/shard_map/pack/pallas_call | solution.py:122
  3.2 11.2 %all-to-all-start = ((bf16[32,8,1664]{2,1,0:T(8,128)(2,1)}), bf16[32,8,1664]{2,1,0:T(8,128)(2,1)}, u32[]{:S(2)}, u32[]{:S(2)}) async-start(bf16[32,8,1664]{2,1,0:T(8,128)(2,1)} %pack.1.sent_ref), calls=%async_computation | async-start | bytes 1703936 | tf_op jit(solution)/shard_map/all_to_all | solution.py:619
  14.5 0.0 copy-start.12
  14.5 2.6 %copy.22.proj_hbm = bf16[2048,544]{1,0:T(8,128)(2,1)} copy(bf16[2048,544]{0,1:T(8,128)(2,1)S(1)} %copy-done.10) | data formatting | bytes 4456448 | tf_op args[12]
  17.1 0.6 select_reduce_fusion.order_ref
  17.7 3.0 %stage.1.prior_hbm = f32[36,8,1024]{2,1,0:T(8,128)} custom-call(s32[32]{0:T(128)} %select_reduce_fusion.order_ref, bf16[32,8,1664]{2,1,0:T(8,128)(2,1)} %pack.1.sent_ref, bf16[3,32,2048]{2,1,0:T(8,128)(2,1)} %bitcast.9, f32[4,2048]{1,0:T(4,128)} %weight_ref.1, f32[1,2048]{1,0:T(1,128)} %bitcast.10), custom_call_target="tpu_custom_call" | custom-call | tf_op jit(solution)/shard_map/stage/pallas_call | solution.py:180
  20.6 18.4 %all-to-all-done.rows_hbm.rows_ref = bf16[32,8,1664]{2,1,0:T(8,128)(2,1)} async-done(((bf16[32,8,1664]{2,1,0:T(8,128)(2,1)}), bf16[32,8,1664]{2,1,0:T(8,128)(2,1)}, u32[]{:S(2)}, u32[]{:S(2)}) %all-to-all-start) | async-done | bytes 852000 | tf_op jit(solution)/shard_map/all_to_all | solution.py:619
  39.0 3.2 %convolve.1 = (bf16[128,2048]{1,0:T(8,128)(2,1)S(1)}, f32[64,544]{1,0:T(8,128)S(1)}, f32[64,544]{1,0:T(8,128)S(1)}) custom-call(s32[1]{0:T(128)} %bitcast.core_ref, bf16[32,8,1664]{2,1,0:T(8,128)(2,1)} %all-to-all-done.rows_hbm.rows_ref, f32[36,8,1024]{2,1,0:T(8,128)} %stage.1.prior_hbm, bf16[2048,544]{1,0:T(8,128)(2,1)} %copy.22.proj_hbm), custom_call_target="tpu_custom_call" | custom-call | tf_op jit(solution)/shard_map/convolve/pallas_call | solution.py:270
  42.2 0.1 collective-permute-start
  42.3 0.1 copy.23.table_ref
  42.4 1.3 %collective-permute-done = f32[64,544]{1,0:T(8,128)S(1)} collective-permute-done((f32[64,544]{1,0:T(8,128)S(1)}, f32[64,544]{1,0:T(8,128)S(1)}, u32[]{:S(2)}, u32[]{:S(2)}) %collective-permute-start) | collective-permute-done | bytes 139296 | tf_op jit(solution)/shard_map/ppermute | solution.py:624
  43.7 0.0 copy-start.6
  43.7 0.0 copy-start.1
  43.7 0.0 copy-start.3
  43.8 3.3 %collective-permute-start.1 = (bf16[64,544]{1,0:T(8,128)(2,1)S(1)}, bf16[64,544]{1,0:T(8,128)(2,1)S(1)}, u32[]{:S(2)}, u32[]{:S(2)}) collective-permute-start(bf16[64,544]{1,0:T(8,128)(2,1)S(1)} %get-tuple-element.8), channel_id=1, source_target_pairs={{0,4},{1,5},{2,6},{3,7},{4,0},{5,1},{6,2},{7,3},{8,12},{9,13},{10,... | collective-permute-start | bytes 208904 | tf_op jit(solution)/shard_map/ppermute | solution.py:627
  47.0 0.7 collective-permute-start.2
  47.7 2.6 %collective-permute-start.3 = (bf16[64,544]{1,0:T(8,128)(2,1)S(1)}, bf16[64,544]{1,0:T(8,128)(2,1)S(1)}, u32[]{:S(2)}, u32[]{:S(2)}) collective-permute-start(bf16[64,544]{1,0:T(8,128)(2,1)S(1)} %get-tuple-element.8), channel_id=1, source_target_pairs={{0,6},{1,7},{2,0},{3,1},{4,2},{5,3},{6,4},{7,5},{8,14},{9,15},{10,... | collective-permute-start | bytes 208904 | tf_op jit(solution)/shard_map/ppermute | solution.py:627
  50.3 3.0 %attend.1.after_ref.attended_ref = bf16[32,8,512]{2,1,0:T(8,128)(2,1)S(1)} custom-call(s32[32]{0:T(128)S(1)} %copy-done.7, s32[32,8]{1,0:T(8,128)S(1)} %copy.23.table_ref, s32[32]{0:T(128)S(1)} %copy-done.9, bf16[32,8,1664]{2,1,0:T(8,128)(2,1)} %all-to-all-done.rows_hbm.rows_ref, bf16[256,2,16,128]{3,2,1,0:T(8,128)(2,1)S(1)} %copy-done.8), custom_call_target="tpu_custom_call" | custom-call | flops 3500000000 | bytes 6000000 | tf_op jit(solution)/shard_map/attend/pallas_call | solution.py:379
  53.3 0.1 normalise.1.ours_ref
  53.4 0.3 collective-permute-start.4
  53.7 1.3 %collective-permute-done.4.theirs_ref = bf16[64,768]{1,0:T(8,128)(2,1)S(1)} collective-permute-done((bf16[64,768]{1,0:T(8,128)(2,1)S(1)}, bf16[64,768]{1,0:T(8,128)(2,1)S(1)}, u32[]{:S(2)}, u32[]{:S(2)}) %collective-permute-start.4) | collective-permute-done | bytes 98336 | tf_op jit(solution)/shard_map/ppermute | solution.py:631
  55.1 7.5 %scan.1 = bf16[32,8,1536]{2,1,0:T(8,128)(2,1)S(1)} custom-call(s32[32]{0:T(128)S(1)} %copy-done.7, s32[1]{0:T(128)} %bitcast.core_ref, bf16[64,768]{1,0:T(8,128)(2,1)S(1)} %normalise.1.ours_ref, bf16[64,768]{1,0:T(8,128)(2,1)S(1)} %collective-permute-done.4.theirs_ref, bf16[128,2048]{1,0:T(8,128)(2,1)S(1)} %get-tuple-element.7.act_ref, ...), custom_call_target="tpu_custom_call" | custom-call | tf_op jit(solution)/shard_map/scan/pallas_call | solution.py:515
  62.5 28.1 %all_to_all.10.back_ref = bf16[32,8,1536]{2,1,0:T(8,128)(2,1)S(1)} all-to-all(bf16[32,8,1536]{2,1,0:T(8,128)(2,1)S(1)} %scan.1), channel_id=1, replica_groups=mesh['req'=32,'tp'=8] {'req'}, dimensions={0} | all-to-all | bytes 1572864 | tf_op jit(solution)/shard_map/all_to_all | solution.py:645
  90.6 1.3 %unpack.1 = (bf16[4,32,1024]{2,1,0:T(8,128)(2,1)}, bf16[4,32,2048]{2,1,0:T(8,128)(2,1)}) custom-call(bf16[32,8,1536]{2,1,0:T(8,128)(2,1)S(1)} %all_to_all.10.back_ref, bf16[4,32,2048]{2,1,0:T(8,128)(2,1)S(1)} %copy-done.2), custom_call_target="tpu_custom_call" | custom-call | tf_op jit(solution)/shard_map/unpack/pallas_call | solution.py:575
  (26 shorter events, 0.1 us)
Async XLA Ops:
  0.6 13.8 %copy-start.10 = (bf16[2048,544]{0,1:T(8,128)(2,1)S(1)}, bf16[2048,544]{0,1:T(8,128)(2,1)}, u32[]{:S(2)}) copy-start(bf16[2048,544]{0,1:T(8,128)(2,1)} %param.30) | copy-start | bytes 6684676
  3.2 35.8 %all-to-all-start = ((bf16[32,8,1664]{2,1,0:T(8,128)(2,1)}), bf16[32,8,1664]{2,1,0:T(8,128)(2,1)}, u32[]{:S(2)}, u32[]{:S(2)}) async-start(bf16[32,8,1664]{2,1,0:T(8,128)(2,1)} %pack.1.sent_ref), calls=%async_computation | async-start | bytes 1703936 | tf_op jit(solution)/shard_map/all_to_all | solution.py:619
  14.5 2.6 %copy-start.12 = (s32[32]{0:T(128)S(1)}, s32[32]{0:T(128)}, u32[]{:S(2)}) copy-start(s32[32]{0:T(128)} %param.23) | copy-start | bytes 388
  39.0 3.3 %copy-start.11 = (s32[32,8]{0,1:T(8,128)S(1)}, s32[32,8]{0,1:T(8,128)}, u32[]{:S(2)}) copy-start(s32[32,8]{0,1:T(8,128)} %param.21) | copy-start | bytes 3076
  39.0 11.3 %copy-start.7 = (s32[32]{0:T(128)S(1)}, s32[32]{0:T(128)}, u32[]{:S(2)}) copy-start(s32[32]{0:T(128)} %select_reduce_fusion.order_ref) | copy-start | bytes 388
  39.0 11.3 %copy-start.8 = (bf16[256,2,16,128]{3,2,1,0:T(8,128)(2,1)S(1)}, bf16[256,2,16,128]{3,2,1,0:T(8,128)(2,1)}, u32[]{:S(2)}) copy-start(bf16[256,2,16,128]{3,2,1,0:T(8,128)(2,1)} %pool_ref.1) | copy-start | bytes 6291460
  39.0 11.3 %copy-start.9 = (s32[32]{0:T(128)S(1)}, s32[32]{0:T(128)}, u32[]{:S(2)}) copy-start(s32[32]{0:T(128)} %length_ref.1) | copy-start | bytes 388
  42.2 1.5 %collective-permute-start = (f32[64,544]{1,0:T(8,128)S(1)}, f32[64,544]{1,0:T(8,128)S(1)}, u32[]{:S(2)}, u32[]{:S(2)}) collective-permute-start(f32[64,544]{1,0:T(8,128)S(1)} %get-tuple-element.6), channel_id=1, source_target_pairs={{0,1},{1,0},{2,3},{3,2},{4,5},{5,4},{6,7},{7,6},{8,9},{9,8},{10,11... | collective-permute-start | bytes 417800 | tf_op jit(solution)/shard_map/ppermute | solution.py:624
  43.7 9.6 %copy-start.6 = (f32[512]{0:T(512)S(1)}, f32[512]{0:T(512)}, u32[]{:S(2)}) copy-start(f32[512]{0:T(512)} %param.31) | copy-start | bytes 6148
  43.7 11.3 %copy-start.1 = (bf16[512,2048]{1,0:T(8,128)(2,1)S(1)}, bf16[512,2048]{1,0:T(8,128)(2,1)}, u32[]{:S(2)}) copy-start(bf16[512,2048]{1,0:T(8,128)(2,1)} %dt_proj_ref.1) | copy-start | bytes 6291460
  43.7 11.3 %copy-start.3 = (f32[16,2048]{1,0:T(8,128)S(1)}, f32[16,2048]{1,0:T(8,128)}, u32[]{:S(2)}) copy-start(f32[16,2048]{1,0:T(8,128)} %a_log_ref.1) | copy-start | bytes 393220
  43.7 11.3 %copy-start.4 = (f32[2048]{0:T(1024)S(1)}, f32[2048]{0:T(1024)}, u32[]{:S(2)}) copy-start(f32[2048]{0:T(1024)} %param.33) | copy-start | bytes 24580
  43.7 11.3 %copy-start.5 = (f32[2048]{0:T(1024)S(1)}, f32[2048]{0:T(1024)}, u32[]{:S(2)}) copy-start(f32[2048]{0:T(1024)} %param.35) | copy-start | bytes 24580
  43.8 9.5 %collective-permute-start.1 = (bf16[64,544]{1,0:T(8,128)(2,1)S(1)}, bf16[64,544]{1,0:T(8,128)(2,1)S(1)}, u32[]{:S(2)}, u32[]{:S(2)}) collective-permute-start(bf16[64,544]{1,0:T(8,128)(2,1)S(1)} %get-tuple-element.8), channel_id=1, source_target_pairs={{0,4},{1,5},{2,6},{3,7},{4,0},{5,1},{6,2},{7,3},{8,12},{9,13},{10,... | collective-permute-start | bytes 208904 | tf_op jit(solution)/shard_map/ppermute | solution.py:627
  47.0 6.2 %collective-permute-start.2 = (bf16[64,544]{1,0:T(8,128)(2,1)S(1)}, bf16[64,544]{1,0:T(8,128)(2,1)S(1)}, u32[]{:S(2)}, u32[]{:S(2)}) collective-permute-start(bf16[64,544]{1,0:T(8,128)(2,1)S(1)} %get-tuple-element.8), channel_id=1, source_target_pairs={{0,2},{1,3},{2,4},{3,5},{4,6},{5,7},{6,0},{7,1},{8,10},{9,11},{10,... | collective-permute-start | bytes 208904 | tf_op jit(solution)/shard_map/ppermute | solution.py:627
  47.7 5.6 %collective-permute-start.3 = (bf16[64,544]{1,0:T(8,128)(2,1)S(1)}, bf16[64,544]{1,0:T(8,128)(2,1)S(1)}, u32[]{:S(2)}, u32[]{:S(2)}) collective-permute-start(bf16[64,544]{1,0:T(8,128)(2,1)S(1)} %get-tuple-element.8), channel_id=1, source_target_pairs={{0,6},{1,7},{2,0},{3,1},{4,2},{5,3},{6,4},{7,5},{8,14},{9,15},{10,... | collective-permute-start | bytes 208904 | tf_op jit(solution)/shard_map/ppermute | solution.py:627
  50.3 4.8 %copy-start = (f32[32,16,2048]{2,1,0:T(8,128)S(1)}, f32[32,16,2048]{2,1,0:T(8,128)}, u32[]{:S(2)}) copy-start(f32[32,16,2048]{2,1,0:T(8,128)} %state_ref.1) | copy-start | bytes 12582916
  53.4 1.6 %collective-permute-start.4 = (bf16[64,768]{1,0:T(8,128)(2,1)S(1)}, bf16[64,768]{1,0:T(8,128)(2,1)S(1)}, u32[]{:S(2)}, u32[]{:S(2)}) collective-permute-start(bf16[64,768]{1,0:T(8,128)(2,1)S(1)} %normalise.1.ours_ref), channel_id=1, source_target_pairs={{0,1},{1,0},{2,3},{3,2},{4,5},{5,4},{6,7},{7,6},{8,9},{9,8},{10,11... | collective-permute-start | bytes 294920 | tf_op jit(solution)/shard_map/ppermute | solution.py:631
  55.0 35.6 %copy-start.2 = (bf16[4,32,2048]{2,1,0:T(8,128)(2,1)S(1)}, bf16[4,32,2048]{2,1,0:T(8,128)(2,1)}, u32[]{:S(2)}) copy-start(bf16[4,32,2048]{2,1,0:T(8,128)(2,1)} %z_ref.1) | copy-start | bytes 1572868
